TPU v7x, 32 devices: a whole 2x2x4 slice. The times are simulated.
32 devices in a mesh: pix: 4 (over x, core), ch: 8 (over z, y).
Axes of the slice: x: 2, y: 2, z: 4, core: 2. Of those that a mesh axis runs over, the one named last changes fastest.
Arguments:
- image_in: bfloat16 [128, 1024, 128], P('pix', 'ch'), may hold values from -6 to 6
- pre_act: bfloat16 [64, 64, 2048], P('pix', None, 'ch'), may hold values from -8 to 8
- grad_out: bfloat16 [64, 64, 2048], P('pix', None, 'ch'), may hold values from -6 to 6
- conv_weight: bfloat16 [3, 3, 1024, 2048], P(None, None, 'ch', 'pix'), may hold values from -0.0625 to 0.0625
- mix_weight: bfloat16 [32, 64, 64], P('ch'), may hold values from -0.75 to 0.75
Outputs:
- grad_in: bfloat16 [128, 1024, 128], P('pix', 'ch')
- grad_conv: float32 [3, 3, 1024, 2048], P(None, None, 'ch', 'pix')
- grad_mix: float32 [32, 64, 64], P('ch')
All inputs are finite; a program needn't handle non-finite values.
Results may differ from a plain program's by a relative error of at most 0.0049.
Values may be sent and summed in bfloat16 or wider, within the bound.
No kernel may reach another device: no remote copies, remote signals or barrier semaphores. Data moves between devices by JAX's collectives and lax.ppermute only.
A program may use at most 128 MiB of HBM per device.

v0:
```python
import jax
import jax.numpy as jnp
from jax import lax
from jax.sharding import PartitionSpec as P

TILES = 4
GROUP_WIDTH = 64


def from_behind(value, axis, steps):
    count = lax.axis_size(axis)
    leading, last = (max(0, -steps), min(count, count - steps))
    return lax.ppermute(value, axis, [(source, source + steps) for source in range(leading, last)])


def select_cols_in(values, col_tap):
    if col_tap == 0:
        zero_col = jnp.zeros(values[:, :1, 1].shape, values.dtype)
        return jnp.concatenate([zero_col, values[:, :-1, 1]], axis=1)
    return values[:, :, col_tap - 1]


def select_cols_grad(values, col_tap):
    if col_tap == 0:
        zero_col = jnp.zeros(values[:, :1].shape, values.dtype)
        return jnp.concatenate([values[:, 1:], zero_col], axis=1)
    return values


def gather_taps(row_sources):
    tap_list = []
    for row_tap in range(3):
        for col_tap in range(3):
            tap_list.append(select_cols_in(row_sources[row_tap], col_tap))
    return jnp.concatenate(tap_list, axis=2)


def pre_gradient(grad_rows, pre_rows, mix_rows):
    tile_rows, width, chans = grad_rows.shape
    groups_here = chans // GROUP_WIDTH
    grad_groups = grad_rows.reshape(tile_rows, width, groups_here, GROUP_WIDTH)
    grad_act = jnp.einsum(
        "rwgi,gji->rwgj", grad_groups, mix_rows, preferred_element_type=jnp.float32
    ).reshape(tile_rows, width, chans)
    pre_f = pre_rows.astype(jnp.float32)
    sigmoid_h = jax.nn.sigmoid(pre_f)
    return (grad_act * (sigmoid_h * (1.0 + pre_f * (1.0 - sigmoid_h)))).astype(jnp.bfloat16)


def input_terms(grad_main, grad_up, kernel_part):
    pixel_count = grad_main.shape[0] * grad_main.shape[1]
    width_k = grad_main.shape[2]

    def term(source, row_tap, col_tap):
        shifted = select_cols_grad(source, col_tap).reshape(pixel_count, width_k)
        return lax.dot_general(
            shifted,
            kernel_part[row_tap, col_tap],
            (((1,), (1,)), ((), ())),
            preferred_element_type=jnp.float32,
        )

    even_even = term(grad_main, 1, 1)
    even_odd = term(grad_main, 1, 2) + term(grad_main, 1, 0)
    odd_even = term(grad_main, 2, 1) + term(grad_up, 0, 1)
    odd_odd = (
        term(grad_main, 2, 2) + term(grad_main, 2, 0) + term(grad_up, 0, 2) + term(grad_up, 0, 0)
    )
    return jnp.stack([even_even, even_odd, odd_even, odd_odd])


def shards(image_in, pre_act, grad_out, conv_weight, mix_weight):
    tile_rows, width, chans = grad_out.shape
    in_chans = image_in.shape[1]
    pix_count = lax.axis_size("pix")
    pix_index = lax.axis_index("pix")
    first_tile = pix_index % TILES == 0
    last_tile = pix_index % TILES == TILES - 1
    scale = 1.0 / float(pix_count * tile_rows * width) ** 0.5
    pre_f = pre_act.astype(jnp.float32)
    act = (pre_f * jax.nn.sigmoid(pre_f)).astype(jnp.bfloat16)
    groups_here = chans // GROUP_WIDTH
    mix_part = jnp.einsum(
        "rwgj,rwgi->gji",
        act.reshape(tile_rows, width, groups_here, GROUP_WIDTH),
        grad_out.reshape(tile_rows, width, groups_here, GROUP_WIDTH),
        preferred_element_type=jnp.float32,
    )
    grad_mix = lax.psum(mix_part, "pix") * scale
    grad_next, pre_next = from_behind((grad_out[:1], pre_act[:1]), "pix", -1)
    grad_next = jnp.where(last_tile, jnp.zeros_like(grad_next), grad_next)
    pre_next = jnp.where(last_tile, jnp.zeros_like(pre_next), pre_next)
    grad_ext = jnp.concatenate([grad_out, grad_next], axis=0)
    pre_ext = jnp.concatenate([pre_act, pre_next], axis=0)
    grad_all, pre_all = (
        lax.all_gather(grad_ext, "ch", axis=2, tiled=True),
        lax.all_gather(pre_ext, "ch", axis=2, tiled=True),
    )
    mix_all = lax.all_gather(mix_weight, "ch", axis=0, tiled=True)
    grad_whole = pre_gradient(grad_all, pre_all, mix_all)
    grad_main = grad_whole[:tile_rows]
    grad_up = grad_whole[1:]
    full_chans = grad_whole.shape[2]
    pixel_count = tile_rows * width
    phases = jnp.transpose(image_in.reshape(tile_rows, 2, in_chans, width, 2), (0, 1, 3, 4, 2))
    odd_prev = from_behind(phases[-1:, 1], "pix", 1)
    odd_prev = jnp.where(first_tile, jnp.zeros_like(odd_prev), odd_prev)
    odd_shift = jnp.concatenate([odd_prev, phases[:-1, 1]], axis=0)
    input_taps = gather_taps([odd_shift, phases[:, 0], phases[:, 1]]).reshape(
        pixel_count, 9 * in_chans
    )
    grad_flat = grad_main.reshape(pixel_count, full_chans)
    filter_part = lax.psum_scatter(
        lax.dot_general(
            grad_flat, input_taps, (((0,), (0,)), ((), ())), preferred_element_type=jnp.float32
        ),
        "pix",
        scatter_dimension=0,
        tiled=True,
    )
    grad_conv = jnp.transpose(filter_part.reshape(-1, 3, 3, in_chans), (1, 2, 3, 0)) * scale
    kernel_all = lax.all_gather(conv_weight, "pix", axis=3, tiled=True)
    phase_sum = input_terms(grad_main, grad_up, kernel_all)
    stacked = phase_sum.reshape(2, 2, tile_rows, width, in_chans)
    grad_in = (
        jnp.transpose(stacked, (2, 0, 4, 3, 1))
        .reshape(2 * tile_rows, in_chans, 2 * width)
        .astype(jnp.bfloat16)
    )
    return (grad_in, grad_conv, grad_mix)


def solution(mesh):
    in_specs = (
        P("pix", "ch", None),
        P("pix", None, "ch"),
        P("pix", None, "ch"),
        P(None, None, "ch", "pix"),
        P("ch", None, None),
    )
    out_specs = (P("pix", "ch", None), P(None, None, "ch", "pix"), P("ch", None, None))
    return jax.shard_map(shards, mesh=mesh, in_specs=in_specs, out_specs=out_specs, check_vma=False)
```

profile of v0, /device:TPU:1, one launch (start us, length us, event | category | flops | bytes accessed | tf_op | source)
XLA Modules:
  0.0 283.8 jit_solution(2361189757455512336)
XLA Ops:
  8.1 0.8 slice.87
  8.9 2.0 collective-permute-start
  10.8 4.1 %collective-permute-done = bf16[1,64,256]{2,1,0:T(8,128)(2,1)S(1)} collective-permute-done((bf16[1,64,256]{2,1,0:T(8,128)(2,1)S(1)}, bf16[1,64,256]{2,1,0:T(8,128)(2,1)S(1)}, u32[]{:S(2)}, u32[]{:S(2)}) %collective-permute-start) | collective-permute-done | bytes 32800 | tf_op jit(solution)/shard_map/ppermute | solution.py:13
  15.0 1.9 pad_maximum_fusion.1
  16.9 0.8 slice.88
  17.7 1.9 collective-permute-start.1
  19.6 3.3 %collective-permute-done.1 = bf16[1,64,256]{2,1,0:T(8,128)(2,1)S(1)} collective-permute-done((bf16[1,64,256]{2,1,0:T(8,128)(2,1)S(1)}, bf16[1,64,256]{2,1,0:T(8,128)(2,1)S(1)}, u32[]{:S(2)}, u32[]{:S(2)}) %collective-permute-start.1) | collective-permute-done | bytes 32800 | tf_op jit(solution)/shard_map/ppermute | solution.py:13
  22.9 1.9 pad_maximum_fusion.2
  24.9 2.1 reshape.55
  27.7 1.1 convolution_bitcast_fusion.1
  28.9 1.6 copy.26
  30.8 2.1 collective-permute-start.2
  33.4 27.3 %all_gather.13 = bf16[32,64,64]{2,1,0:T(8,128)(2,1)S(1)} all-gather(bf16[4,64,64]{2,1,0:T(8,128)(2,1)S(1)} %copy-done.7), channel_id=1, replica_groups=mesh['pix'=4,'ch'=8] {'ch'}, dimensions={0}, use_global_device_ids=true | all-gather | bytes 294912 | tf_op jit(solution)/shard_map/all_gather | solution.py:99
  60.8 0.8 pad_dynamic-update-slice_fusion.2
  63.0 0.8 pad_dynamic-update-slice_fusion.1
  65.2 0.8 pad_dynamic-update-slice_fusion
  67.4 32.7 %all-gather.4.cloned.1.call-done = bf16[17,64,2048]{2,1,0:T(8,128)(2,1)} async-done(((bf16[17,64,256]{2,1,0:T(8,128)(2,1)}), bf16[17,64,2048]{2,1,0:T(8,128)(2,1)}) %all-gather.4.cloned.1.call-update) | async-done | bytes 4456464 | tf_op jit(solution)/shard_map/all_gather | solution.py:96
  100.2 13.6 %reshape.47 = bf16[17,64,32,64]{3,2,1,0:T(8,128)(2,1)} reshape(bf16[17,64,2048]{2,1,0:T(8,128)(2,1)} %all-gather.4.cloned.1.call-done) | data formatting | bytes 8912896 | tf_op jit(solution)/shard_map/reshape | solution.py:41
  113.8 14.3 %fusion.9 = f32[17,64,32,64]{3,1,0,2:T(8,128)} fusion(bf16[17,64,32,64]{3,2,1,0:T(8,128)(2,1)} %reshape.47, bf16[32,64,64]{2,1,0:T(8,128)(2,1)S(1)} %all_gather.13), kind=kOutput, calls=%fused_computation.12 | convolution fusion | flops 285212672 | bytes 13631488 | tf_op jit(solution)/shard_map/rwgi,gji->rwgj/dot_general | solution.py:42
  128.1 16.8 %copy.24 = f32[17,64,32,64]{3,2,1,0:T(8,128)} copy(f32[17,64,32,64]{3,1,0,2:T(8,128)} %fusion.9) | data formatting | bytes 17825792 | tf_op jit(solution)/shard_map/rwgi,gji->rwgj/transpose | solution.py:42
  145.0 16.0 %reshape.48 = f32[17,64,2048]{2,1,0:T(8,128)} reshape(f32[17,64,32,64]{3,2,1,0:T(8,128)} %copy.24) | data formatting | bytes 17825792 | tf_op jit(solution)/shard_map/reshape | solution.py:44
  160.9 16.0 %all-gather.6.cloned.1.call-done = bf16[17,64,2048]{2,1,0:T(8,128)(2,1)} async-done(((bf16[17,64,256]{2,1,0:T(8,128)(2,1)}), bf16[17,64,2048]{2,1,0:T(8,128)(2,1)}) %all-gather.6.cloned.1.call-update) | async-done | bytes 4456464 | tf_op jit(solution)/shard_map/all_gather | solution.py:97
  176.9 6.7 %fusion.6 = bf16[17,64,2048]{2,1,0:T(8,128)(2,1)S(1)} fusion(f32[17,64,2048]{2,1,0:T(8,128)} %reshape.48, bf16[17,64,2048]{2,1,0:T(8,128)(2,1)} %all-gather.6.cloned.1.call-done), kind=kLoop, calls=%fused_computation.8 | loop fusion | flops 22282240 | bytes 17825792 | tf_op jit(solution)/shard_map/convert_element_type | solution.py:47
  183.6 2.1 copy-done
  185.7 10.3 %convolution_bitcast_fusion = f32[2048,1152]{1,0:T(8,128)} fusion(bf16[17,64,2048]{2,1,0:T(8,128)(2,1)S(1)} %fusion.6, bf16[16,64,1152]{2,1,0:T(8,128)(2,1)} %fusion.34), kind=kOutput, calls=%fused_computation.11 | convolution fusion | flops 4831838208 | bytes 16252928 | tf_op jit(solution)/shard_map/dot_general | solution.py:114
  196.0 1.6 broadcast_multiply_fusion.1
  197.6 5.7 %fusion.40 = (bf16[16,63,2048]{2,1,0:T(8,128)(2,1)S(1)}, bf16[16,63,2048]{2,1,0:T(8,128)(2,1)S(1)}) fusion(bf16[17,64,2048]{2,1,0:T(8,128)(2,1)} %copy-done), kind=kLoop, calls=%fused_computation.87 | loop fusion | bytes 16515072 | tf_op jit(solution)/shard_map/slice | solution.py:26
  203.3 3.1 %concatenate.30 = bf16[16,64,2048]{2,1,0:T(8,128)(2,1)} pad(bf16[16,63,2048]{2,1,0:T(8,128)(2,1)S(1)} %get-tuple-element.10, bf16[]{:T(256)} %constant.30.clone.1), padding=0_0x0_1x0_0 | pad | bytes 8323074 | tf_op jit(solution)/shard_map/concatenate | solution.py:26
  206.4 3.0 %concatenate.31 = bf16[16,64,2048]{2,1,0:T(8,128)(2,1)} pad(bf16[16,63,2048]{2,1,0:T(8,128)(2,1)S(1)} %get-tuple-element.9, bf16[]{:T(256)} %constant.30.clone.1), padding=0_0x0_1x0_0 | pad | bytes 8323074 | tf_op jit(solution)/shard_map/concatenate | solution.py:26
  209.4 1.5 slice-done
  211.0 3.7 %fusion.41 = (bf16[16,64,2048]{2,1,0:T(8,128)(2,1)}, bf16[16,64,2048]{2,1,0:T(8,128)(2,1)}) fusion(bf16[17,64,2048]{2,1,0:T(8,128)(2,1)S(1)} %bitcast.117), kind=kLoop, calls=%fused_computation.88 | loop fusion | bytes 16777216 | tf_op jit(solution)/shard_map/slice | solution.py:102
  215.0 3.7 %fusion.27 = f32[1024,128]{1,0:T(8,128)S(1)} fusion(bf16[1024,2048]{1,0:T(8,128)(2,1)} %bitcast.129, bf16[3,3,128,2048]{3,2,1,0:T(8,128)(2,1)} %all-gather.8.cloned.1.call-done), kind=kOutput, calls=%fused_computation.55 | convolution fusion | flops 536870912 | bytes 5242880 | tf_op jit(solution)/shard_map/dot_general | solution.py:56
  218.7 2.6 fusion.26
  221.9 1.2 fusion.25
  223.2 1.3 fusion.15
  224.4 0.9 copy-done.1
  225.4 1.3 fusion.18
  226.7 1.3 convolution_add_fusion.2
  227.9 1.0 copy-done.2
  228.9 1.3 fusion.17
  230.2 1.3 convolution_add_fusion.1
  231.5 0.9 copy-done.3
  232.4 1.3 fusion.16
  233.8 1.1 copy.25
  234.9 1.3 copy.32
  236.2 36.7 %reduce-scatter.2.cloned.1.call-done = f32[512,1152]{1,0:T(8,128)} async-done(((f32[2048,1152]{1,0:T(8,128)}), f32[512,1152]{1,0:T(8,128)}) %reduce-scatter.2.cloned.1.call-update) | async-done | bytes 2359312 | tf_op jit(solution)/shard_map/reduce_scatter | solution.py:113
  272.9 1.8 broadcast_multiply_fusion
  274.7 2.0 copy.29
  (49 shorter events, 7.2 us)
Async XLA Ops:
  8.0 19.0 %copy-start.5 = (bf16[16,64,256]{2,1,0:T(8,128)(2,1)S(1)}, bf16[16,64,256]{2,1,0:T(8,128)(2,1)}, u32[]{:S(2)}) copy-start(bf16[16,64,256]{2,1,0:T(8,128)(2,1)} %param.6) | copy-start | bytes 1572868
  8.0 92.2 %all-gather.4.cloned.1.call-start = ((), (), s32[]{:S(2)}) async-start(), calls=%async_computation.1 | async-start | bytes 5013504 | tf_op jit(solution)/shard_map/all_gather | solution.py:96
  8.9 6.1 %collective-permute-start = (bf16[1,64,256]{2,1,0:T(8,128)(2,1)S(1)}, bf16[1,64,256]{2,1,0:T(8,128)(2,1)S(1)}, u32[]{:S(2)}, u32[]{:S(2)}) collective-permute-start(bf16[1,64,256]{2,1,0:T(8,128)(2,1)S(1)} %slice.87), channel_id=1, source_target_pairs={{8,0},{16,8},{24,16},{9,1},{17,9},{25,17},{10,2},{18,10},{26,18},{... | collective-permute-start | bytes 98312 | tf_op jit(solution)/shard_map/ppermute | solution.py:13
  16.9 160.0 %all-gather.6.cloned.1.call-start = ((), (), s32[]{:S(2)}) async-start(), calls=%async_computation.2 | async-start | bytes 5013504 | tf_op jit(solution)/shard_map/all_gather | solution.py:97
  17.7 5.2 %collective-permute-start.1 = (bf16[1,64,256]{2,1,0:T(8,128)(2,1)S(1)}, bf16[1,64,256]{2,1,0:T(8,128)(2,1)S(1)}, u32[]{:S(2)}, u32[]{:S(2)}) collective-permute-start(bf16[1,64,256]{2,1,0:T(8,128)(2,1)S(1)} %slice.88), channel_id=1, source_target_pairs={{8,0},{16,8},{24,16},{9,1},{17,9},{25,17},{10,2},{18,10},{26,18},{... | collective-permute-start | bytes 98312 | tf_op jit(solution)/shard_map/ppermute | solution.py:13
  24.9 171.2 %all-reduce.7.cloned.1.call-start = ((), (), s32[]{:S(2)}) async-start(), calls=%async_computation.5 | async-start | bytes 262144 | tf_op jit(solution)/shard_map/psum | solution.py:89
  28.8 186.1 %all-gather.8.cloned.1.call-start = ((), (), s32[]{:S(2)}) async-start(), calls=%async_computation.3 | async-start | bytes 5898240 | tf_op jit(solution)/shard_map/all_gather | solution.py:122
  30.8 2.6 copy-start.7
  30.8 29.9 %collective-permute-start.2 = (bf16[1,64,2,128]{3,1,0,2:T(8,128)(2,1)S(1)}, bf16[1,64,2,128]{3,1,0,2:T(8,128)(2,1)S(1)}, u32[]{:S(2)}, u32[]{:S(2)}) collective-permute-start(bf16[1,64,2,128]{3,1,0,2:T(8,128)(2,1)S(1)} %slice_bitcast_fusion.27), channel_id=1, source_target_pairs={{0,8},{8,16},{16,24},{1,9},{9,17},{17,25},{2,10},{10,18},{18,26},{... | collective-permute-start | bytes 98312 | tf_op jit(solution)/shard_map/ppermute | solution.py:13
  32.9 240.0 %reduce-scatter.2.cloned.1.call-start = ((), (), s32[]{:S(2)}) async-start(), calls=%async_computation.4 | async-start | bytes 11796480 | tf_op jit(solution)/shard_map/reduce_scatter | solution.py:113
  183.6 2.1 copy-start
  206.4 4.5 %slice-start = ((s8[4456448]{0:T(1024)(128)(4,1)}), s8[4194304]{0:T(1024)(128)(4,1)S(1)}, s32[]{:S(2)}) async-start(s8[4456448]{0:T(1024)(128)(4,1)} %bitcast.116), calls=%async_computation.6 | async-start | bytes 8388608
  206.4 4.6 %slice-start.1 = ((s8[4456448]{0:T(1024)(128)(4,1)}), s8[262144]{0:T(1024)(128)(4,1)S(1)}, s32[]{:S(2)}) async-start(s8[4456448]{0:T(1024)(128)(4,1)} %bitcast.116), calls=%async_computation.7 | async-start | bytes 524288
  215.0 3.7 %copy-start.4 = (bf16[16,64,2048]{2,1,0:T(8,128)(2,1)S(1)}, bf16[16,64,2048]{2,1,0:T(8,128)(2,1)}, u32[]{:S(2)}) copy-start(bf16[16,64,2048]{2,1,0:T(8,128)(2,1)} %get-tuple-element.12) | copy-start | bytes 12582916
  218.7 3.2 %copy-start.6 = (bf16[3,3,128,2048]{3,2,1,0:T(8,128)(2,1)S(1)}, bf16[3,3,128,2048]{3,2,1,0:T(8,128)(2,1)}, u32[]{:S(2)}) copy-start(bf16[3,3,128,2048]{3,2,1,0:T(8,128)(2,1)} %all-gather.8.cloned.1.call-done) | copy-start | bytes 14155780
  223.2 2.2 copy-start.1
  226.7 2.2 copy-start.2
  230.2 2.2 copy-start.3
Sparse Core Ops, SparseCore 0:
  17.0 83.1 all-gather.3
  102.2 74.6 all-gather.5
  178.5 36.4 all-gather.7
Sparse Core Ops, SparseCore 1:
  28.9 29.5 all-reduce.6
  196.1 76.7 reduce-scatter.1
where the time goes:
time: 286 us; the launch traced here: 284 us
  waiting for transfers between devices  93.3 us (33%)
  local copies, waits for them, and re-layouts  84.9 us (30%)
  matrix products  40.9 us (14%)
  blocking collectives  27.3 us (10%)
  other arithmetic  15.8 us (6%)
  between operations  15.5 us (5%)
  starting transfers between devices  6.12 us (2%)
    reduce_scatter x1, waiting for transfers between devices, shards(): lax.psum_scatter(lax.dot_general(grad_flat, input_taps, (((0,), (0,)), ((...  36.7 us
    all_gather x1, waiting for transfers between devices, shards(): lax.all_gather(grad_ext, 'ch', axis=2, tiled=True)  32.7 us
    all_gather x1, blocking collectives, shards(): mix_all = lax.all_gather(mix_weight, 'ch', axis=0, tiled=True)  27.3 us
    transpose x1, local copies, waits for them, and re-layouts, pre_gradient(): jnp.einsum('rwgi,gji->rwgj', grad_groups, mix_rows, preferred_element_typ...  16.8 us
    all_gather x1, waiting for transfers between devices, shards(): lax.all_gather(pre_ext, 'ch', axis=2, tiled=True)  16 us
    reshape x1, local copies, waits for them, and re-layouts, pre_gradient(): grad_act = jnp.einsum('rwgi,gji->rwgj', grad_groups, mix_rows, preferred_...  16 us
    dot_general x9, matrix products, term(): lax.dot_general(shifted, kernel_part[row_tap, col_tap], (((1,), (1,)), ((...  15.2 us
    unnamed x28, local copies, waits for them, and re-layouts  14.6 us
  transfers between devices with their start and end apart: 8, of which 6 were waited for; matrix products, arithmetic and copies ran while one was open for 45% of the time, Pallas kernels for 0%

commit v1 on v0

v1 whole, which is shorter than its diff:
```python
import functools

import jax
import jax.numpy as jnp
from jax import lax
from jax.experimental import pallas as pl
from jax.experimental.pallas import tpu as pltpu
from jax.sharding import PartitionSpec as P

TILES = 4
GROUP_WIDTH = 64
BF = jnp.bfloat16
F32 = jnp.float32
VMEM_LIMIT = 56 * 2**20


def params():
    return pltpu.CompilerParams(vmem_limit_bytes=VMEM_LIMIT)


def dot_nn(a, b):
    return lax.dot_general(a, b, (((1,), (0,)), ((), ())), preferred_element_type=F32)


def dot_nt(a, b):
    return lax.dot_general(a, b, (((1,), (1,)), ((), ())), preferred_element_type=F32)


def dot_tn(a, b):
    return lax.dot_general(a, b, (((0,), (0,)), ((), ())), preferred_element_type=F32)


def iota(shape, dim):
    return lax.broadcasted_iota(jnp.int32, shape, dim)


def pre_kernel(grad_ref, pre_ref, mix_ref, out_ref, mix_out_ref):
    chans = grad_ref.shape[1]
    spread = (iota((GROUP_WIDTH, chans), 0) == iota((GROUP_WIDTH, chans), 1) % GROUP_WIDTH).astype(BF)
    same = iota((chans, chans), 0) // GROUP_WIDTH == iota((chans, chans), 1) // GROUP_WIDTH
    blocks = jnp.where(same, dot_nn(mix_ref[...], spread), 0.0).astype(BF)
    grad = grad_ref[...]
    pre = pre_ref[...].astype(F32)
    sig = jax.nn.sigmoid(pre)
    act = (pre * sig).astype(BF)
    grad_act = dot_nt(grad, blocks)
    out_ref[...] = (grad_act * (sig * (1.0 + pre * (1.0 - sig)))).astype(BF)
    full = jnp.where(same, dot_tn(act, grad), 0.0)
    total = full
    for step in range(1, chans // GROUP_WIDTH):
        total = total + pltpu.roll(full, step * GROUP_WIDTH, 1)
    mix_out_ref[...] = total[:, :GROUP_WIDTH]


def pre_gradient(grad_out, pre_act, mix_weight):
    pixels, chans = grad_out.shape
    return pl.pallas_call(
        pre_kernel,
        out_shape=(
            jax.ShapeDtypeStruct((pixels, chans), BF),
            jax.ShapeDtypeStruct((chans, GROUP_WIDTH), F32),
        ),
        compiler_params=params(),
        cost_estimate=pl.CostEstimate(
            flops=4 * pixels * chans * chans, bytes_accessed=6 * pixels * chans, transcendentals=pixels * chans
        ),
        name="pre_grad",
    )(grad_out, pre_act, mix_weight)


def taps_kernel(image_ref, prev_ref, out_ref):
    rows, chans, width = image_ref.shape
    half = width // 2
    col_in = iota((2 * width, 6 * half), 0)
    col_out = iota((2 * width, 6 * half), 1)
    pick = (
        (col_in // width == (col_out % width) // half)
        & (col_in % width == 2 * (col_out % half) + col_out // width - 1)
    ).astype(BF)
    for pair in range(rows // 4):
        for row_tap in range(3):
            first = 4 * pair + row_tap - 1
            upper = prev_ref[...] if first < 0 else image_ref[first]
            both = jnp.concatenate([upper, image_ref[first + 2]], axis=1)
            picked = dot_nn(both, pick).astype(BF)
            for col_tap in range(3):
                tap = 3 * row_tap + col_tap
                out_ref[tap * chans : (tap + 1) * chans, pair * width : (pair + 1) * width] = picked[
                    :, col_tap * width : (col_tap + 1) * width
                ]


def image_taps(image_in, prev_row):
    rows, chans, width = image_in.shape
    pixels = rows * width // 4
    return pl.pallas_call(
        taps_kernel,
        out_shape=jax.ShapeDtypeStruct((9 * chans, pixels), BF),
        compiler_params=params(),
        cost_estimate=pl.CostEstimate(
            flops=rows * chans * width * width * 9 // 2, bytes_accessed=13 * rows * chans * width // 2, transcendentals=0
        ),
        name="taps",
    )(image_in, prev_row)


def image_kernel(
    grad_count, part_count, width, ids_ref, halo_ref, *refs
):
    grads, parts = refs[:grad_count], refs[grad_count : grad_count + part_count]
    out_ref, grad_all, part_all, grad_sem, part_sem = refs[grad_count + part_count :]
    pixels, span = grads[0].shape
    outs, part_span = parts[0].shape
    chans = outs // 9
    tile = 4 * width
    tiles = pixels // tile

    def part_copy(index):
        start = pl.multiple_of(ids_ref[grad_count + index] * part_span, part_span)
        return pltpu.make_async_copy(
            parts[index], part_all.at[:, pl.ds(start, part_span)], part_sem.at[index]
        )

    def grad_copy(index):
        start = pl.multiple_of(ids_ref[index] * span, span)
        return pltpu.make_async_copy(
            grads[index], grad_all.at[:, pl.ds(start, span)], grad_sem.at[index]
        )

    for index in range(part_count):
        part_copy(index).start()
    for index in range(grad_count):
        grad_copy(index).start()

    lane = iota((chans, tile), 1)
    last_col = lane % width == width - 1
    row_end = lane >= tile - width
    place_in = iota((tile, tile), 0)
    place_out = iota((tile, tile), 1)
    place = (
        ((place_in % (2 * width)) // width == place_out // (2 * width))
        & (2 * (place_in % width) + place_in // (2 * width) == place_out % (2 * width))
    ).astype(BF)

    def left(value):
        return jnp.where(last_col, 0.0, pltpu.roll(value, tile - 1, 1))

    def up_terms(terms):
        even, odd = terms[chans : 2 * chans], terms[2 * chans : 3 * chans] + left(terms[:chans])
        return pltpu.roll(even, tile - width, 1), pltpu.roll(odd, tile - width, 1)

    for index in range(part_count):
        part_copy(index).wait()
    for index in range(grad_count):
        grad_copy(index).wait()
    halo = dot_nt(part_all[: 3 * chans], halo_ref[...])
    below = up_terms(jnp.concatenate([halo, jnp.zeros_like(halo)], axis=1))
    for step in reversed(range(tiles)):
        terms = dot_nt(part_all[...], grad_all[step * tile : (step + 1) * tile])
        own = up_terms(terms[: 3 * chans])
        tap = lambda index: terms[index * chans : (index + 1) * chans]
        phases = (
            (tap(4), tap(5) + left(tap(3))),
            (
                tap(7) + jnp.where(row_end, below[0], own[0]),
                tap(8) + left(tap(6)) + jnp.where(row_end, below[1], own[1]),
            ),
        )
        below = own
        for parity in range(2):
            even, odd = (value.astype(BF) for value in phases[parity])
            for pair in range(2):
                cols = slice(pair * 2 * width, (pair + 1) * 2 * width)
                placed = dot_nn(jnp.concatenate([even[:, cols], odd[:, cols]], axis=1), place).astype(BF)
                first = 8 * step + 4 * pair + parity
                out_ref[first] = placed[:, : 2 * width]
                out_ref[first + 2] = placed[:, 2 * width :]


def image_gradient(grads, grad_ids, parts, part_ids, halo, width):
    pixels, span = grads[0].shape
    outs, part_span = parts[0].shape
    full = span * len(grads)
    chans = outs // 9
    ids = jnp.stack([jnp.asarray(value, jnp.int32) for value in (*grad_ids, *part_ids)])
    kernel = functools.partial(image_kernel, len(grads), len(parts), width)
    anywhere = pl.BlockSpec(memory_space=pl.ANY)
    return pl.pallas_call(
        kernel,
        out_shape=jax.ShapeDtypeStruct((2 * pixels // width, chans, 2 * width), BF),
        in_specs=[pl.BlockSpec(memory_space=pltpu.SMEM), pl.BlockSpec(memory_space=pltpu.VMEM)]
        + [anywhere] * (len(grads) + len(parts)),
        out_specs=pl.BlockSpec(memory_space=pltpu.VMEM),
        scratch_shapes=[
            pltpu.VMEM((pixels, full), BF),
            pltpu.VMEM((outs, full), BF),
            pltpu.SemaphoreType.DMA((len(grads),)),
            pltpu.SemaphoreType.DMA((len(parts),)),
        ],
        compiler_params=params(),
        cost_estimate=pl.CostEstimate(
            flops=2 * pixels * outs * full, bytes_accessed=2 * full * (pixels + outs), transcendentals=0
        ),
        name="image_grad",
    )(ids, halo, *grads, *parts)


def step_along(value, axis, steps):
    count = lax.axis_size(axis)
    return lax.ppermute(
        value, axis, [(source, source + steps) for source in range(count) if 0 <= source + steps < count]
    )


def shards(image_in, pre_act, grad_out, conv_weight, mix_weight):
    tile_rows, width, chans = grad_out.shape
    in_chans = image_in.shape[1]
    pix_count, ch_count = lax.axis_size("pix"), lax.axis_size("ch")
    pix_index = lax.axis_index("pix")
    first_tile = pix_index % TILES == 0
    last_tile = pix_index % TILES == TILES - 1
    pixels = tile_rows * width
    scale = 1.0 / float(pix_count * pixels) ** 0.5

    prev_row = step_along(image_in[-1], "pix", 1)
    prev_row = jnp.where(first_tile, jnp.zeros_like(prev_row), prev_row)
    grad_pre, mix_part = pre_gradient(
        grad_out.reshape(pixels, chans),
        pre_act.reshape(pixels, chans),
        mix_weight.reshape(chans, GROUP_WIDTH),
    )
    grad_mix = (lax.psum(mix_part, "pix") * scale).reshape(mix_weight.shape)
    halo = step_along(grad_pre[:width], "pix", -1)
    halo = jnp.where(last_tile, jnp.zeros_like(halo), halo)
    halo_all = lax.all_gather(halo, "ch", axis=1, tiled=True)
    halo_all = jnp.concatenate([halo_all, jnp.zeros_like(halo_all)], axis=0)
    kernel_own = conv_weight.reshape(9 * in_chans, -1)
    taps = image_taps(image_in, prev_row)

    grad_all = lax.all_gather(grad_pre, "ch", axis=0)
    kernel_all = lax.all_gather(kernel_own, "pix", axis=0)
    partial = jnp.concatenate([dot_nn(taps, grad_all[index]).astype(BF) for index in range(ch_count)], axis=1)
    grad_conv = lax.psum_scatter(partial, "pix", scatter_dimension=1, tiled=True).astype(F32) * scale
    grad_in = image_gradient(
        [grad_all[index] for index in range(ch_count)],
        range(ch_count),
        [kernel_all[index] for index in range(pix_count)],
        range(pix_count),
        halo_all,
        width,
    )
    return (grad_in, grad_conv.reshape(conv_weight.shape), grad_mix)


def solution(mesh):
    in_specs = (
        P("pix", "ch", None),
        P("pix", None, "ch"),
        P("pix", None, "ch"),
        P(None, None, "ch", "pix"),
        P("ch", None, None),
    )
    out_specs = (P("pix", "ch", None), P(None, None, "ch", "pix"), P("ch", None, None))
    return jax.shard_map(shards, mesh=mesh, in_specs=in_specs, out_specs=out_specs, check_vma=False)
```

time: 286 us -> 177 us (0.62)
  the two profiles are of different devices: /device:TPU:1 before, /device:TPU:0 now
where the time goes in v1:
time: 177 us
  waiting for transfers between devices  71.2 us (40%)
  blocking collectives  30.9 us (17%)
  Pallas kernels  22.7 us (13%)
  matrix products  17.9 us (10%)
  between operations  15.6 us (9%)
  local copies, waits for them, and re-layouts  11.2 us (6%)
  starting transfers between devices  3.79 us (2%)
  other arithmetic  3.63 us (2%)
    all_gather x1, waiting for transfers between devices, shards(): grad_all = lax.all_gather(grad_pre, 'ch', axis=0)  67.3 us
    all_gather x1, blocking collectives, shards(): halo_all = lax.all_gather(halo, 'ch', axis=1, tiled=True)  30.9 us
    dot_general x8, matrix products, dot_nn(): lax.dot_general(a, b, (((1,), (0,)), ((), ())), preferred_element_type=F32)  17.9 us
    pallas_call x1, Pallas kernels, image_gradient(): pl.pallas_call(kernel, out_shape=jax.ShapeDtypeStruct((2 * pixels // widt...  16.3 us
    squeeze x1, local copies, waits for them, and re-layouts, shards(): kernel_all[index]  4.78 us
    pallas_call x1, Pallas kernels, image_taps(): pl.pallas_call(taps_kernel, out_shape=jax.ShapeDtypeStruct((9 * chans, pi...  3.68 us
    ppermute x2, starting transfers between devices, step_along(): lax.ppermute(value, axis, [(source, source + steps) for source in range(c...  3.63 us
  transfers between devices with their start and end apart: 6, of which 3 were waited for; matrix products, arithmetic and copies ran while one was open for 17% of the time, Pallas kernels for 11%

profile of v1, /device:TPU:0, one launch (start us, length us, event | category | flops | bytes accessed | tf_op | source)
XLA Modules:
  0.0 176.9 jit_solution(6326970100733547600)
XLA Ops:
  8.0 0.0 all-gather.6.cloned.1.call-start
  8.0 2.6 %pre_grad.1 = (bf16[1024,256]{1,0:T(8,128)(2,1)}, f32[256,64]{1,0:T(8,128)}) custom-call(bf16[1024,256]{1,0:T(8,128)(2,1)} %bitcast.26, bf16[1024,256]{1,0:T(8,128)(2,1)} %bitcast.27, bf16[256,64]{1,0:T(8,128)(2,1)} %bitcast.29), custom_call_target="tpu_custom_call" | custom-call | flops 268435456 | bytes 1572864 | tf_op jit(solution)/shard_map/pre_grad/pallas_call | solution.py:57
  10.7 0.0 all-gather.6.cloned.1.call-update
  10.7 0.0 all-reduce.3.cloned.1.call-start
  10.8 0.5 all-reduce.3.cloned.1.call-update
  11.3 0.0 all-gather.4.cloned.1.call-start
  11.3 0.7 all-gather.4.cloned.1.call-update
  12.0 0.0 reduce-scatter.2.cloned.1.call-start
  12.1 0.8 slice_bitcast_fusion.4
  12.8 2.3 %collective-permute-start.1 = (bf16[128,128]{1,0:T(8,128)(2,1)S(1)}, bf16[128,128]{1,0:T(8,128)(2,1)S(1)}, u32[]{:S(2)}, u32[]{:S(2)}) collective-permute-start(bf16[128,128]{1,0:T(8,128)(2,1)S(1)} %slice_bitcast_fusion.4), channel_id=1, source_target_pairs={{0,8},{8,16},{16,24},{1,9},{9,17},{17,25},{2,10},{10,18},{18,26},{... | collective-permute-start | bytes 98312 | tf_op jit(solution)/shard_map/ppermute | solution.py:210
  15.2 0.8 collective-permute-done.1
  16.0 0.6 broadcast_select_fusion.prev_ref
  16.7 3.7 %taps.1 = bf16[1152,1024]{1,0:T(8,128)(2,1)} custom-call(bf16[32,128,128]{2,1,0:T(8,128)(2,1)} %image_ref.1, bf16[128,128]{1,0:T(8,128)(2,1)} %broadcast_select_fusion.prev_ref), custom_call_target="tpu_custom_call" | custom-call | flops 301989888 | bytes 3407872 | tf_op jit(solution)/shard_map/taps/pallas_call | solution.py:96
  20.3 67.3 %all-gather.6.cloned.1.call-done = bf16[8192,256]{1,0:T(8,128)(2,1)} async-done(((bf16[1024,256]{1,0:T(8,128)(2,1)}), bf16[8192,256]{1,0:T(8,128)(2,1)}) %all-gather.6.cloned.1.call-update) | async-done | bytes 4194320 | tf_op jit(solution)/shard_map/all_gather | solution.py:240
  87.7 0.0 copy-start
  87.7 3.6 %fusion = bf16[1152,2048]{0,1:T(8,128)(2,1)} fusion(bf16[1152,1024]{1,0:T(8,128)(2,1)} %taps.1, bf16[8192,256]{1,0:T(8,128)(2,1)} %all-gather.6.cloned.1.call-done), kind=kOutput, calls=%fused_computation.8 | convolution fusion | flops 604274688 | bytes 3473408 | tf_op jit(solution)/shard_map/dot_general | solution.py:22
  91.3 0.0 copy-done
  91.3 0.0 copy-start.2
  91.3 3.6 %fusion.1 = bf16[1152,2048]{0,1:T(8,128)(2,1)} fusion(bf16[1152,2048]{0,1:T(8,128)(2,1)} %fusion, bf16[1152,1024]{1,0:T(8,128)(2,1)} %taps.1, bf16[8192,256]{1,0:T(8,128)(2,1)S(1)} %copy-done), kind=kOutput, calls=%fused_computation.9 | convolution fusion | flops 604274688 | bytes 3473408 | tf_op jit(solution)/shard_map/dot_general | solution.py:22
  94.9 0.0 copy-done.2
  94.9 1.8 fusion.2
  96.6 1.8 %fusion.3 = bf16[1152,2048]{0,1:T(8,128)(2,1)} fusion(bf16[1152,2048]{0,1:T(8,128)(2,1)} %fusion.2, bf16[1152,1024]{1,0:T(8,128)(2,1)S(1)} %copy-done.2, bf16[8192,256]{1,0:T(8,128)(2,1)S(1)} %copy-done), kind=kOutput, calls=%fused_computation.11 | convolution fusion | flops 604274688 | bytes 3473408 | tf_op jit(solution)/shard_map/dot_general | solution.py:22
  98.4 1.8 fusion.4
  100.2 1.8 %fusion.5 = bf16[1152,2048]{0,1:T(8,128)(2,1)} fusion(bf16[1152,2048]{0,1:T(8,128)(2,1)} %fusion.4, bf16[1152,1024]{1,0:T(8,128)(2,1)S(1)} %copy-done.2, bf16[8192,256]{1,0:T(8,128)(2,1)S(1)} %copy-done), kind=kOutput, calls=%fused_computation.13 | convolution fusion | flops 604274688 | bytes 3473408 | tf_op jit(solution)/shard_map/dot_general | solution.py:22
  102.0 1.8 %fusion.6 = bf16[1152,2048]{0,1:T(8,128)(2,1)} fusion(bf16[1152,2048]{0,1:T(8,128)(2,1)} %fusion.5, bf16[1152,1024]{1,0:T(8,128)(2,1)S(1)} %copy-done.2, bf16[8192,256]{1,0:T(8,128)(2,1)S(1)} %copy-done), kind=kOutput, calls=%fused_computation.14 | convolution fusion | flops 604274688 | bytes 3473408 | tf_op jit(solution)/shard_map/dot_general | solution.py:22
  103.8 1.8 %fusion.7 = bf16[1152,2048]{0,1:T(8,128)(2,1)} fusion(bf16[1152,2048]{0,1:T(8,128)(2,1)} %fusion.6, bf16[1152,1024]{1,0:T(8,128)(2,1)S(1)} %copy-done.2, bf16[8192,256]{1,0:T(8,128)(2,1)S(1)} %copy-done), kind=kOutput, calls=%fused_computation.15 | convolution fusion | flops 604274688 | bytes 3473408 | tf_op jit(solution)/shard_map/dot_general | solution.py:22
  105.6 0.0 reduce-scatter.2.cloned.1.call-update
  105.6 0.8 slice.50
  106.4 1.3 collective-permute-start
  107.7 1.8 %collective-permute-done = bf16[64,256]{1,0:T(8,128)(2,1)S(1)} collective-permute-done((bf16[64,256]{1,0:T(8,128)(2,1)S(1)}, bf16[64,256]{1,0:T(8,128)(2,1)S(1)}, u32[]{:S(2)}, u32[]{:S(2)}) %collective-permute-start) | collective-permute-done | bytes 32800 | tf_op jit(solution)/shard_map/ppermute | solution.py:210
  109.5 30.9 %all_gather.12 = bf16[64,2048]{1,0:T(8,128)(2,1)S(1)} all-gather(bf16[64,256]{1,0:T(8,128)(2,1)S(1)} %broadcast_select_fusion.1), channel_id=1, replica_groups=mesh['pix'=4,'ch'=8] {'ch'}, dimensions={1}, use_global_device_ids=true | all-gather | bytes 294912 | tf_op jit(solution)/shard_map/all_gather | solution.py:235
  140.4 0.8 concatenate.6.halo_ref
  141.2 0.0 all-reduce.3.cloned.1.call-done
  141.2 1.6 broadcast_multiply_fusion
  142.8 0.0 all-gather.4.cloned.1.call-done
  142.8 0.0 copy-start.1
  142.8 4.8 %slice_bitcast_fusion = (bf16[1152,512]{1,0:T(8,128)(2,1)}, bf16[1152,512]{1,0:T(8,128)(2,1)}, bf16[1152,512]{1,0:T(8,128)(2,1)}, bf16[1152,512]{1,0:T(8,128)(2,1)}) fusion(bf16[4,1152,512]{2,1,0:T(8,128)(2,1)} %all-gather.4.cloned.1.call-done), kind=kLoop, calls=%fused_computation.17 | loop fusion | bytes 9437184 | tf_op jit(solution)/shard_map/squeeze | solution.py:247
  147.6 0.0 copy-done.1
  147.6 2.1 %fusion.16 = (bf16[1024,256]{1,0:T(8,128)(2,1)}, bf16[1024,256]{1,0:T(8,128)(2,1)}, bf16[1024,256]{1,0:T(8,128)(2,1)}, bf16[1024,256]{1,0:T(8,128)(2,1)}, bf16[1...) fusion(bf16[8192,256]{1,0:T(8,128)(2,1)S(1)} %copy-done.1), kind=kLoop, calls=%fused_computation.33 | loop fusion | bytes 8388608 | tf_op jit(solution)/shard_map/slice | solution.py:245
  149.7 16.3 %image_grad.1 = bf16[32,128,128]{2,1,0:T(8,128)(2,1)} custom-call(s32[12]{0:T(128)} %constant.11.clone.1.ids_ref, bf16[128,2048]{1,0:T(8,128)(2,1)} %concatenate.6.halo_ref, bf16[1024,256]{1,0:T(8,128)(2,1)} %get-tuple-element.21.refs_0_, bf16[1024,256]{1,0:T(8,128)(2,1)} %get-tuple-element.20.refs_1_, bf16[1024,256]{1,0:T(8,128)(2,1)} %get-tuple-element.19.refs_2_, ...), custom_call_target="tpu_custom_call" | custom-call | flops 4831838208 | bytes 8912896 | tf_op jit(solution)/shard_map/image_grad/pallas_call | solution.py:188
  166.1 0.0 reduce-scatter.2.cloned.1.call-done
  166.1 1.4 convert_multiply_fusion
  167.6 2.0 %copy.10 = f32[1152,512]{1,0:T(8,128)} copy(f32[1152,512]{0,1:T(8,128)S(1)} %convert_multiply_fusion) | data formatting | bytes 4718592 | tf_op jit(solution)/shard_map/mul | solution.py:243
  (1 shorter events, 0.0 us)
Async XLA Ops:
  8.0 79.7 %all-gather.6.cloned.1.call-start = ((), (), s32[]{:S(2)}) async-start(), calls=%async_computation.4 | async-start | bytes 4718592 | tf_op jit(solution)/shard_map/all_gather | solution.py:240
  10.7 130.5 %all-reduce.3.cloned.1.call-start = ((), (), s32[]{:S(2)}) async-start(), calls=%async_computation.3 | async-start | bytes 262144 | tf_op jit(solution)/shard_map/psum | solution.py:232
  11.3 131.5 %all-gather.4.cloned.1.call-start = ((), (), s32[]{:S(2)}) async-start(), calls=%async_computation.1 | async-start | bytes 5898240 | tf_op jit(solution)/shard_map/all_gather | solution.py:241
  12.0 154.1 %reduce-scatter.2.cloned.1.call-start = ((), (), s32[]{:S(2)}) async-start(), calls=%async_computation.2 | async-start | bytes 5898240 | tf_op jit(solution)/shard_map/reduce_scatter | solution.py:243
  12.8 3.2 %collective-permute-start.1 = (bf16[128,128]{1,0:T(8,128)(2,1)S(1)}, bf16[128,128]{1,0:T(8,128)(2,1)S(1)}, u32[]{:S(2)}, u32[]{:S(2)}) collective-permute-start(bf16[128,128]{1,0:T(8,128)(2,1)S(1)} %slice_bitcast_fusion.4), channel_id=1, source_target_pairs={{0,8},{8,16},{16,24},{1,9},{9,17},{17,25},{2,10},{10,18},{18,26},{... | collective-permute-start | bytes 98312 | tf_op jit(solution)/shard_map/ppermute | solution.py:210
  87.7 3.6 %copy-start = (bf16[8192,256]{1,0:T(8,128)(2,1)S(1)}, bf16[8192,256]{1,0:T(8,128)(2,1)}, u32[]{:S(2)}) copy-start(bf16[8192,256]{1,0:T(8,128)(2,1)} %all-gather.6.cloned.1.call-done) | copy-start | bytes 12582916
  91.3 3.6 %copy-start.2 = (bf16[1152,1024]{1,0:T(8,128)(2,1)S(1)}, bf16[1152,1024]{1,0:T(8,128)(2,1)}, u32[]{:S(2)}) copy-start(bf16[1152,1024]{1,0:T(8,128)(2,1)} %taps.1) | copy-start | bytes 7077892
  106.4 3.1 %collective-permute-start = (bf16[64,256]{1,0:T(8,128)(2,1)S(1)}, bf16[64,256]{1,0:T(8,128)(2,1)S(1)}, u32[]{:S(2)}, u32[]{:S(2)}) collective-permute-start(bf16[64,256]{1,0:T(8,128)(2,1)S(1)} %slice.50), channel_id=1, source_target_pairs={{8,0},{16,8},{24,16},{9,1},{17,9},{25,17},{10,2},{18,10},{26,18},{... | collective-permute-start | bytes 98312 | tf_op jit(solution)/shard_map/ppermute | solution.py:210
  142.8 4.8 %copy-start.1 = (bf16[8192,256]{1,0:T(8,128)(2,1)S(1)}, bf16[8192,256]{1,0:T(8,128)(2,1)}, u32[]{:S(2)}) copy-start(bf16[8192,256]{1,0:T(8,128)(2,1)} %all-gather.6.cloned.1.call-done) | copy-start | bytes 12582916
Sparse Core Ops, SparseCore 0:
  11.5 76.0 all-gather.5
  89.2 36.0 all-gather.3
Sparse Core Ops, SparseCore 1:
  14.1 34.0 all-reduce.2
  105.7 46.0 reduce-scatter.1

commit v2 on v1

--- a/solution.py
+++ b/solution.py
@@ -11,11 +11,11 @@
 GROUP_WIDTH = 64
 BF = jnp.bfloat16
 F32 = jnp.float32
-VMEM_LIMIT = 56 * 2**20
-
-
-def params():
-    return pltpu.CompilerParams(vmem_limit_bytes=VMEM_LIMIT)
+SMALL = pl.CostEstimate(flops=1, bytes_accessed=1, transcendentals=0)
+
+
+def params(mebibytes):
+    return pltpu.CompilerParams(vmem_limit_bytes=mebibytes * 2**20)
 
 
 def dot_nn(a, b):
@@ -60,10 +60,8 @@
             jax.ShapeDtypeStruct((pixels, chans), BF),
             jax.ShapeDtypeStruct((chans, GROUP_WIDTH), F32),
         ),
-        compiler_params=params(),
-        cost_estimate=pl.CostEstimate(
-            flops=4 * pixels * chans * chans, bytes_accessed=6 * pixels * chans, transcendentals=pixels * chans
-        ),
+        compiler_params=params(56),
+        cost_estimate=SMALL,
         name="pre_grad",
     )(grad_out, pre_act, mix_weight)
 
@@ -96,19 +94,27 @@
     return pl.pallas_call(
         taps_kernel,
         out_shape=jax.ShapeDtypeStruct((9 * chans, pixels), BF),
-        compiler_params=params(),
-        cost_estimate=pl.CostEstimate(
-            flops=rows * chans * width * width * 9 // 2, bytes_accessed=13 * rows * chans * width // 2, transcendentals=0
-        ),
+        compiler_params=params(24),
+        cost_estimate=SMALL,
         name="taps",
     )(image_in, prev_row)
 
 
+def grad_place(place_ref, flips, index):
+    if not flips:
+        return index
+    return ((place_ref[1] + 8 - 2 * (index % 4)) & 7) ^ (index // 4)
+
+
+def part_place(place_ref, flips, index):
+    return place_ref[0] ^ index if flips else index
+
+
 def image_kernel(
-    grad_count, part_count, width, ids_ref, halo_ref, *refs
+    grad_count, part_count, flips, width, place_ref, halo_ref, *refs
 ):
     grads, parts = refs[:grad_count], refs[grad_count : grad_count + part_count]
-    out_ref, grad_all, part_all, grad_sem, part_sem = refs[grad_count + part_count :]
+    out_ref, grad_all, part_all, values, grad_sem, part_sem = refs[grad_count + part_count :]
     pixels, span = grads[0].shape
     outs, part_span = parts[0].shape
     chans = outs // 9
@@ -116,21 +122,23 @@
     tiles = pixels // tile
 
     def part_copy(index):
-        start = pl.multiple_of(ids_ref[grad_count + index] * part_span, part_span)
+        start = pl.multiple_of(part_place(place_ref, flips, index) * part_span, part_span)
         return pltpu.make_async_copy(
             parts[index], part_all.at[:, pl.ds(start, part_span)], part_sem.at[index]
         )
 
-    def grad_copy(index):
-        start = pl.multiple_of(ids_ref[index] * span, span)
+    def grad_copy(index, step):
+        start = pl.multiple_of(grad_place(place_ref, flips, index) * span, span)
+        rows = pl.ds(step * tile, tile)
         return pltpu.make_async_copy(
-            grads[index], grad_all.at[:, pl.ds(start, span)], grad_sem.at[index]
+            grads[index].at[rows], grad_all.at[rows, pl.ds(start, span)], grad_sem.at[index, step]
         )
 
     for index in range(part_count):
         part_copy(index).start()
-    for index in range(grad_count):
-        grad_copy(index).start()
+    for step in reversed(range(tiles)):
+        for index in range(grad_count):
+            grad_copy(index, step).start()
 
     lane = iota((chans, tile), 1)
     last_col = lane % width == width - 1
@@ -151,11 +159,11 @@
 
     for index in range(part_count):
         part_copy(index).wait()
-    for index in range(grad_count):
-        grad_copy(index).wait()
-    halo = dot_nt(part_all[: 3 * chans], halo_ref[...])
-    below = up_terms(jnp.concatenate([halo, jnp.zeros_like(halo)], axis=1))
+    wide = jnp.concatenate([halo_ref[...]] * 2, axis=1)
+    below = (wide[:chans], wide[chans:])
     for step in reversed(range(tiles)):
+        for index in range(grad_count):
+            grad_copy(index, step).wait()
         terms = dot_nt(part_all[...], grad_all[step * tile : (step + 1) * tile])
         own = up_terms(terms[: 3 * chans])
         tap = lambda index: terms[index * chans : (index + 1) * chans]
@@ -171,20 +179,25 @@
             even, odd = (value.astype(BF) for value in phases[parity])
             for pair in range(2):
                 cols = slice(pair * 2 * width, (pair + 1) * 2 * width)
-                placed = dot_nn(jnp.concatenate([even[:, cols], odd[:, cols]], axis=1), place).astype(BF)
+                rows = slice((2 * parity + pair) * chans, (2 * parity + pair + 1) * chans)
+                values[rows, : 2 * width] = even[:, cols]
+                values[rows, 2 * width :] = odd[:, cols]
+        placed = dot_nn(values[...], place).astype(BF)
+        for parity in range(2):
+            for pair in range(2):
+                rows = slice((2 * parity + pair) * chans, (2 * parity + pair + 1) * chans)
                 first = 8 * step + 4 * pair + parity
-                out_ref[first] = placed[:, : 2 * width]
-                out_ref[first + 2] = placed[:, 2 * width :]
-
-
-def image_gradient(grads, grad_ids, parts, part_ids, halo, width):
+                out_ref[first] = placed[rows, : 2 * width]
+                out_ref[first + 2] = placed[rows, 2 * width :]
+
+
+def image_gradient(place, flips, grads, parts, halo, width):
     pixels, span = grads[0].shape
     outs, part_span = parts[0].shape
     full = span * len(grads)
     chans = outs // 9
-    ids = jnp.stack([jnp.asarray(value, jnp.int32) for value in (*grad_ids, *part_ids)])
-    kernel = functools.partial(image_kernel, len(grads), len(parts), width)
-    anywhere = pl.BlockSpec(memory_space=pl.ANY)
+    kernel = functools.partial(image_kernel, len(grads), len(parts), flips, width)
+    anywhere = pl.BlockSpec(memory_space=pltpu.HBM)
     return pl.pallas_call(
         kernel,
         out_shape=jax.ShapeDtypeStruct((2 * pixels // width, chans, 2 * width), BF),
@@ -194,15 +207,141 @@
         scratch_shapes=[
             pltpu.VMEM((pixels, full), BF),
             pltpu.VMEM((outs, full), BF),
+            pltpu.VMEM((4 * chans, 4 * width), BF),
+            pltpu.SemaphoreType.DMA((len(grads), pixels // (4 * width))),
+            pltpu.SemaphoreType.DMA((len(parts),)),
+        ],
+        compiler_params=params(32),
+        cost_estimate=SMALL,
+        name="image_grad",
+    )(place, halo, *grads, *parts)
+
+
+def edge_kernel(grad_count, part_count, flips, width, place_ref, *refs):
+    grads, parts = refs[:grad_count], refs[grad_count : grad_count + part_count]
+    out_ref, grad_all, part_all, grad_sem, part_sem = refs[grad_count + part_count :]
+    span = grads[0].shape[1]
+    outs, part_span = parts[0].shape
+    chans = outs // 9
+    tops = 3 * chans
+    copies = []
+    for index in range(part_count):
+        start = pl.multiple_of(part_place(place_ref, flips, index) * part_span, part_span)
+        copies.append(
+            pltpu.make_async_copy(
+                parts[index].at[pl.ds(0, tops)], part_all.at[:, pl.ds(start, part_span)], part_sem.at[index]
+            )
+        )
+    for index in range(grad_count):
+        start = pl.multiple_of(grad_place(place_ref, flips, index) * span, span)
+        copies.append(
+            pltpu.make_async_copy(
+                grads[index].at[pl.ds(0, 2 * width)], grad_all.at[:, pl.ds(start, span)], grad_sem.at[index]
+            )
+        )
+    for copy in copies:
+        copy.start()
+    for copy in copies:
+        copy.wait()
+    terms = dot_nt(part_all[...], grad_all[...])
+    lane = iota((chans, 2 * width), 1)
+    moved = jnp.where(lane % width == width - 1, 0.0, pltpu.roll(terms[:chans], 2 * width - 1, 1))
+    even, odd = terms[chans : 2 * chans], terms[2 * chans :] + moved
+    out_ref[:chans] = pltpu.roll(even, width, 1)
+    out_ref[chans:] = pltpu.roll(odd, width, 1)
+
+
+def edge_terms(place, flips, grads, parts, width):
+    span = grads[0].shape[1]
+    outs, part_span = parts[0].shape
+    full = span * len(grads)
+    kernel = functools.partial(edge_kernel, len(grads), len(parts), flips, width)
+    anywhere = pl.BlockSpec(memory_space=pltpu.HBM)
+    return pl.pallas_call(
+        kernel,
+        out_shape=jax.ShapeDtypeStruct((2 * outs // 9, 2 * width), F32),
+        in_specs=[pl.BlockSpec(memory_space=pltpu.SMEM)] + [anywhere] * (len(grads) + len(parts)),
+        out_specs=pl.BlockSpec(memory_space=pltpu.VMEM),
+        scratch_shapes=[
+            pltpu.VMEM((2 * width, full), BF),
+            pltpu.VMEM((outs // 3, full), BF),
             pltpu.SemaphoreType.DMA((len(grads),)),
             pltpu.SemaphoreType.DMA((len(parts),)),
         ],
-        compiler_params=params(),
-        cost_estimate=pl.CostEstimate(
-            flops=2 * pixels * outs * full, bytes_accessed=2 * full * (pixels + outs), transcendentals=0
-        ),
-        name="image_grad",
-    )(ids, halo, *grads, *parts)
+        compiler_params=params(16),
+        cost_estimate=SMALL,
+        name="edge",
+    )(place, *grads, *parts)
+
+
+CUTS = 3
+
+
+def partial_kernel(count, chosen_blocks, place_ref, taps_ref, *refs):
+    picks = len(chosen_blocks)
+    core, turn = place_ref[0] & 1, (place_ref[1] >> 1) & 1
+    blocks, outs = refs[:count], refs[count : count + picks]
+    taps, grads, sums, grad_sems, taps_sems, out_sems = refs[count + picks :]
+    rows = taps.shape[1]
+    part = lambda ref, cut: ref.at[pl.ds(cut * rows, rows)]
+
+    def chosen(pick, index):
+        return pltpu.make_async_copy(blocks[index], grads.at[pick], grad_sems.at[pick])
+
+    def out_copy(pick, cut):
+        return pltpu.make_async_copy(sums.at[pick, cut], part(outs[pick], cut), out_sems.at[pick, cut])
+
+    taps_in = [pltpu.make_async_copy(part(taps_ref, cut), taps.at[cut], taps_sems.at[cut]) for cut in range(CUTS)]
+
+    def start(pick):
+        kept, phase, base = chosen_blocks[pick]
+        step = base + ((2 * phase + (core if kept else 1 - core) + turn) & 3)
+        for index in range(count):
+
+            @pl.when(step == index)
+            def _():
+                chosen(pick, index).start()
+
+    start(0)
+    for copy in taps_in:
+        copy.start()
+    for pick in range(1, picks):
+        start(pick)
+    for pick in range(picks):
+        chosen(pick, 0).wait()
+        for cut in range(CUTS):
+            if pick == 0:
+                taps_in[cut].wait()
+            sums[pick, cut] = dot_nn(taps[cut], grads[pick]).astype(BF)
+            out_copy(pick, cut).start()
+    for pick in range(picks):
+        for cut in range(CUTS):
+            out_copy(pick, cut).wait()
+
+
+def kernel_partials(place, taps, blocks, chosen):
+    outs, pixels = taps.shape
+    span = blocks[0].shape[1]
+    rows = outs // CUTS
+    picks = len(chosen)
+    anywhere = pl.BlockSpec(memory_space=pltpu.HBM)
+    return pl.pallas_call(
+        functools.partial(partial_kernel, len(blocks), tuple(chosen)),
+        out_shape=(jax.ShapeDtypeStruct((outs, span), BF),) * picks,
+        in_specs=[pl.BlockSpec(memory_space=pltpu.SMEM)] + [anywhere] * (1 + len(blocks)),
+        out_specs=(anywhere,) * picks,
+        scratch_shapes=[
+            pltpu.VMEM((CUTS, rows, pixels), BF),
+            pltpu.VMEM((picks, pixels, span), BF),
+            pltpu.VMEM((picks, CUTS, rows, span), BF),
+            pltpu.SemaphoreType.DMA((picks,)),
+            pltpu.SemaphoreType.DMA((CUTS,)),
+            pltpu.SemaphoreType.DMA((picks, CUTS)),
+        ],
+        compiler_params=params(16),
+        cost_estimate=SMALL,
+        name="partials",
+    )(place, taps, *blocks)
 
 
 def step_along(value, axis, steps):
@@ -212,44 +351,123 @@
     )
 
 
+def swap(value, axis, bits):
+    return lax.ppermute(value, axis, [(source, source ^ bits) for source in range(lax.axis_size(axis))])
+
+
+def kernel_sum_plain(taps, grads):
+    partial = jnp.concatenate([dot_nn(taps, grad).astype(BF) for grad in grads], axis=1)
+    return lax.psum_scatter(partial, "pix", scatter_dimension=1, tiled=True).astype(F32)
+
+
+def kept_step(core, outer, phase):
+    return (2 * phase + core + outer % 2) % 4
+
+
+def kept_here(pix, outer, phase):
+    return (outer - kept_step(pix % 2, outer, phase)) % 4 // 2 == pix // 2
+
+
+def send_over(value, phase):
+    pairs = []
+    for pix in range(4):
+        for ch in range(8):
+            if not kept_here(pix, ch // 2, phase):
+                pairs.append((pix * 8 + ch, (pix ^ 2) * 8 + ch))
+    return lax.ppermute(value, ("pix", "ch"), pairs)
+
+
+def ring(value):
+    return lax.ppermute(value, "ch", [(source, (source + 2) % 8) for source in range(8)])
+
+
 def shards(image_in, pre_act, grad_out, conv_weight, mix_weight):
     tile_rows, width, chans = grad_out.shape
     in_chans = image_in.shape[1]
     pix_count, ch_count = lax.axis_size("pix"), lax.axis_size("ch")
-    pix_index = lax.axis_index("pix")
-    first_tile = pix_index % TILES == 0
-    last_tile = pix_index % TILES == TILES - 1
+    pix, ch = lax.axis_index("pix"), lax.axis_index("ch")
+    first_tile = pix % TILES == 0
+    last_tile = pix % TILES == TILES - 1
     pixels = tile_rows * width
     scale = 1.0 / float(pix_count * pixels) ** 0.5
 
+    tie = lax.optimization_barrier
+    place = jnp.stack([pix, ch]).astype(jnp.int32)
     prev_row = step_along(image_in[-1], "pix", 1)
-    prev_row = jnp.where(first_tile, jnp.zeros_like(prev_row), prev_row)
     grad_pre, mix_part = pre_gradient(
         grad_out.reshape(pixels, chans),
         pre_act.reshape(pixels, chans),
         mix_weight.reshape(chans, GROUP_WIDTH),
     )
-    grad_mix = (lax.psum(mix_part, "pix") * scale).reshape(mix_weight.shape)
-    halo = step_along(grad_pre[:width], "pix", -1)
-    halo = jnp.where(last_tile, jnp.zeros_like(halo), halo)
-    halo_all = lax.all_gather(halo, "ch", axis=1, tiled=True)
-    halo_all = jnp.concatenate([halo_all, jnp.zeros_like(halo_all)], axis=0)
     kernel_own = conv_weight.reshape(9 * in_chans, -1)
-    taps = image_taps(image_in, prev_row)
-
-    grad_all = lax.all_gather(grad_pre, "ch", axis=0)
-    kernel_all = lax.all_gather(kernel_own, "pix", axis=0)
-    partial = jnp.concatenate([dot_nn(taps, grad_all[index]).astype(BF) for index in range(ch_count)], axis=1)
-    grad_conv = lax.psum_scatter(partial, "pix", scatter_dimension=1, tiled=True).astype(F32) * scale
-    grad_in = image_gradient(
-        [grad_all[index] for index in range(ch_count)],
-        range(ch_count),
-        [kernel_all[index] for index in range(pix_count)],
-        range(pix_count),
-        halo_all,
-        width,
-    )
-    return (grad_in, grad_conv.reshape(conv_weight.shape), grad_mix)
+    rings = pix_count == 4 and ch_count == 8
+    if rings:
+        mix_other = swap(mix_part, "pix", 2)
+        kernel_own, prev_row, mix_other = tie((kernel_own, prev_row, mix_other))
+    taps = image_taps(image_in, jnp.where(first_tile, jnp.zeros_like(prev_row), prev_row))
+
+    if rings:
+        kernel_x = swap(kernel_own, "pix", 2)
+        kernel_core = swap(kernel_own, "pix", 1)
+        mix_sum = mix_part + mix_other
+        mix_sum = mix_sum + swap(mix_sum, "pix", 1)
+        near, far = [grad_pre], [swap(grad_pre, "ch", 1)]
+        totals, arrived = [[None] * 2, [None] * 2], [[None] * 2, [None] * 2]
+
+        def add_up(sums, phase, half):
+            total = sums[1] + swap(sums[0], "pix", 1)
+            totals[phase][half] = total
+            arrived[phase][half] = send_over(total, phase)
+
+        near.append(ring(near[0]))
+        near[1], far[0], taps, mix_sum = tie((near[1], far[0], taps, mix_sum))
+        far.append(swap(near[1], "ch", 1))
+        near.append(ring(near[1]))
+        near[2], far[1], kernel_core = tie((near[2], far[1], kernel_core))
+        far.append(swap(near[2], "ch", 1))
+        near.append(ring(near[2]))
+        first = kernel_partials(place, taps, near[:3], [(0, 0, 0), (1, 0, 0)])
+        near[3], far[2], first = tie((near[3], far[2], first))
+        far.append(swap(near[3], "ch", 1))
+        add_up(first, 0, 0)
+        kernel_xcore = swap(kernel_x, "pix", 1)
+        second = kernel_partials(
+            place, taps, near + far[:3], [(0, 0, 4), (0, 1, 0), (1, 0, 4), (1, 1, 0)]
+        )
+        far[3], arrived[0][0], second, kernel_xcore = tie((far[3], arrived[0][0], second, kernel_xcore))
+        add_up(second[::2], 0, 1)
+        add_up(second[1::2], 1, 0)
+        third = kernel_partials(place, taps, far, [(0, 1, 0), (1, 1, 0)])
+        third, _ = tie((third, (totals[0][1], totals[1][0])))
+        add_up(third, 1, 1)
+        core, outer, side = pix % 2, ch // 2, ch % 2
+        mine = kept_here(pix, outer, 0)
+        halves = [
+            jnp.where(mine, totals[0][half], totals[1][half]).astype(F32)
+            + jnp.where(mine, arrived[0][half], arrived[1][half]).astype(F32)
+            for half in range(2)
+        ]
+        grad_conv = jnp.concatenate(
+            [jnp.where(side == 0, halves[0], halves[1]), jnp.where(side == 0, halves[1], halves[0])], axis=1
+        )
+        grads = near + far
+        parts = [kernel_own, kernel_core, kernel_x, kernel_xcore]
+        edge_at, _ = tie((place, third))
+        image_at = (place, totals[1][1])
+    else:
+        mix_sum = lax.psum(mix_part, "pix")
+        grad_all = lax.all_gather(grad_pre, "ch", axis=0)
+        kernel_all = lax.all_gather(kernel_own, "pix", axis=0)
+        grads = [grad_all[index] for index in range(ch_count)]
+        parts = [kernel_all[index] for index in range(pix_count)]
+        grad_conv = kernel_sum_plain(taps, grads)
+        edge_at, image_at = place, (place,)
+    edge = step_along(edge_terms(edge_at, rings, grads, parts, width), "pix", -1)
+    edge = jnp.where(last_tile, jnp.zeros_like(edge), edge)
+    image_at = tie(image_at)[0]
+    grad_in = image_gradient(image_at, rings, grads, parts, edge, width)
+    grad_mix = (mix_sum * scale).reshape(mix_weight.shape)
+    return (grad_in, (grad_conv * scale).reshape(conv_weight.shape), grad_mix)
 
 
 def solution(mesh):

time: 177 us -> 129 us (0.73)
  the two profiles are of different devices: /device:TPU:0 before, /device:TPU:1 now
where the time goes in v2:
time: 129 us; the launch traced here: 127 us
  Pallas kernels  44.3 us (34%)
  starting transfers between devices  34.1 us (26%)
  waiting for transfers between devices  33.9 us (26%)
  other arithmetic  8.76 us (7%)
  local copies, waits for them, and re-layouts  4.61 us (4%)
    ppermute x13, waiting for transfers between devices, swap(): lax.ppermute(value, axis, [(source, source ^ bits) for source in range(la...  23.6 us
    pallas_call x3, Pallas kernels, kernel_partials(): pl.pallas_call(functools.partial(partial_kernel, len(blocks), tuple(chose...  22.8 us
    pallas_call x1, Pallas kernels, image_gradient(): pl.pallas_call(kernel, out_shape=jax.ShapeDtypeStruct((2 * pixels // widt...  15.3 us
    ppermute x13, starting transfers between devices, swap(): lax.ppermute(value, axis, [(source, source ^ bits) for source in range(la...  13.5 us
    ppermute x4, starting transfers between devices, send_over(): return lax.ppermute(value, ('pix', 'ch'), pairs)  12.8 us
    ppermute x2, starting transfers between devices, step_along(): lax.ppermute(value, axis, [(source, source + steps) for source in range(c...  6.55 us
    ppermute x3, waiting for transfers between devices, ring(): lax.ppermute(value, 'ch', [(source, (source + 2) % 8) for source in range...  6.31 us
    ppermute x2, waiting for transfers between devices, step_along(): lax.ppermute(value, axis, [(source, source + steps) for source in range(c...  3.99 us
  transfers between devices with their start and end apart: 22, of which 9 were waited for; matrix products, arithmetic and copies ran while one was open for 4% of the time, Pallas kernels for 33%

profile of v2, /device:TPU:1, one launch (start us, length us, event | category | flops | bytes accessed | tf_op | source)
XLA Modules:
  0.0 126.7 jit_solution(9478118266965183659)
XLA Ops:
  0.6 2.6 %pre_grad.1 = (bf16[1024,256]{1,0:T(8,128)(2,1)}, f32[256,64]{1,0:T(8,128)}) custom-call(bf16[1024,256]{1,0:T(8,128)(2,1)} %bitcast.13, bf16[1024,256]{1,0:T(8,128)(2,1)} %bitcast.14, bf16[256,64]{1,0:T(8,128)(2,1)} %bitcast.16), custom_call_target="tpu_custom_call" | custom-call | flops 1 | bytes 1 | tf_op jit(solution)/shard_map/pre_grad/pallas_call | solution.py:57
  3.3 2.0 %collective-permute-start.3 = (f32[256,64]{1,0:T(8,128)}, f32[256,64]{1,0:T(8,128)S(1)}, u32[]{:S(2)}, u32[]{:S(2)}) collective-permute-start(f32[256,64]{1,0:T(8,128)} %get-tuple-element.39), channel_id=1, source_target_pairs={{0,16},{8,24},{16,0},{24,8},{1,17},{9,25},{17,1},{25,9},{2,18},{10... | collective-permute-start | bytes 196616 | tf_op jit(solution)/shard_map/ppermute | solution.py:355
  5.3 0.8 slice_bitcast_fusion
  6.1 2.5 %collective-permute-start.2 = (bf16[128,128]{1,0:T(8,128)(2,1)S(1)}, bf16[128,128]{1,0:T(8,128)(2,1)S(1)}, u32[]{:S(2)}, u32[]{:S(2)}) collective-permute-start(bf16[128,128]{1,0:T(8,128)(2,1)S(1)} %slice_bitcast_fusion), channel_id=1, source_target_pairs={{0,8},{8,16},{16,24},{1,9},{9,17},{17,25},{2,10},{10,18},{18,26},{... | collective-permute-start | bytes 98312 | tf_op jit(solution)/shard_map/ppermute | solution.py:349
  8.5 1.0 collective-permute-done.2
  9.5 0.4 collective-permute-start.7
  10.0 1.5 %collective-permute-start.1 = (bf16[1024,256]{1,0:T(8,128)(2,1)}, bf16[1024,256]{1,0:T(8,128)(2,1)S(1)}, u32[]{:S(2)}, u32[]{:S(2)}) collective-permute-start(bf16[1024,256]{1,0:T(8,128)(2,1)} %get-tuple-element.38.refs_0_), channel_id=1, source_target_pairs={{0,1},{1,0},{2,3},{3,2},{4,5},{5,4},{6,7},{7,6},{8,9},{9,8},{10,11... | collective-permute-start | bytes 1572872 | tf_op jit(solution)/shard_map/ppermute | solution.py:355
  11.5 1.3 %collective-permute-start = (bf16[1024,256]{1,0:T(8,128)(2,1)}, bf16[1024,256]{1,0:T(8,128)(2,1)}, u32[]{:S(2)}, u32[]{:S(2)}) collective-permute-start(bf16[1024,256]{1,0:T(8,128)(2,1)} %get-tuple-element.38.refs_0_), channel_id=1, source_target_pairs={{0,2},{1,3},{2,4},{3,5},{4,6},{5,7},{6,0},{7,1},{8,10},{9,11},{10,... | collective-permute-start | bytes 1572872 | tf_op jit(solution)/shard_map/ppermute | solution.py:381
  12.8 2.3 %collective-permute-start.13 = (bf16[1152,512]{1,0:T(8,128)(2,1)}, bf16[1152,512]{1,0:T(8,128)(2,1)}, u32[]{:S(2)}, u32[]{:S(2)}) collective-permute-start(bf16[1152,512]{1,0:T(8,128)(2,1)} %bitcast.5.refs_8_), channel_id=1, source_target_pairs={{0,16},{8,24},{16,0},{24,8},{1,17},{9,25},{17,1},{25,9},{2,18},{10... | collective-permute-start | bytes 3538952 | tf_op jit(solution)/shard_map/ppermute | solution.py:355
  15.0 0.9 add.51
  16.0 0.9 collective-permute-start.4
  16.9 1.2 copy-done.8
  18.1 1.1 taps.1.taps_ref
  19.2 4.6 %collective-permute-done.1.refs_4_.refs_0_ = bf16[1024,256]{1,0:T(8,128)(2,1)S(1)} collective-permute-done((bf16[1024,256]{1,0:T(8,128)(2,1)}, bf16[1024,256]{1,0:T(8,128)(2,1)S(1)}, u32[]{:S(2)}, u32[]{:S(2)}) %collective-permute-start.1) | collective-permute-done | bytes 524320 | tf_op jit(solution)/shard_map/ppermute | solution.py:355
  23.8 2.8 %collective-permute-done.refs_1_ = bf16[1024,256]{1,0:T(8,128)(2,1)} collective-permute-done((bf16[1024,256]{1,0:T(8,128)(2,1)}, bf16[1024,256]{1,0:T(8,128)(2,1)}, u32[]{:S(2)}, u32[]{:S(2)}) %collective-permute-start) | collective-permute-done | bytes 524320 | tf_op jit(solution)/shard_map/ppermute | solution.py:381
  26.6 0.4 collective-permute-start.6
  27.0 11.9 %collective-permute-done.6.refs_5_.refs_1_ = bf16[1024,256]{1,0:T(8,128)(2,1)S(1)} collective-permute-done((bf16[1024,256]{1,0:T(8,128)(2,1)}, bf16[1024,256]{1,0:T(8,128)(2,1)S(1)}, u32[]{:S(2)}, u32[]{:S(2)}) %collective-permute-start.6) | collective-permute-done | bytes 524320 | tf_op jit(solution)/shard_map/ppermute | solution.py:355
  38.9 0.8 copy-done.1
  39.7 1.4 %collective-permute-done.5.refs_2_ = bf16[1024,256]{1,0:T(8,128)(2,1)} collective-permute-done((bf16[1024,256]{1,0:T(8,128)(2,1)}, bf16[1024,256]{1,0:T(8,128)(2,1)}, u32[]{:S(2)}, u32[]{:S(2)}) %collective-permute-start.5) | collective-permute-done | bytes 524320 | tf_op jit(solution)/shard_map/ppermute | solution.py:381
  41.1 0.8 collective-permute-start.9
  41.9 0.1 pad_add_fusion.place_ref
  42.0 5.7 %partials.3 = (bf16[1152,256]{1,0:T(8,128)(2,1)S(1)}, bf16[1152,256]{1,0:T(8,128)(2,1)S(1)}) custom-call(s32[2]{0:T(128)S(1)} %pad_add_fusion.place_ref, bf16[1152,1024]{1,0:T(8,128)(2,1)S(1)} %taps.1.taps_ref, bf16[1024,256]{1,0:T(8,128)(2,1)S(1)} %copy-done, bf16[1024,256]{1,0:T(8,128)(2,1)} %collective-permute-done.refs_1_, ...), custom_call_target="tpu_custom_call" | custom-call | flops 1 | bytes 1 | tf_op jit(solution)/shard_map/partials/pallas_call | solution.py:328
  47.7 4.8 %collective-permute-done.9.refs_6_.refs_2_ = bf16[1024,256]{1,0:T(8,128)(2,1)} collective-permute-done((bf16[1024,256]{1,0:T(8,128)(2,1)}, bf16[1024,256]{1,0:T(8,128)(2,1)}, u32[]{:S(2)}, u32[]{:S(2)}) %collective-permute-start.9) | collective-permute-done | bytes 524320 | tf_op jit(solution)/shard_map/ppermute | solution.py:355
  52.4 2.1 %collective-permute-done.8.refs_3_ = bf16[1024,256]{1,0:T(8,128)(2,1)} collective-permute-done((bf16[1024,256]{1,0:T(8,128)(2,1)}, bf16[1024,256]{1,0:T(8,128)(2,1)}, u32[]{:S(2)}, u32[]{:S(2)}) %collective-permute-start.8) | collective-permute-done | bytes 524320 | tf_op jit(solution)/shard_map/ppermute | solution.py:381
  54.5 3.8 %collective-permute-start.11 = (bf16[1152,256]{1,0:T(8,128)(2,1)S(1)}, bf16[1152,256]{1,0:T(8,128)(2,1)S(1)}, u32[]{:S(2)}, u32[]{:S(2)}) collective-permute-start(bf16[1152,256]{1,0:T(8,128)(2,1)S(1)} %get-tuple-element.53), channel_id=1, source_target_pairs={{0,8},{8,0},{16,24},{24,16},{1,9},{9,1},{17,25},{25,17},{2,10},{10... | collective-permute-start | bytes 1769480 | tf_op jit(solution)/shard_map/ppermute | solution.py:355
  58.4 0.0 collective-permute-start.14
  58.4 2.4 %collective-permute-done.11 = bf16[1152,256]{1,0:T(8,128)(2,1)S(1)} collective-permute-done((bf16[1152,256]{1,0:T(8,128)(2,1)S(1)}, bf16[1152,256]{1,0:T(8,128)(2,1)S(1)}, u32[]{:S(2)}, u32[]{:S(2)}) %collective-permute-start.11) | collective-permute-done | bytes 589856 | tf_op jit(solution)/shard_map/ppermute | solution.py:355
  60.8 0.2 add.53
  60.9 5.0 %collective-permute-start.12 = (bf16[1152,256]{1,0:T(8,128)(2,1)S(1)}, bf16[1152,256]{1,0:T(8,128)(2,1)S(1)}, u32[]{:S(2)}, u32[]{:S(2)}) collective-permute-start(bf16[1152,256]{1,0:T(8,128)(2,1)S(1)} %add.53), channel_id=1, source_target_pairs={{4,20},{5,21},{6,22},{7,23},{8,24},{9,25},{10,26},{11,27},{16,0},{... | collective-permute-start | bytes 1769480 | tf_op jit(solution)/shard_map/ppermute | solution.py:377
  66.0 0.7 collective-permute-start.10
  66.7 10.6 %partials.4 = (bf16[1152,256]{1,0:T(8,128)(2,1)S(1)}, bf16[1152,256]{1,0:T(8,128)(2,1)S(1)}, bf16[1152,256]{1,0:T(8,128)(2,1)S(1)}, bf16[1152,256]{1,0:T(8,128)(2,1)S(1)}) custom-call(s32[2]{0:T(128)S(1)} %pad_add_fusion.place_ref, bf16[1152,1024]{1,0:T(8,128)(2,1)S(1)} %taps.1.taps_ref, bf16[1024,256]{1,0:T(8,128)(2,1)S(1)} %copy-done, ...), custom_call_target="tpu_custom_call" | custom-call | flops 1 | bytes 1 | tf_op jit(solution)/shard_map/partials/pallas_call | solution.py:328
  77.4 1.0 copy-done.4
  78.4 0.5 collective-permute-start.16
  78.9 6.5 %partials.5 = (bf16[1152,256]{1,0:T(8,128)(2,1)S(1)}, bf16[1152,256]{1,0:T(8,128)(2,1)S(1)}) custom-call(s32[2]{0:T(128)S(1)} %pad_add_fusion.place_ref, bf16[1152,1024]{1,0:T(8,128)(2,1)S(1)} %taps.1.taps_ref, bf16[1024,256]{1,0:T(8,128)(2,1)S(1)} %collective-permute-done.1.refs_4_.refs_0_, bf16[1024,256]{1,0:T(8,128)(2,1)S(1)} %copy-done.2, ...), custom_call_target="tpu_custom_call" | custom-call | flops 1 | bytes 1 | tf_op jit(solution)/shard_map/partials/pallas_call | solution.py:328
  85.5 0.8 copy-done.6
  86.2 1.0 add.54
  87.2 1.0 add.55
  88.2 5.0 %collective-permute-start.20 = (bf16[1152,256]{1,0:T(8,128)(2,1)}, bf16[1152,256]{1,0:T(8,128)(2,1)}, u32[]{:S(2)}, u32[]{:S(2)}) collective-permute-start(bf16[1152,256]{1,0:T(8,128)(2,1)} %add.54), channel_id=1, source_target_pairs={{4,20},{5,21},{6,22},{7,23},{8,24},{9,25},{10,26},{11,27},{16,0},{... | collective-permute-start | bytes 1769480 | tf_op jit(solution)/shard_map/ppermute | solution.py:377
  93.2 1.5 %collective-permute-start.19 = (bf16[1152,256]{1,0:T(8,128)(2,1)}, bf16[1152,256]{1,0:T(8,128)(2,1)}, u32[]{:S(2)}, u32[]{:S(2)}) collective-permute-start(bf16[1152,256]{1,0:T(8,128)(2,1)} %add.55), channel_id=1, source_target_pairs={{0,16},{1,17},{2,18},{3,19},{12,28},{13,29},{14,30},{15,31},{20,4}... | collective-permute-start | bytes 1769480 | tf_op jit(solution)/shard_map/ppermute | solution.py:377
  94.7 1.0 add.56
  95.7 1.3 %collective-permute-start.21 = (bf16[1152,256]{1,0:T(8,128)(2,1)}, bf16[1152,256]{1,0:T(8,128)(2,1)}, u32[]{:S(2)}, u32[]{:S(2)}) collective-permute-start(bf16[1152,256]{1,0:T(8,128)(2,1)} %add.56), channel_id=1, source_target_pairs={{0,16},{1,17},{2,18},{3,19},{12,28},{13,29},{14,30},{15,31},{20,4}... | collective-permute-start | bytes 1769480 | tf_op jit(solution)/shard_map/ppermute | solution.py:377
  97.1 2.6 %edge.1 = f32[256,128]{1,0:T(8,128)S(1)} custom-call(s32[2]{0:T(128)S(1)} %pad_add_fusion.place_ref, bf16[1024,256]{1,0:T(8,128)(2,1)S(1)} %copy-done, bf16[1024,256]{1,0:T(8,128)(2,1)} %collective-permute-done.refs_1_, bf16[1024,256]{1,0:T(8,128)(2,1)} %collective-permute-done.5.refs_2_, bf16[1024,256]{1,0:T(8,128)(2,1)} %collective-permute-done.8.refs_3_, ...), custom_call_target="tpu_custom_call" | custom-call | flops 1 | bytes 1 | tf_op jit(solution)/shard_map/edge/pallas_call | solution.py:260
  99.7 4.1 %collective-permute-start.18 = (f32[256,128]{1,0:T(8,128)S(1)}, f32[256,128]{1,0:T(8,128)S(1)}, u32[]{:S(2)}, u32[]{:S(2)}) collective-permute-start(f32[256,128]{1,0:T(8,128)S(1)} %edge.1), channel_id=1, source_target_pairs={{8,0},{16,8},{24,16},{9,1},{17,9},{25,17},{10,2},{18,10},{26,18},{... | collective-permute-start | bytes 393224 | tf_op jit(solution)/shard_map/ppermute | solution.py:349
  103.8 0.7 broadcast_multiply_fusion
  104.5 3.0 %collective-permute-done.18 = f32[256,128]{1,0:T(8,128)S(1)} collective-permute-done((f32[256,128]{1,0:T(8,128)S(1)}, f32[256,128]{1,0:T(8,128)S(1)}, u32[]{:S(2)}, u32[]{:S(2)}) %collective-permute-start.18) | collective-permute-done | bytes 131104 | tf_op jit(solution)/shard_map/ppermute | solution.py:349
  107.5 15.3 %image_grad.1 = bf16[32,128,128]{2,1,0:T(8,128)(2,1)} custom-call(s32[2]{0:T(128)S(1)} %pad_add_fusion.place_ref, f32[256,128]{1,0:T(8,128)S(1)} %broadcast_select_fusion.4.halo_ref, bf16[1024,256]{1,0:T(8,128)(2,1)S(1)} %copy-done, bf16[1024,256]{1,0:T(8,128)(2,1)} %collective-permute-done.refs_1_, bf16[1024,256]{1,0:T(8,128)(2,1)} %collective-permute-done.5.refs_2_, ...), custom_call_target="tpu_custom_call" | custom-call | flops 1 | bytes 1 | tf_op jit(solution)/shard_map/image_grad/pallas_call | solution.py:201
  122.8 2.2 %fusion.1 = (f32[1152,256]{1,0:T(8,128)S(1)}, f32[1152,256]{1,0:T(8,128)S(1)}) fusion(pred[]{:T(512)S(6)} %eq.23, bf16[1152,256]{1,0:T(8,128)(2,1)S(1)} %copy-done.10, bf16[1152,256]{1,0:T(8,128)(2,1)} %add.55, pred[]{:T(512)S(6)} %eq.24, bf16[1152,256]{1,0:T(8,128)(2,1)S(1)} %copy-done.12, bf16[1152,256]{1,0:T(8,128)(2,1)} %collective-permute-done.19, ...), kind=kLoop, calls=%fused_computation.4 | loop fusion | flops 3538944 | bytes 7077890 | tf_op jit(solution)/shard_map/jit(_where)/select_n | solution.py:451
  125.0 1.7 %maximum_multiply_fusion = f32[3,3,128,512]{3,2,1,0:T(8,128)} fusion(f32[3,3,128,256]{3,2,1,0:T(8,128)S(1)} %bitcast.12, f32[3,3,128,256]{3,2,1,0:T(8,128)S(1)} %bitcast.11), kind=kLoop, calls=%fused_computation | loop fusion | flops 1179648 | bytes 4718592 | tf_op jit(solution)/shard_map/mul | solution.py:470
  (42 shorter events, 0.1 us)
Async XLA Ops:
  3.3 6.3 %collective-permute-start.3 = (f32[256,64]{1,0:T(8,128)}, f32[256,64]{1,0:T(8,128)S(1)}, u32[]{:S(2)}, u32[]{:S(2)}) collective-permute-start(f32[256,64]{1,0:T(8,128)} %get-tuple-element.39), channel_id=1, source_target_pairs={{0,16},{8,24},{16,0},{24,8},{1,17},{9,25},{17,1},{25,9},{2,18},{10... | collective-permute-start | bytes 196616 | tf_op jit(solution)/shard_map/ppermute | solution.py:355
  6.1 3.5 %collective-permute-start.2 = (bf16[128,128]{1,0:T(8,128)(2,1)S(1)}, bf16[128,128]{1,0:T(8,128)(2,1)S(1)}, u32[]{:S(2)}, u32[]{:S(2)}) collective-permute-start(bf16[128,128]{1,0:T(8,128)(2,1)S(1)} %slice_bitcast_fusion), channel_id=1, source_target_pairs={{0,8},{8,16},{16,24},{1,9},{9,17},{17,25},{2,10},{10,18},{18,26},{... | collective-permute-start | bytes 98312 | tf_op jit(solution)/shard_map/ppermute | solution.py:349
  9.5 31.6 %collective-permute-start.7 = (bf16[1152,512]{1,0:T(8,128)(2,1)}, bf16[1152,512]{1,0:T(8,128)(2,1)}, u32[]{:S(2)}, u32[]{:S(2)}) collective-permute-start(bf16[1152,512]{1,0:T(8,128)(2,1)} %bitcast.5.refs_8_), channel_id=1, source_target_pairs={{0,8},{8,0},{16,24},{24,16},{1,9},{9,1},{17,25},{25,17},{2,10},{10... | collective-permute-start | bytes 3538952 | tf_op jit(solution)/shard_map/ppermute | solution.py:355
  10.0 13.8 %collective-permute-start.1 = (bf16[1024,256]{1,0:T(8,128)(2,1)}, bf16[1024,256]{1,0:T(8,128)(2,1)S(1)}, u32[]{:S(2)}, u32[]{:S(2)}) collective-permute-start(bf16[1024,256]{1,0:T(8,128)(2,1)} %get-tuple-element.38.refs_0_), channel_id=1, source_target_pairs={{0,1},{1,0},{2,3},{3,2},{4,5},{5,4},{6,7},{7,6},{8,9},{9,8},{10,11... | collective-permute-start | bytes 1572872 | tf_op jit(solution)/shard_map/ppermute | solution.py:355
  11.5 15.1 %collective-permute-start = (bf16[1024,256]{1,0:T(8,128)(2,1)}, bf16[1024,256]{1,0:T(8,128)(2,1)}, u32[]{:S(2)}, u32[]{:S(2)}) collective-permute-start(bf16[1024,256]{1,0:T(8,128)(2,1)} %get-tuple-element.38.refs_0_), channel_id=1, source_target_pairs={{0,2},{1,3},{2,4},{3,5},{4,6},{5,7},{6,0},{7,1},{8,10},{9,11},{10,... | collective-permute-start | bytes 1572872 | tf_op jit(solution)/shard_map/ppermute | solution.py:381
  12.8 45.6 %collective-permute-start.13 = (bf16[1152,512]{1,0:T(8,128)(2,1)}, bf16[1152,512]{1,0:T(8,128)(2,1)}, u32[]{:S(2)}, u32[]{:S(2)}) collective-permute-start(bf16[1152,512]{1,0:T(8,128)(2,1)} %bitcast.5.refs_8_), channel_id=1, source_target_pairs={{0,16},{8,24},{16,0},{24,8},{1,17},{9,25},{17,1},{25,9},{2,18},{10... | collective-permute-start | bytes 3538952 | tf_op jit(solution)/shard_map/ppermute | solution.py:355
  16.0 3.2 %collective-permute-start.4 = (f32[256,64]{1,0:T(8,128)S(1)}, f32[256,64]{1,0:T(8,128)S(1)}, u32[]{:S(2)}, u32[]{:S(2)}) collective-permute-start(f32[256,64]{1,0:T(8,128)S(1)} %add.51), channel_id=1, source_target_pairs={{0,8},{8,0},{16,24},{24,16},{1,9},{9,1},{17,25},{25,17},{2,10},{10... | collective-permute-start | bytes 196616 | tf_op jit(solution)/shard_map/ppermute | solution.py:355
  16.9 1.2 copy-start.8
  18.1 23.9 %copy-start = (bf16[1024,256]{1,0:T(8,128)(2,1)S(1)}, bf16[1024,256]{1,0:T(8,128)(2,1)}, u32[]{:S(2)}) copy-start(bf16[1024,256]{1,0:T(8,128)(2,1)} %get-tuple-element.38.refs_0_) | copy-start | bytes 1572868
  26.6 12.3 %collective-permute-start.6 = (bf16[1024,256]{1,0:T(8,128)(2,1)}, bf16[1024,256]{1,0:T(8,128)(2,1)S(1)}, u32[]{:S(2)}, u32[]{:S(2)}) collective-permute-start(bf16[1024,256]{1,0:T(8,128)(2,1)} %collective-permute-done.refs_1_), channel_id=1, source_target_pairs={{0,1},{1,0},{2,3},{3,2},{4,5},{5,4},{6,7},{7,6},{8,9},{9,8},{10,11... | collective-permute-start | bytes 1572872 | tf_op jit(solution)/shard_map/ppermute | solution.py:355
  27.0 14.1 %collective-permute-start.5 = (bf16[1024,256]{1,0:T(8,128)(2,1)}, bf16[1024,256]{1,0:T(8,128)(2,1)}, u32[]{:S(2)}, u32[]{:S(2)}) collective-permute-start(bf16[1024,256]{1,0:T(8,128)(2,1)} %collective-permute-done.refs_1_), channel_id=1, source_target_pairs={{0,2},{1,3},{2,4},{3,5},{4,6},{5,7},{6,0},{7,1},{8,10},{9,11},{10,... | collective-permute-start | bytes 1572872 | tf_op jit(solution)/shard_map/ppermute | solution.py:381
  38.9 0.8 copy-start.1
  41.1 11.3 %collective-permute-start.9 = (bf16[1024,256]{1,0:T(8,128)(2,1)}, bf16[1024,256]{1,0:T(8,128)(2,1)}, u32[]{:S(2)}, u32[]{:S(2)}) collective-permute-start(bf16[1024,256]{1,0:T(8,128)(2,1)} %collective-permute-done.5.refs_2_), channel_id=1, source_target_pairs={{0,1},{1,0},{2,3},{3,2},{4,5},{5,4},{6,7},{7,6},{8,9},{9,8},{10,11... | collective-permute-start | bytes 1572872 | tf_op jit(solution)/shard_map/ppermute | solution.py:355
  41.9 12.6 %collective-permute-start.8 = (bf16[1024,256]{1,0:T(8,128)(2,1)}, bf16[1024,256]{1,0:T(8,128)(2,1)}, u32[]{:S(2)}, u32[]{:S(2)}) collective-permute-start(bf16[1024,256]{1,0:T(8,128)(2,1)} %collective-permute-done.5.refs_2_), channel_id=1, source_target_pairs={{0,2},{1,3},{2,4},{3,5},{4,6},{5,7},{6,0},{7,1},{8,10},{9,11},{10,... | collective-permute-start | bytes 1572872 | tf_op jit(solution)/shard_map/ppermute | solution.py:381
  47.7 19.0 %copy-start.2 = (bf16[1024,256]{1,0:T(8,128)(2,1)S(1)}, bf16[1024,256]{1,0:T(8,128)(2,1)}, u32[]{:S(2)}) copy-start(bf16[1024,256]{1,0:T(8,128)(2,1)} %copy-done.1) | copy-start | bytes 1572868
  54.5 6.2 %collective-permute-start.11 = (bf16[1152,256]{1,0:T(8,128)(2,1)S(1)}, bf16[1152,256]{1,0:T(8,128)(2,1)S(1)}, u32[]{:S(2)}, u32[]{:S(2)}) collective-permute-start(bf16[1152,256]{1,0:T(8,128)(2,1)S(1)} %get-tuple-element.53), channel_id=1, source_target_pairs={{0,8},{8,0},{16,24},{24,16},{1,9},{9,1},{17,25},{25,17},{2,10},{10... | collective-permute-start | bytes 1769480 | tf_op jit(solution)/shard_map/ppermute | solution.py:355
  58.4 19.0 %collective-permute-start.14 = (bf16[1152,512]{1,0:T(8,128)(2,1)}, bf16[1152,512]{1,0:T(8,128)(2,1)S(1)}, u32[]{:S(2)}, u32[]{:S(2)}) collective-permute-start(bf16[1152,512]{1,0:T(8,128)(2,1)} %collective-permute-done.13.refs_10_), channel_id=1, source_target_pairs={{0,8},{8,0},{16,24},{24,16},{1,9},{9,1},{17,25},{25,17},{2,10},{10... | collective-permute-start | bytes 3538952 | tf_op jit(solution)/shard_map/ppermute | solution.py:355
  60.9 16.4 %copy-start.9 = (bf16[1152,256]{1,0:T(8,128)(2,1)}, bf16[1152,256]{1,0:T(8,128)(2,1)S(1)}, u32[]{:S(2)}) copy-start(bf16[1152,256]{1,0:T(8,128)(2,1)S(1)} %add.53) | copy-start | bytes 1769476
  60.9 17.5 %collective-permute-start.12 = (bf16[1152,256]{1,0:T(8,128)(2,1)S(1)}, bf16[1152,256]{1,0:T(8,128)(2,1)S(1)}, u32[]{:S(2)}, u32[]{:S(2)}) collective-permute-start(bf16[1152,256]{1,0:T(8,128)(2,1)S(1)} %add.53), channel_id=1, source_target_pairs={{4,20},{5,21},{6,22},{7,23},{8,24},{9,25},{10,26},{11,27},{16,0},{... | collective-permute-start | bytes 1769480 | tf_op jit(solution)/shard_map/ppermute | solution.py:377
  66.0 11.4 %collective-permute-start.10 = (bf16[1024,256]{1,0:T(8,128)(2,1)}, bf16[1024,256]{1,0:T(8,128)(2,1)S(1)}, u32[]{:S(2)}, u32[]{:S(2)}) collective-permute-start(bf16[1024,256]{1,0:T(8,128)(2,1)} %collective-permute-done.8.refs_3_), channel_id=1, source_target_pairs={{0,1},{1,0},{2,3},{3,2},{4,5},{5,4},{6,7},{7,6},{8,9},{9,8},{10,11... | collective-permute-start | bytes 1572872 | tf_op jit(solution)/shard_map/ppermute | solution.py:355
  77.4 1.0 copy-start.4
  78.4 7.0 %copy-start.11 = (bf16[1152,256]{1,0:T(8,128)(2,1)}, bf16[1152,256]{1,0:T(8,128)(2,1)S(1)}, u32[]{:S(2)}) copy-start(bf16[1152,256]{1,0:T(8,128)(2,1)S(1)} %collective-permute-done.12) | copy-start | bytes 1769476
  78.4 7.8 %collective-permute-start.15 = (bf16[1152,256]{1,0:T(8,128)(2,1)S(1)}, bf16[1152,256]{1,0:T(8,128)(2,1)S(1)}, u32[]{:S(2)}, u32[]{:S(2)}) collective-permute-start(bf16[1152,256]{1,0:T(8,128)(2,1)S(1)} %get-tuple-element.62), channel_id=1, source_target_pairs={{0,8},{8,0},{16,24},{24,16},{1,9},{9,1},{17,25},{25,17},{2,10},{10... | collective-permute-start | bytes 1769480 | tf_op jit(solution)/shard_map/ppermute | solution.py:355
  78.4 8.8 %collective-permute-start.16 = (bf16[1152,256]{1,0:T(8,128)(2,1)S(1)}, bf16[1152,256]{1,0:T(8,128)(2,1)S(1)}, u32[]{:S(2)}, u32[]{:S(2)}) collective-permute-start(bf16[1152,256]{1,0:T(8,128)(2,1)S(1)} %get-tuple-element.64), channel_id=1, source_target_pairs={{0,8},{8,0},{16,24},{24,16},{1,9},{9,1},{17,25},{25,17},{2,10},{10... | collective-permute-start | bytes 1769480 | tf_op jit(solution)/shard_map/ppermute | solution.py:355
  85.4 0.8 copy-start.6
  87.2 9.8 %copy-start.7 = (bf16[1024,256]{1,0:T(8,128)(2,1)S(1)}, bf16[1024,256]{1,0:T(8,128)(2,1)}, u32[]{:S(2)}) copy-start(bf16[1024,256]{1,0:T(8,128)(2,1)} %copy-done.6) | copy-start | bytes 1572868
  88.2 8.9 %copy-start.3 = (bf16[1024,256]{1,0:T(8,128)(2,1)S(1)}, bf16[1024,256]{1,0:T(8,128)(2,1)}, u32[]{:S(2)}) copy-start(bf16[1024,256]{1,0:T(8,128)(2,1)} %copy-done.1) | copy-start | bytes 1572868
  88.2 8.9 %copy-start.5 = (bf16[1152,512]{1,0:T(8,128)(2,1)S(1)}, bf16[1152,512]{1,0:T(8,128)(2,1)}, u32[]{:S(2)}) copy-start(bf16[1152,512]{1,0:T(8,128)(2,1)} %copy-done.4) | copy-start | bytes 3538948
  88.2 6.4 %collective-permute-start.17 = (bf16[1152,256]{1,0:T(8,128)(2,1)S(1)}, bf16[1152,256]{1,0:T(8,128)(2,1)S(1)}, u32[]{:S(2)}, u32[]{:S(2)}) collective-permute-start(bf16[1152,256]{1,0:T(8,128)(2,1)S(1)} %get-tuple-element.66), channel_id=1, source_target_pairs={{0,8},{8,0},{16,24},{24,16},{1,9},{9,1},{17,25},{25,17},{2,10},{10... | collective-permute-start | bytes 1769480 | tf_op jit(solution)/shard_map/ppermute | solution.py:355
  88.2 34.5 %collective-permute-start.20 = (bf16[1152,256]{1,0:T(8,128)(2,1)}, bf16[1152,256]{1,0:T(8,128)(2,1)}, u32[]{:S(2)}, u32[]{:S(2)}) collective-permute-start(bf16[1152,256]{1,0:T(8,128)(2,1)} %add.54), channel_id=1, source_target_pairs={{4,20},{5,21},{6,22},{7,23},{8,24},{9,25},{10,26},{11,27},{16,0},{... | collective-permute-start | bytes 1769480 | tf_op jit(solution)/shard_map/ppermute | solution.py:377
  93.2 29.6 %collective-permute-start.19 = (bf16[1152,256]{1,0:T(8,128)(2,1)}, bf16[1152,256]{1,0:T(8,128)(2,1)}, u32[]{:S(2)}, u32[]{:S(2)}) collective-permute-start(bf16[1152,256]{1,0:T(8,128)(2,1)} %add.55), channel_id=1, source_target_pairs={{0,16},{1,17},{2,18},{3,19},{12,28},{13,29},{14,30},{15,31},{20,4}... | collective-permute-start | bytes 1769480 | tf_op jit(solution)/shard_map/ppermute | solution.py:377
  95.7 27.1 %collective-permute-start.21 = (bf16[1152,256]{1,0:T(8,128)(2,1)}, bf16[1152,256]{1,0:T(8,128)(2,1)}, u32[]{:S(2)}, u32[]{:S(2)}) collective-permute-start(bf16[1152,256]{1,0:T(8,128)(2,1)} %add.56), channel_id=1, source_target_pairs={{0,16},{1,17},{2,18},{3,19},{12,28},{13,29},{14,30},{15,31},{20,4}... | collective-permute-start | bytes 1769480 | tf_op jit(solution)/shard_map/ppermute | solution.py:377
  99.7 7.8 %collective-permute-start.18 = (f32[256,128]{1,0:T(8,128)S(1)}, f32[256,128]{1,0:T(8,128)S(1)}, u32[]{:S(2)}, u32[]{:S(2)}) collective-permute-start(f32[256,128]{1,0:T(8,128)S(1)} %edge.1), channel_id=1, source_target_pairs={{8,0},{16,8},{24,16},{9,1},{17,9},{25,17},{10,2},{18,10},{26,18},{... | collective-permute-start | bytes 393224 | tf_op jit(solution)/shard_map/ppermute | solution.py:349
  107.5 15.3 %copy-start.10 = (bf16[1152,256]{1,0:T(8,128)(2,1)S(1)}, bf16[1152,256]{1,0:T(8,128)(2,1)}, u32[]{:S(2)}) copy-start(bf16[1152,256]{1,0:T(8,128)(2,1)} %copy-done.9) | copy-start | bytes 1769476
  107.5 15.3 %copy-start.12 = (bf16[1152,256]{1,0:T(8,128)(2,1)S(1)}, bf16[1152,256]{1,0:T(8,128)(2,1)}, u32[]{:S(2)}) copy-start(bf16[1152,256]{1,0:T(8,128)(2,1)} %copy-done.11) | copy-start | bytes 1769476

commit v3 on v2

v3 whole, which is shorter than its diff:
```python
import functools

import jax
import jax.numpy as jnp
from jax import lax
from jax.experimental import pallas as pl
from jax.experimental.pallas import tpu as pltpu
from jax.sharding import PartitionSpec as P

TILES = 4
CUTS = 3
GROUP_WIDTH = 64
BF = jnp.bfloat16
F32 = jnp.float32
SMALL = pl.CostEstimate(flops=1, bytes_accessed=1, transcendentals=0)


def params(mebibytes):
    return pltpu.CompilerParams(vmem_limit_bytes=mebibytes * 2**20)


def dot_nn(a, b):
    return lax.dot_general(a, b, (((1,), (0,)), ((), ())), preferred_element_type=F32)


def dot_nt(a, b):
    return lax.dot_general(a, b, (((1,), (1,)), ((), ())), preferred_element_type=F32)


def dot_tn(a, b):
    return lax.dot_general(a, b, (((0,), (0,)), ((), ())), preferred_element_type=F32)


def iota(shape, dim):
    return lax.broadcasted_iota(jnp.int32, shape, dim)


def pre_kernel(grad_ref, pre_ref, mix_ref, out_ref, mix_out_ref):
    chans = grad_ref.shape[1]
    spread = (iota((GROUP_WIDTH, chans), 0) == iota((GROUP_WIDTH, chans), 1) % GROUP_WIDTH).astype(BF)
    same = iota((chans, chans), 0) // GROUP_WIDTH == iota((chans, chans), 1) // GROUP_WIDTH
    blocks = jnp.where(same, dot_nn(mix_ref[...], spread), 0.0).astype(BF)
    grad = grad_ref[...]
    pre = pre_ref[...].astype(F32)
    sig = jax.nn.sigmoid(pre)
    act = (pre * sig).astype(BF)
    grad_act = dot_nt(grad, blocks)
    out_ref[...] = (grad_act * (sig * (1.0 + pre * (1.0 - sig)))).astype(BF)
    full = jnp.where(same, dot_tn(act, grad), 0.0)
    total = full
    for step in range(1, chans // GROUP_WIDTH):
        total = total + pltpu.roll(full, step * GROUP_WIDTH, 1)
    mix_out_ref[...] = total[:, :GROUP_WIDTH]


def pre_gradient(grad_out, pre_act, mix_weight):
    pixels, chans = grad_out.shape
    return pl.pallas_call(
        pre_kernel,
        out_shape=(
            jax.ShapeDtypeStruct((pixels, chans), BF),
            jax.ShapeDtypeStruct((chans, GROUP_WIDTH), F32),
        ),
        compiler_params=params(60),
        cost_estimate=SMALL,
        name="pre_grad",
    )(grad_out, pre_act, mix_weight)


def taps_kernel(image_ref, prev_ref, out_ref):
    rows, chans, width = image_ref.shape
    half = width // 2
    col_in = iota((2 * width, 6 * half), 0)
    col_out = iota((2 * width, 6 * half), 1)
    pick = (
        (col_in // width == (col_out % width) // half)
        & (col_in % width == 2 * (col_out % half) + col_out // width - 1)
    ).astype(BF)
    for pair in range(rows // 4):
        for row_tap in range(3):
            first = 4 * pair + row_tap - 1
            upper = prev_ref[...] if first < 0 else image_ref[first]
            both = jnp.concatenate([upper, image_ref[first + 2]], axis=1)
            picked = dot_nn(both, pick).astype(BF)
            for col_tap in range(3):
                tap = 3 * row_tap + col_tap
                out_ref[tap * chans : (tap + 1) * chans, pair * width : (pair + 1) * width] = picked[
                    :, col_tap * width : (col_tap + 1) * width
                ]


def image_taps(image_in, prev_row):
    rows, chans, width = image_in.shape
    pixels = rows * width // 4
    return pl.pallas_call(
        taps_kernel,
        out_shape=jax.ShapeDtypeStruct((9 * chans, pixels), BF),
        compiler_params=params(60),
        cost_estimate=SMALL,
        name="taps",
    )(image_in, prev_row)


def grad_place(place_ref, flips, index):
    if not flips:
        return index
    return ((place_ref[1] + 8 - 2 * (index % 4)) & 7) ^ (index // 4)


def part_place(place_ref, flips, index):
    return place_ref[0] ^ index if flips else index


def interleave(width):
    place_in = iota((4 * width, 4 * width), 0)
    place_out = iota((4 * width, 4 * width), 1)
    return (
        ((place_in % (2 * width)) // width == place_out // (2 * width))
        & (2 * (place_in % width) + place_in // (2 * width) == place_out % (2 * width))
    ).astype(BF)


def image_kernel(
    grad_count, part_count, flips, width, place_ref, *refs
):
    grads, parts = refs[:grad_count], refs[grad_count : grad_count + part_count]
    out_ref, last_ref, edge_ref, grad_all, part_all, values, grad_sem, part_sem = refs[grad_count + part_count :]
    pixels, span = grads[0].shape
    outs, part_span = parts[0].shape
    chans = outs // 9
    pairs = pixels // (2 * width)
    tile = pixels

    def part_copy(index):
        start = pl.multiple_of(part_place(place_ref, flips, index) * part_span, part_span)
        return pltpu.make_async_copy(parts[index], part_all.at[:, pl.ds(start, part_span)], part_sem.at[index])

    def grad_copy(index):
        rows = grads[index].shape[0]
        start = pl.multiple_of(grad_place(place_ref, flips, min(index, grad_count - 2) if flips else index) * span, span)
        first = rows if flips and index == grad_count - 1 else 0
        return pltpu.make_async_copy(
            grads[index], grad_all.at[pl.ds(first, rows), pl.ds(start, span)], grad_sem.at[index]
        )

    for index in range(part_count):
        part_copy(index).start()
    for index in range(grad_count):
        grad_copy(index).start()

    lane = iota((chans, tile), 1)
    last_col = lane % width == width - 1
    row_end = lane >= tile - width
    place = interleave(width)

    def left(value):
        return jnp.where(last_col, 0.0, pltpu.roll(value, tile - 1, 1))

    def up_terms(terms):
        even, odd = terms[chans : 2 * chans], terms[2 * chans : 3 * chans] + left(terms[:chans])
        return pltpu.roll(even, tile - width, 1), pltpu.roll(odd, tile - width, 1)

    def tap_row(tap):
        return dot_nt(part_all[3 * tap * chans : 3 * (tap + 1) * chans], grad_all[...])

    third = lambda terms, index: terms[index * chans : (index + 1) * chans]
    for index in range(part_count):
        part_copy(index).wait()
    for index in range(grad_count):
        grad_copy(index).wait()
    upper = tap_row(0)
    own = up_terms(upper)
    middle = tap_row(1)
    lower = tap_row(2)
    phases = (
        (third(middle, 1), third(middle, 2) + left(third(middle, 0))),
        (
            third(lower, 1) + jnp.where(row_end, 0.0, own[0]),
            third(lower, 2) + left(third(lower, 0)) + jnp.where(row_end, 0.0, own[1]),
        ),
    )
    for index in range(2):
        at = slice(index * chans, (index + 1) * chans)
        edge_ref[at] = own[index][:, tile - 2 * width :]
        last_ref[at] = phases[1][index][:, tile - 2 * width :]
    for parity in range(2):
        even, odd = (value.astype(BF) for value in phases[parity])
        for pair in range(pairs):
            cols = slice(pair * 2 * width, (pair + 1) * 2 * width)
            at = slice((pairs * parity + pair) * chans, (pairs * parity + pair + 1) * chans)
            values[at, : 2 * width] = even[:, cols]
            values[at, 2 * width :] = odd[:, cols]
    placed = dot_nn(values[...], place).astype(BF)
    for parity in range(2):
        for pair in range(pairs):
            at = slice((pairs * parity + pair) * chans, (pairs * parity + pair + 1) * chans)
            first = 4 * pair + parity
            out_ref[first] = placed[at, : 2 * width]
            out_ref[first + 2] = placed[at, 2 * width :]


def image_gradient(place, flips, grads, parts, width):
    pixels, span = grads[0].shape
    outs, part_span = parts[0].shape
    full = part_span * len(parts)
    if flips:
        grads = [*grads[:-1], *grads[-1]]
    chans = outs // 9
    kernel = functools.partial(image_kernel, len(grads), len(parts), flips, width)
    anywhere = pl.BlockSpec(memory_space=pl.ANY)
    return pl.pallas_call(
        kernel,
        out_shape=(
            jax.ShapeDtypeStruct((2 * pixels // width, chans, 2 * width), BF),
            jax.ShapeDtypeStruct((2 * chans, 2 * width), F32),
            jax.ShapeDtypeStruct((2 * chans, 2 * width), F32),
        ),
        in_specs=[pl.BlockSpec(memory_space=pltpu.SMEM)] + [anywhere] * (len(grads) + len(parts)),
        out_specs=(pl.BlockSpec(memory_space=pltpu.VMEM),) * 3,
        scratch_shapes=[
            pltpu.VMEM((pixels, full), BF),
            pltpu.VMEM((outs, full), BF),
            pltpu.VMEM((pixels // width * chans, 4 * width), BF),
            pltpu.SemaphoreType.DMA((len(grads),)),
            pltpu.SemaphoreType.DMA((len(parts),)),
        ],
        compiler_params=params(60),
        cost_estimate=SMALL,
        name="image_grad",
    )(place, *grads, *parts)


def last_row(image_ref, last_ref, edge_ref, out_ref, row, sem, place_ref):
    doubled, width = last_ref.shape
    chans, half = doubled // 2, width // 2
    inside = place_ref[0] % TILES != TILES - 1
    total = last_ref[...] + jnp.where((iota((doubled, width), 1) >= half) & inside, edge_ref[...], 0.0)
    both = jnp.concatenate([total[:chans], total[chans:]], axis=1).astype(BF)
    row[...] = dot_nn(both, interleave(half))[:, width:].astype(BF)
    copy = pltpu.make_async_copy(row, out_ref.at[out_ref.shape[0] - 1], sem)
    copy.start()
    return copy


def finish_kernel(place_ref, image_ref, last_ref, edge_ref, out_ref, row, sem):
    last_row(image_ref, last_ref, edge_ref, out_ref, row, sem, place_ref).wait()


def finish_both_kernel(scale, place_ref, image_ref, last_ref, edge_ref, *refs):
    totals, others, (out_ref, conv_ref) = refs[:4], refs[4:7], refs[7:9]
    row, sem, held, sums, in_sems, out_sems = refs[9:]
    outs, span = totals[0].shape
    rows = outs // CUTS
    core, outer, side = place_ref[0] & 1, place_ref[1] >> 1, place_ref[1] & 1
    step = (core + (outer & 1)) & 3
    mine = (((outer - step) & 3) >> 1) == (place_ref[0] >> 1)
    pairs = ((totals[0], others[0], totals[1], others[1]), (totals[2], others[1], totals[3], others[2]))

    def load(ref, half, which, cut):
        return pltpu.make_async_copy(
            ref.at[pl.ds(cut * rows, rows)], held.at[half, which, cut], in_sems.at[half, which, cut]
        )

    def store(half, cut):
        start = pl.multiple_of((side if half == 0 else 1 - side) * span, span)
        return pltpu.make_async_copy(
            sums.at[half, cut], conv_ref.at[pl.ds(cut * rows, rows), pl.ds(start, span)], out_sems.at[half, cut]
        )

    for cut in range(CUTS):
        for half in range(2):
            for which in range(2):

                @pl.when(mine)
                def _():
                    load(pairs[half][which], half, which, cut).start()

                @pl.when(jnp.logical_not(mine))
                def _():
                    load(pairs[half][2 + which], half, which, cut).start()

    row_copy = last_row(image_ref, last_ref, edge_ref, out_ref, row, sem, place_ref)
    for cut in range(CUTS):
        for half in range(2):
            for which in range(2):
                load(totals[0], half, which, cut).wait()
            sums[half, cut] = (held[half, 0, cut].astype(F32) + held[half, 1, cut].astype(F32)) * scale
            store(half, cut).start()
    for cut in range(CUTS):
        for half in range(2):
            store(half, cut).wait()
    row_copy.wait()


def finish_image(place, image, last, edge):
    anywhere, here = pl.BlockSpec(memory_space=pl.ANY), pl.BlockSpec(memory_space=pltpu.VMEM)
    return pl.pallas_call(
        finish_kernel,
        out_shape=jax.ShapeDtypeStruct(image.shape, BF),
        in_specs=[pl.BlockSpec(memory_space=pltpu.SMEM), anywhere, here, here],
        out_specs=anywhere,
        scratch_shapes=[pltpu.VMEM(image.shape[1:], BF), pltpu.SemaphoreType.DMA(())],
        input_output_aliases={1: 0},
        compiler_params=params(60),
        cost_estimate=SMALL,
        name="finish",
    )(place, image, last, edge)


def finish_both(place, image, last, edge, totals, others, scale):
    anywhere, here = pl.BlockSpec(memory_space=pl.ANY), pl.BlockSpec(memory_space=pltpu.VMEM)
    outs, span = totals[0].shape
    rows = outs // CUTS
    return pl.pallas_call(
        functools.partial(finish_both_kernel, scale),
        out_shape=(jax.ShapeDtypeStruct(image.shape, BF), jax.ShapeDtypeStruct((outs, 2 * span), F32)),
        in_specs=[pl.BlockSpec(memory_space=pltpu.SMEM), anywhere, here, here] + [anywhere] * 7,
        out_specs=(anywhere, anywhere),
        scratch_shapes=[
            pltpu.VMEM(image.shape[1:], BF),
            pltpu.SemaphoreType.DMA(()),
            pltpu.VMEM((2, 2, CUTS, rows, span), BF),
            pltpu.VMEM((2, CUTS, rows, span), F32),
            pltpu.SemaphoreType.DMA((2, 2, CUTS)),
            pltpu.SemaphoreType.DMA((2, CUTS)),
        ],
        input_output_aliases={1: 0},
        compiler_params=params(60),
        cost_estimate=SMALL,
        name="finish",
    )(place, image, last, edge, *totals, *others)


def partial_kernel(count, split, chosen_blocks, place_ref, taps_ref, *refs):
    picks = len(chosen_blocks)
    core, turn = place_ref[0] & 1, (place_ref[1] >> 1) & 1
    whole = count - 1 if split else count
    inputs = whole + (2 if split else 0)
    blocks, outs = refs[:inputs], refs[inputs : inputs + picks]
    taps, grads, sums, grad_sems, taps_sems, out_sems = refs[inputs + picks :]
    half = taps_ref.shape[1] // 2
    rows = taps.shape[1]
    part = lambda ref, cut: ref.at[pl.ds(cut * rows, rows)]

    def chosen(pick, index):
        return pltpu.make_async_copy(blocks[index], grads.at[pick], grad_sems.at[pick])

    def out_copy(pick, cut):
        return pltpu.make_async_copy(sums.at[pick, cut], part(outs[pick], cut), out_sems.at[pick, cut])

    taps_in = [pltpu.make_async_copy(part(taps_ref, cut), taps.at[cut], taps_sems.at[cut]) for cut in range(CUTS)]

    def start(pick):
        kept, phase, base = chosen_blocks[pick]
        step = base + ((2 * phase + (core if kept else 1 - core) + turn) & 3)
        for index in range(count):

            @pl.when(step == index)
            def _():
                if index < whole:
                    chosen(pick, index).start()
                else:
                    for piece in range(2):
                        pltpu.make_async_copy(
                            blocks[whole + piece],
                            grads.at[pick, pl.ds(piece * half, half)],
                            grad_sems.at[pick],
                        ).start()

    start(0)
    for copy in taps_in:
        copy.start()
    for pick in range(1, picks):
        start(pick)
    for pick in range(picks):
        chosen(pick, 0).wait()
        for cut in range(CUTS):
            if pick == 0:
                taps_in[cut].wait()
            sums[pick, cut] = dot_nn(taps[cut], grads[pick]).astype(BF)
            out_copy(pick, cut).start()
    for pick in range(picks):
        for cut in range(CUTS):
            out_copy(pick, cut).wait()


def kernel_partials(place, taps, blocks, chosen):
    outs, pixels = taps.shape
    span = blocks[0].shape[1]
    count, split = len(blocks), isinstance(blocks[-1], tuple)
    if split:
        blocks = [*blocks[:-1], *blocks[-1]]
    rows = outs // CUTS
    picks = len(chosen)
    anywhere = pl.BlockSpec(memory_space=pl.ANY)
    return pl.pallas_call(
        functools.partial(partial_kernel, count, split, tuple(chosen)),
        out_shape=(jax.ShapeDtypeStruct((outs, span), BF),) * picks,
        in_specs=[pl.BlockSpec(memory_space=pltpu.SMEM)] + [anywhere] * (1 + len(blocks)),
        out_specs=(anywhere,) * picks,
        scratch_shapes=[
            pltpu.VMEM((CUTS, rows, pixels), BF),
            pltpu.VMEM((picks, pixels, span), BF),
            pltpu.VMEM((picks, CUTS, rows, span), BF),
            pltpu.SemaphoreType.DMA((picks,)),
            pltpu.SemaphoreType.DMA((CUTS,)),
            pltpu.SemaphoreType.DMA((picks, CUTS)),
        ],
        compiler_params=params(60),
        cost_estimate=SMALL,
        name="partials",
    )(place, taps, *blocks)


def step_along(value, axis, steps):
    count = lax.axis_size(axis)
    return lax.ppermute(
        value, axis, [(source, source + steps) for source in range(count) if 0 <= source + steps < count]
    )


def swap(value, axis, bits):
    return lax.ppermute(value, axis, [(source, source ^ bits) for source in range(lax.axis_size(axis))])


def kernel_sum_plain(taps, grads):
    partial = jnp.concatenate([dot_nn(taps, grad).astype(BF) for grad in grads], axis=1)
    return lax.psum_scatter(partial, "pix", scatter_dimension=1, tiled=True).astype(F32)


def kept_step(core, outer, phase):
    return (2 * phase + core + outer % 2) % 4


def kept_here(pix, outer, phase):
    return (outer - kept_step(pix % 2, outer, phase)) % 4 // 2 == pix // 2


def send_over(value, phase):
    pairs = []
    for pix in range(4):
        for ch in range(8):
            if not kept_here(pix, ch // 2, phase):
                pairs.append((pix * 8 + ch, (pix ^ 2) * 8 + ch))
    return lax.ppermute(value, ("pix", "ch"), pairs)


def ring(value):
    return lax.ppermute(value, "ch", [(source, (source + 2) % 8) for source in range(8)])


def shards(image_in, pre_act, grad_out, conv_weight, mix_weight):
    tile_rows, width, chans = grad_out.shape
    in_chans = image_in.shape[1]
    pix_count, ch_count = lax.axis_size("pix"), lax.axis_size("ch")
    pix, ch = lax.axis_index("pix"), lax.axis_index("ch")
    first_tile = pix % TILES == 0
    last_tile = pix % TILES == TILES - 1
    pixels = tile_rows * width
    scale = 1.0 / float(pix_count * pixels) ** 0.5

    tie = lax.optimization_barrier
    place = jnp.stack([pix, ch]).astype(jnp.int32)
    prev_row = step_along(image_in[-1], "pix", 1)
    grad_pre, mix_part = pre_gradient(
        grad_out.reshape(pixels, chans),
        pre_act.reshape(pixels, chans),
        mix_weight.reshape(chans, GROUP_WIDTH),
    )
    kernel_own = conv_weight.reshape(9 * in_chans, -1)
    rings = pix_count == 4 and ch_count == 8
    taps = image_taps(image_in, jnp.where(first_tile, jnp.zeros_like(prev_row), prev_row))

    if rings:
        near, far = [grad_pre], [swap(grad_pre, "ch", 1)]
        near.append(ring(near[0]))
        mix_sum = mix_part + swap(mix_part, "pix", 2)
        grad_mix = (mix_sum + swap(mix_sum, "pix", 1)) * scale
        totals = [[None] * 2, [None] * 2]

        def add_up(sums, phase, half):
            totals[phase][half] = sums[1] + swap(sums[0], "pix", 1)

        near[1], far[0], taps, grad_mix, kernel_own = tie((near[1], far[0], taps, grad_mix, kernel_own))
        far.append(swap(near[1], "ch", 1))
        near.append(ring(near[1]))
        kernel_x = swap(kernel_own, "pix", 2)
        kernel_core = swap(kernel_own, "pix", 1)
        near[2], far[1], kernel_core = tie((near[2], far[1], kernel_core))
        far.append(swap(near[2], "ch", 1))
        near.append(ring(near[2]))
        first = kernel_partials(place, taps, near[:3], [(0, 0, 0), (1, 0, 0)])
        near[3], far[2], first, kernel_x = tie((near[3], far[2], first, kernel_x))
        half = pixels // 2
        far.append((swap(near[3][:half], "ch", 1), ring(far[2][half:])))
        add_up(first, 0, 0)
        kernel_xcore = swap(kernel_x, "pix", 1)
        second = kernel_partials(
            place, taps, near + far[:3], [(0, 0, 4), (0, 1, 0), (1, 0, 4), (1, 1, 0)]
        )
        far[3], totals[0][0], second, kernel_xcore = tie((far[3], totals[0][0], second, kernel_xcore))
        mine = kept_here(pix, ch // 2, 0)
        arrived_first = send_over(totals[0][0], 0)
        add_up(second[::2], 0, 1)
        add_up(second[1::2], 1, 0)
        crossing = jnp.where(mine, totals[1][0], totals[0][1])
        crossing, taps = tie((crossing, taps))
        arrived_both = swap(crossing, "pix", 2)
        third = kernel_partials(place, taps, far, [(0, 1, 0), (1, 1, 0)])
        third, arrived_first = tie((third, arrived_first))
        add_up(third, 1, 1)
        arrived_last = send_over(totals[1][1], 1)
        grads = near + far
        parts = [kernel_own, kernel_core, kernel_x, kernel_xcore]
        image_at = (place, totals[1][1])
    else:
        grad_mix = lax.psum(mix_part, "pix") * scale
        grad_all = lax.all_gather(grad_pre, "ch", axis=0)
        kernel_all = lax.all_gather(kernel_own, "pix", axis=0)
        grads = [grad_all[index] for index in range(ch_count)]
        parts = [kernel_all[index] for index in range(pix_count)]
        grad_conv = kernel_sum_plain(taps, grads)
        image_at = (place,)
    grad_in, last, edge = image_gradient(tie(image_at)[0], rings, grads, parts, width)
    edge = step_along(edge, "pix", -1)
    if rings:
        grad_in, grad_conv = finish_both(
            place,
            grad_in,
            last,
            edge,
            [totals[0][0], totals[1][0], totals[0][1], totals[1][1]],
            [arrived_first, arrived_both, arrived_last],
            scale,
        )
    else:
        grad_in = finish_image(place, grad_in, last, edge)
        grad_conv = grad_conv * scale
    return (grad_in, grad_conv.reshape(conv_weight.shape), grad_mix.reshape(mix_weight.shape))


def solution(mesh):
    in_specs = (
        P("pix", "ch", None),
        P("pix", None, "ch"),
        P("pix", None, "ch"),
        P(None, None, "ch", "pix"),
        P("ch", None, None),
    )
    out_specs = (P("pix", "ch", None), P(None, None, "ch", "pix"), P("ch", None, None))
    return jax.shard_map(shards, mesh=mesh, in_specs=in_specs, out_specs=out_specs, check_vma=False)
```

time: 129 us -> 109 us (0.84); the launches traced: 127 us -> 108 us
  starting transfers between devices: 34.1 us -> 26.1 us
  Pallas kernels: 44.3 us -> 39.4 us
  waiting for transfers between devices: 33.9 us -> 29.7 us
    ppermute x4 -> x2, starting transfers between devices: 12.8 us -> 3.66 us  [send_over(): return lax.ppermute(value, ('pix', 'ch'), pairs)]
    pallas_call x5, Pallas kernels: 40.7 us -> 33.1 us  [the longest x3 18.8 us: kernel_partials(): pl.pallas_call(functools.partial(partial_kernel, count, split, tuple(chos...]
    ppermute x13 -> x14, waiting for transfers between devices: 23.6 us -> 20.1 us  [swap(): lax.ppermute(value, axis, [(source, source ^ bits) for source in range(la...]
    pallas_call x1, Pallas kernels: 1.06 us -> 3.68 us  [image_taps(): pl.pallas_call(taps_kernel, out_shape=jax.ShapeDtypeStruct((9 * chans, pi...]
    unnamed x26 -> x40, local copies, waits for them, and re-layouts: 3.85 us -> 2.02 us
    mul x2 -> x1, other arithmetic: 2.37 us -> 0.67 us  [shards(): grad_mix = (mix_sum + swap(mix_sum, 'pix', 1)) * scale]
    slice x0 -> x2, local copies, waits for them, and re-layouts: none -> 1.43 us  [shards(): far.append((swap(near[3][:half], 'ch', 1), ring(far[2][half:])))]
    ppermute x3 -> x4, waiting for transfers between devices: 6.31 us -> 5.35 us  [ring(): lax.ppermute(value, 'ch', [(source, (source + 2) % 8) for source in range...]
  transfers between devices with their start and end apart: 22 -> 22, of which waited for: 9 -> 9; matrix products, arithmetic and copies ran while one was open for 4% -> 9% of each run, Pallas kernels for 33% -> 30%
where the time goes in v3:
time: 109 us; the launch traced here: 108 us
  Pallas kernels  39.4 us (36%)
  waiting for transfers between devices  29.7 us (27%)
  starting transfers between devices  26.1 us (24%)
  other arithmetic  7.89 us (7%)
  local copies, waits for them, and re-layouts  4.2 us (4%)
  between operations  1.11 us (1%)
    ppermute x14, waiting for transfers between devices, swap(): lax.ppermute(value, axis, [(source, source ^ bits) for source in range(la...  20.1 us
    pallas_call x3, Pallas kernels, kernel_partials(): pl.pallas_call(functools.partial(partial_kernel, count, split, tuple(chos...  18.8 us
    ppermute x14, starting transfers between devices, swap(): lax.ppermute(value, axis, [(source, source ^ bits) for source in range(la...  14.3 us
    pallas_call x1, Pallas kernels, image_gradient(): pl.pallas_call(kernel, out_shape=(jax.ShapeDtypeStruct((2 * pixels // wid...  10.6 us
    ppermute x2, starting transfers between devices, step_along(): lax.ppermute(value, axis, [(source, source + steps) for source in range(c...  6.89 us
    ppermute x4, waiting for transfers between devices, ring(): lax.ppermute(value, 'ch', [(source, (source + 2) % 8) for source in range...  5.35 us
    ppermute x2, waiting for transfers between devices, step_along(): lax.ppermute(value, axis, [(source, source + steps) for source in range(c...  4.21 us
    pallas_call x1, Pallas kernels, finish_both(): pl.pallas_call(functools.partial(finish_both_kernel, scale), out_shape=(j...  3.7 us
  transfers between devices with their start and end apart: 22, of which 9 were waited for; matrix products, arithmetic and copies ran while one was open for 9% of the time, Pallas kernels for 30%

profile of v3, /device:TPU:1, one launch (start us, length us, event | category | flops | bytes accessed | tf_op | source)
XLA Modules:
  0.0 108.5 jit_solution(4601687854218086805)
XLA Ops:
  0.6 2.7 %pre_grad.1 = (bf16[1024,256]{1,0:T(8,128)(2,1)}, f32[256,64]{1,0:T(8,128)}) custom-call(bf16[1024,256]{1,0:T(8,128)(2,1)} %bitcast.10, bf16[1024,256]{1,0:T(8,128)(2,1)} %bitcast.11, bf16[256,64]{1,0:T(8,128)(2,1)} %bitcast.13), custom_call_target="tpu_custom_call" | custom-call | flops 1 | bytes 1 | tf_op jit(solution)/shard_map/pre_grad/pallas_call | solution.py:58
  3.3 2.1 %collective-permute-start.1 = (bf16[1024,256]{1,0:T(8,128)(2,1)}, bf16[1024,256]{1,0:T(8,128)(2,1)S(1)}, u32[]{:S(2)}, u32[]{:S(2)}) collective-permute-start(bf16[1024,256]{1,0:T(8,128)(2,1)} %get-tuple-element.45.refs_0_), channel_id=1, source_target_pairs={{0,1},{1,0},{2,3},{3,2},{4,5},{5,4},{6,7},{7,6},{8,9},{9,8},{10,11... | collective-permute-start | bytes 1572872 | tf_op jit(solution)/shard_map/ppermute | solution.py:423
  5.4 1.3 %collective-permute-start = (bf16[1024,256]{1,0:T(8,128)(2,1)}, bf16[1024,256]{1,0:T(8,128)(2,1)S(1)}, u32[]{:S(2)}, u32[]{:S(2)}) collective-permute-start(bf16[1024,256]{1,0:T(8,128)(2,1)} %get-tuple-element.45.refs_0_), channel_id=1, source_target_pairs={{0,2},{1,3},{2,4},{3,5},{4,6},{5,7},{6,0},{7,1},{8,10},{9,11},{10,... | collective-permute-start | bytes 1572872 | tf_op jit(solution)/shard_map/ppermute | solution.py:449
  6.7 1.2 %collective-permute-start.3 = (f32[256,64]{1,0:T(8,128)}, f32[256,64]{1,0:T(8,128)S(1)}, u32[]{:S(2)}, u32[]{:S(2)}) collective-permute-start(f32[256,64]{1,0:T(8,128)} %get-tuple-element.46), channel_id=1, source_target_pairs={{0,16},{8,24},{16,0},{24,8},{1,17},{9,25},{17,1},{25,9},{2,18},{10... | collective-permute-start | bytes 196616 | tf_op jit(solution)/shard_map/ppermute | solution.py:423
  7.9 0.8 slice_bitcast_fusion
  8.6 3.6 %collective-permute-start.2 = (bf16[128,128]{1,0:T(8,128)(2,1)S(1)}, bf16[128,128]{1,0:T(8,128)(2,1)S(1)}, u32[]{:S(2)}, u32[]{:S(2)}) collective-permute-start(bf16[128,128]{1,0:T(8,128)(2,1)S(1)} %slice_bitcast_fusion), channel_id=1, source_target_pairs={{0,8},{8,16},{16,24},{1,9},{9,17},{17,25},{2,10},{10,18},{18,26},{... | collective-permute-start | bytes 98312 | tf_op jit(solution)/shard_map/ppermute | solution.py:417
  12.2 0.9 add.46
  13.1 0.9 collective-permute-start.4
  14.1 0.6 broadcast_select_fusion.1.prev_ref
  14.7 3.7 %taps.1.taps_ref = bf16[1152,1024]{1,0:T(8,128)(2,1)} custom-call(bf16[32,128,128]{2,1,0:T(8,128)(2,1)} %image_ref.1, bf16[128,128]{1,0:T(8,128)(2,1)} %broadcast_select_fusion.1.prev_ref), custom_call_target="tpu_custom_call" | custom-call | flops 1 | bytes 1 | tf_op jit(solution)/shard_map/taps/pallas_call | solution.py:95
  18.4 0.7 add_multiply_fusion
  19.0 1.0 collective-permute-done.refs_1_
  20.0 1.8 %collective-permute-start.7 = (bf16[1152,512]{1,0:T(8,128)(2,1)}, bf16[1152,512]{1,0:T(8,128)(2,1)S(1)}, u32[]{:S(2)}, u32[]{:S(2)}) collective-permute-start(bf16[1152,512]{1,0:T(8,128)(2,1)} %bitcast.6.refs_9_), channel_id=1, source_target_pairs={{0,8},{8,0},{16,24},{24,16},{1,9},{9,1},{17,25},{25,17},{2,10},{10... | collective-permute-start | bytes 3538952 | tf_op jit(solution)/shard_map/ppermute | solution.py:423
  21.8 1.2 %collective-permute-start.10 = (bf16[1152,512]{1,0:T(8,128)(2,1)}, bf16[1152,512]{1,0:T(8,128)(2,1)}, u32[]{:S(2)}, u32[]{:S(2)}) collective-permute-start(bf16[1152,512]{1,0:T(8,128)(2,1)} %bitcast.6.refs_9_), channel_id=1, source_target_pairs={{0,16},{8,24},{16,0},{24,8},{1,17},{9,25},{17,1},{25,9},{2,18},{10... | collective-permute-start | bytes 3538952 | tf_op jit(solution)/shard_map/ppermute | solution.py:423
  23.0 0.2 collective-permute-start.6
  23.2 13.1 %collective-permute-done.6.refs_5_.refs_1_ = bf16[1024,256]{1,0:T(8,128)(2,1)S(1)} collective-permute-done((bf16[1024,256]{1,0:T(8,128)(2,1)S(1)}, bf16[1024,256]{1,0:T(8,128)(2,1)S(1)}, u32[]{:S(2)}, u32[]{:S(2)}) %collective-permute-start.6) | collective-permute-done | bytes 524320 | tf_op jit(solution)/shard_map/ppermute | solution.py:423
  36.4 1.6 %collective-permute-done.5.refs_2_ = bf16[1024,256]{1,0:T(8,128)(2,1)S(1)} collective-permute-done((bf16[1024,256]{1,0:T(8,128)(2,1)S(1)}, bf16[1024,256]{1,0:T(8,128)(2,1)S(1)}, u32[]{:S(2)}, u32[]{:S(2)}) %collective-permute-start.5) | collective-permute-done | bytes 524320 | tf_op jit(solution)/shard_map/ppermute | solution.py:449
  38.0 1.1 copy-done.8
  39.0 1.2 %collective-permute-start.9 = (bf16[1024,256]{1,0:T(8,128)(2,1)S(1)}, bf16[1024,256]{1,0:T(8,128)(2,1)S(1)}, u32[]{:S(2)}, u32[]{:S(2)}) collective-permute-start(bf16[1024,256]{1,0:T(8,128)(2,1)S(1)} %collective-permute-done.5.refs_2_), channel_id=1, source_target_pairs={{0,1},{1,0},{2,3},{3,2},{4,5},{5,4},{6,7},{7,6},{8,9},{9,8},{10,11... | collective-permute-start | bytes 1572872 | tf_op jit(solution)/shard_map/ppermute | solution.py:423
  40.3 0.6 pad_add_fusion.place_ref
  40.9 5.4 %partials.3 = (bf16[1152,256]{1,0:T(8,128)(2,1)}, bf16[1152,256]{1,0:T(8,128)(2,1)}) custom-call(s32[2]{0:T(128)} %pad_add_fusion.place_ref, bf16[1152,1024]{1,0:T(8,128)(2,1)} %taps.1.taps_ref, bf16[1024,256]{1,0:T(8,128)(2,1)} %get-tuple-element.45.refs_0_, bf16[1024,256]{1,0:T(8,128)(2,1)} %copy-done.2, bf16[1024,256]{1,0:T(8,128)(2,1)} %copy-done.4), custom_call_target="tpu_custom_call" | custom-call | flops 1 | bytes 1 | tf_op jit(solution)/shard_map/partials/pallas_call | solution.py:396
  46.3 3.5 %collective-permute-done.10.refs_11_ = bf16[1152,512]{1,0:T(8,128)(2,1)} collective-permute-done((bf16[1152,512]{1,0:T(8,128)(2,1)}, bf16[1152,512]{1,0:T(8,128)(2,1)}, u32[]{:S(2)}, u32[]{:S(2)}) %collective-permute-start.10) | collective-permute-done | bytes 1179680 | tf_op jit(solution)/shard_map/ppermute | solution.py:423
  49.7 1.3 %collective-permute-done.9.refs_6_.refs_2_ = bf16[1024,256]{1,0:T(8,128)(2,1)S(1)} collective-permute-done((bf16[1024,256]{1,0:T(8,128)(2,1)S(1)}, bf16[1024,256]{1,0:T(8,128)(2,1)S(1)}, u32[]{:S(2)}, u32[]{:S(2)}) %collective-permute-start.9) | collective-permute-done | bytes 524320 | tf_op jit(solution)/shard_map/ppermute | solution.py:423
  51.0 2.8 %collective-permute-done.8.refs_3_ = bf16[1024,256]{1,0:T(8,128)(2,1)S(1)} collective-permute-done((bf16[1024,256]{1,0:T(8,128)(2,1)S(1)}, bf16[1024,256]{1,0:T(8,128)(2,1)S(1)}, u32[]{:S(2)}, u32[]{:S(2)}) %collective-permute-start.8) | collective-permute-done | bytes 524320 | tf_op jit(solution)/shard_map/ppermute | solution.py:449
  53.8 2.6 %collective-permute-start.14 = (bf16[1152,512]{1,0:T(8,128)(2,1)}, bf16[1152,512]{1,0:T(8,128)(2,1)S(1)}, u32[]{:S(2)}, u32[]{:S(2)}) collective-permute-start(bf16[1152,512]{1,0:T(8,128)(2,1)} %collective-permute-done.10.refs_11_), channel_id=1, source_target_pairs={{0,8},{8,0},{16,24},{24,16},{1,9},{9,1},{17,25},{25,17},{2,10},{10... | collective-permute-start | bytes 3538952 | tf_op jit(solution)/shard_map/ppermute | solution.py:423
  56.4 0.7 slice.10
  57.1 0.7 slice.11
  57.8 0.2 collective-permute-start.11
  58.1 7.9 %partials.4 = (bf16[1152,256]{1,0:T(8,128)(2,1)}, bf16[1152,256]{1,0:T(8,128)(2,1)}, bf16[1152,256]{1,0:T(8,128)(2,1)}, bf16[1152,256]{1,0:T(8,128)(2,1)}) custom-call(s32[2]{0:T(128)} %pad_add_fusion.place_ref, bf16[1152,1024]{1,0:T(8,128)(2,1)} %taps.1.taps_ref, bf16[1024,256]{1,0:T(8,128)(2,1)} %get-tuple-element.45.refs_0_, bf16[1024,256]{1,0:T(8,128)(2,1)} %copy-done.2, ...), custom_call_target="tpu_custom_call" | custom-call | flops 1 | bytes 1 | tf_op jit(solution)/shard_map/partials/pallas_call | solution.py:396
  66.0 1.3 %add.48.refs_0_ = bf16[1152,256]{1,0:T(8,128)(2,1)S(1)} add(bf16[1152,256]{1,0:T(8,128)(2,1)S(1)} %copy-done.15, bf16[1152,256]{1,0:T(8,128)(2,1)} %collective-permute-done.13) | non-fusion elementwise | flops 294912 | bytes 1769472 | tf_op jit(solution)/shard_map/add | solution.py:482
  67.4 1.2 %collective-permute-start.15 = (bf16[1152,256]{1,0:T(8,128)(2,1)}, bf16[1152,256]{1,0:T(8,128)(2,1)}, u32[]{:S(2)}, u32[]{:S(2)}) collective-permute-start(bf16[1152,256]{1,0:T(8,128)(2,1)} %get-tuple-element.65), channel_id=1, source_target_pairs={{0,8},{8,0},{16,24},{24,16},{1,9},{9,1},{17,25},{25,17},{2,10},{10... | collective-permute-start | bytes 1769480 | tf_op jit(solution)/shard_map/ppermute | solution.py:423
  68.7 0.1 collective-permute-start.16
  68.7 2.2 %collective-permute-start.17 = (bf16[1152,256]{1,0:T(8,128)(2,1)S(1)}, bf16[1152,256]{1,0:T(8,128)(2,1)S(1)}, u32[]{:S(2)}, u32[]{:S(2)}) collective-permute-start(bf16[1152,256]{1,0:T(8,128)(2,1)S(1)} %add.48.refs_0_), channel_id=1, source_target_pairs={{4,20},{5,21},{6,22},{7,23},{8,24},{9,25},{10,26},{11,27},{16,0},{... | collective-permute-start | bytes 1769480 | tf_op jit(solution)/shard_map/ppermute | solution.py:445
  70.9 0.5 collective-permute-done.16
  71.5 2.6 %broadcast_select_fusion = (bf16[1152,256]{1,0:T(8,128)(2,1)}, bf16[1152,256]{1,0:T(8,128)(2,1)}, bf16[1152,256]{1,0:T(8,128)(2,1)}) fusion(pred[]{:T(512)S(6)} %eq.12, bf16[1152,256]{1,0:T(8,128)(2,1)S(1)} %copy-done.12, bf16[1152,256]{1,0:T(8,128)(2,1)} %collective-permute-done.16, bf16[1152,256]{1,0:T(8,128)(2,1)S(1)} %copy-done.13, ...), kind=kLoop, calls=%fused_computation | loop fusion | flops 884736 | bytes 4128769 | tf_op jit(solution)/shard_map/jit(_where)/select_n | solution.py:506
  74.1 0.0 copy-start.14
  74.1 5.5 %partials.5 = (bf16[1152,256]{1,0:T(8,128)(2,1)}, bf16[1152,256]{1,0:T(8,128)(2,1)}) custom-call(s32[2]{0:T(128)} %pad_add_fusion.place_ref, bf16[1152,1024]{1,0:T(8,128)(2,1)} %taps.1.taps_ref, bf16[1024,256]{1,0:T(8,128)(2,1)} %copy-done.1, bf16[1024,256]{1,0:T(8,128)(2,1)} %copy-done.3, bf16[1024,256]{1,0:T(8,128)(2,1)} %copy-done, ...), custom_call_target="tpu_custom_call" | custom-call | flops 1 | bytes 1 | tf_op jit(solution)/shard_map/partials/pallas_call | solution.py:396
  79.6 1.3 %collective-permute-start.18 = (bf16[1152,256]{1,0:T(8,128)(2,1)}, bf16[1152,256]{1,0:T(8,128)(2,1)S(1)}, u32[]{:S(2)}, u32[]{:S(2)}) collective-permute-start(bf16[1152,256]{1,0:T(8,128)(2,1)} %get-tuple-element.75), channel_id=1, source_target_pairs={{0,8},{8,0},{16,24},{24,16},{1,9},{9,1},{17,25},{25,17},{2,10},{10... | collective-permute-start | bytes 1769480 | tf_op jit(solution)/shard_map/ppermute | solution.py:423
  80.9 0.1 collective-permute-start.20
  81.1 1.7 %collective-permute-done.18 = bf16[1152,256]{1,0:T(8,128)(2,1)S(1)} collective-permute-done((bf16[1152,256]{1,0:T(8,128)(2,1)}, bf16[1152,256]{1,0:T(8,128)(2,1)S(1)}, u32[]{:S(2)}, u32[]{:S(2)}) %collective-permute-start.18) | collective-permute-done | bytes 589856 | tf_op jit(solution)/shard_map/ppermute | solution.py:423
  82.8 1.2 %add.51.refs_3_ = bf16[1152,256]{1,0:T(8,128)(2,1)S(1)} add(bf16[1152,256]{1,0:T(8,128)(2,1)} %get-tuple-element.74, bf16[1152,256]{1,0:T(8,128)(2,1)S(1)} %collective-permute-done.18) | non-fusion elementwise | flops 294912 | bytes 1769472 | tf_op jit(solution)/shard_map/add | solution.py:482
  84.0 1.5 %collective-permute-start.21 = (bf16[1152,256]{1,0:T(8,128)(2,1)S(1)}, bf16[1152,256]{1,0:T(8,128)(2,1)S(1)}, u32[]{:S(2)}, u32[]{:S(2)}) collective-permute-start(bf16[1152,256]{1,0:T(8,128)(2,1)S(1)} %add.51.refs_3_), channel_id=1, source_target_pairs={{0,16},{1,17},{2,18},{3,19},{12,28},{13,29},{14,30},{15,31},{20,4}... | collective-permute-start | bytes 1769480 | tf_op jit(solution)/shard_map/ppermute | solution.py:445
  85.5 10.6 %image_grad.1 = (bf16[32,128,128]{2,1,0:T(8,128)(2,1)}, f32[256,128]{1,0:T(8,128)}, f32[256,128]{1,0:T(8,128)}) custom-call(s32[2]{0:T(128)} %pad_add_fusion.place_ref, bf16[1024,256]{1,0:T(8,128)(2,1)} %get-tuple-element.45.refs_0_, bf16[1024,256]{1,0:T(8,128)(2,1)} %copy-done.2, bf16[1024,256]{1,0:T(8,128)(2,1)} %copy-done.4, bf16[1024,256]{1,0:T(8,128)(2,1)} %copy-done.5, ...), custom_call_target="tpu_custom_call" | custom-call | flops 1 | bytes 1 | tf_op jit(solution)/shard_map/image_grad/pallas_call | solution.py:211
  96.1 3.3 %collective-permute-start.19 = (f32[256,128]{1,0:T(8,128)}, f32[256,128]{1,0:T(8,128)S(1)}, u32[]{:S(2)}, u32[]{:S(2)}) collective-permute-start(f32[256,128]{1,0:T(8,128)} %get-tuple-element.81), channel_id=1, source_target_pairs={{8,0},{16,8},{24,16},{9,1},{17,9},{25,17},{10,2},{18,10},{26,18},{... | collective-permute-start | bytes 393224 | tf_op jit(solution)/shard_map/ppermute | solution.py:417
  99.5 4.2 %collective-permute-done.19.edge_ref = f32[256,128]{1,0:T(8,128)S(1)} collective-permute-done((f32[256,128]{1,0:T(8,128)}, f32[256,128]{1,0:T(8,128)S(1)}, u32[]{:S(2)}, u32[]{:S(2)}) %collective-permute-start.19) | collective-permute-done | bytes 131104 | tf_op jit(solution)/shard_map/ppermute | solution.py:417
  103.7 0.6 copy-done.19
  104.4 0.2 copy-done.18
  104.6 3.7 %finish.1 = (bf16[32,128,128]{2,1,0:T(8,128)(2,1)}, f32[1152,512]{1,0:T(8,128)}) custom-call(s32[2]{0:T(128)} %pad_add_fusion.place_ref, bf16[32,128,128]{2,1,0:T(8,128)(2,1)} %get-tuple-element.79.image_ref, f32[256,128]{1,0:T(8,128)} %get-tuple-element.80.last_ref, f32[256,128]{1,0:T(8,128)} %copy-done.19, ...), custom_call_target="tpu_custom_call", output_to_operand_aliasing={{0}: (1, {})} | custom-call | flops 1 | bytes 1 | tf_op jit(solution)/shard_map/finish/pallas_call | solution.py:314
  (53 shorter events, 0.1 us)
Async XLA Ops:
  3.3 15.7 %collective-permute-start.1 = (bf16[1024,256]{1,0:T(8,128)(2,1)}, bf16[1024,256]{1,0:T(8,128)(2,1)S(1)}, u32[]{:S(2)}, u32[]{:S(2)}) collective-permute-start(bf16[1024,256]{1,0:T(8,128)(2,1)} %get-tuple-element.45.refs_0_), channel_id=1, source_target_pairs={{0,1},{1,0},{2,3},{3,2},{4,5},{5,4},{6,7},{7,6},{8,9},{9,8},{10,11... | collective-permute-start | bytes 1572872 | tf_op jit(solution)/shard_map/ppermute | solution.py:423
  5.4 14.7 %collective-permute-start = (bf16[1024,256]{1,0:T(8,128)(2,1)}, bf16[1024,256]{1,0:T(8,128)(2,1)S(1)}, u32[]{:S(2)}, u32[]{:S(2)}) collective-permute-start(bf16[1024,256]{1,0:T(8,128)(2,1)} %get-tuple-element.45.refs_0_), channel_id=1, source_target_pairs={{0,2},{1,3},{2,4},{3,5},{4,6},{5,7},{6,0},{7,1},{8,10},{9,11},{10,... | collective-permute-start | bytes 1572872 | tf_op jit(solution)/shard_map/ppermute | solution.py:449
  6.7 5.5 %collective-permute-start.3 = (f32[256,64]{1,0:T(8,128)}, f32[256,64]{1,0:T(8,128)S(1)}, u32[]{:S(2)}, u32[]{:S(2)}) collective-permute-start(f32[256,64]{1,0:T(8,128)} %get-tuple-element.46), channel_id=1, source_target_pairs={{0,16},{8,24},{16,0},{24,8},{1,17},{9,25},{17,1},{25,9},{2,18},{10... | collective-permute-start | bytes 196616 | tf_op jit(solution)/shard_map/ppermute | solution.py:423
  8.6 5.4 %collective-permute-start.2 = (bf16[128,128]{1,0:T(8,128)(2,1)S(1)}, bf16[128,128]{1,0:T(8,128)(2,1)S(1)}, u32[]{:S(2)}, u32[]{:S(2)}) collective-permute-start(bf16[128,128]{1,0:T(8,128)(2,1)S(1)} %slice_bitcast_fusion), channel_id=1, source_target_pairs={{0,8},{8,16},{16,24},{1,9},{9,17},{17,25},{2,10},{10,18},{18,26},{... | collective-permute-start | bytes 98312 | tf_op jit(solution)/shard_map/ppermute | solution.py:417
  13.1 5.2 %collective-permute-start.4 = (f32[256,64]{1,0:T(8,128)S(1)}, f32[256,64]{1,0:T(8,128)S(1)}, u32[]{:S(2)}, u32[]{:S(2)}) collective-permute-start(f32[256,64]{1,0:T(8,128)S(1)} %add.46), channel_id=1, source_target_pairs={{0,8},{8,0},{16,24},{24,16},{1,9},{9,1},{17,25},{25,17},{2,10},{10... | collective-permute-start | bytes 196616 | tf_op jit(solution)/shard_map/ppermute | solution.py:423
  19.0 27.2 %copy-start.1 = (bf16[1024,256]{1,0:T(8,128)(2,1)}, bf16[1024,256]{1,0:T(8,128)(2,1)S(1)}, u32[]{:S(2)}) copy-start(bf16[1024,256]{1,0:T(8,128)(2,1)S(1)} %collective-permute-done.1.refs_4_.refs_0_) | copy-start | bytes 1572868
  20.0 20.8 %copy-start.2 = (bf16[1024,256]{1,0:T(8,128)(2,1)}, bf16[1024,256]{1,0:T(8,128)(2,1)S(1)}, u32[]{:S(2)}) copy-start(bf16[1024,256]{1,0:T(8,128)(2,1)S(1)} %collective-permute-done.refs_1_) | copy-start | bytes 1572868
  20.0 17.9 %collective-permute-start.7 = (bf16[1152,512]{1,0:T(8,128)(2,1)}, bf16[1152,512]{1,0:T(8,128)(2,1)S(1)}, u32[]{:S(2)}, u32[]{:S(2)}) collective-permute-start(bf16[1152,512]{1,0:T(8,128)(2,1)} %bitcast.6.refs_9_), channel_id=1, source_target_pairs={{0,8},{8,0},{16,24},{24,16},{1,9},{9,1},{17,25},{25,17},{2,10},{10... | collective-permute-start | bytes 3538952 | tf_op jit(solution)/shard_map/ppermute | solution.py:423
  21.8 27.9 %collective-permute-start.10 = (bf16[1152,512]{1,0:T(8,128)(2,1)}, bf16[1152,512]{1,0:T(8,128)(2,1)}, u32[]{:S(2)}, u32[]{:S(2)}) collective-permute-start(bf16[1152,512]{1,0:T(8,128)(2,1)} %bitcast.6.refs_9_), channel_id=1, source_target_pairs={{0,16},{8,24},{16,0},{24,8},{1,17},{9,25},{17,1},{25,9},{2,18},{10... | collective-permute-start | bytes 3538952 | tf_op jit(solution)/shard_map/ppermute | solution.py:423
  23.0 13.3 %collective-permute-start.6 = (bf16[1024,256]{1,0:T(8,128)(2,1)S(1)}, bf16[1024,256]{1,0:T(8,128)(2,1)S(1)}, u32[]{:S(2)}, u32[]{:S(2)}) collective-permute-start(bf16[1024,256]{1,0:T(8,128)(2,1)S(1)} %collective-permute-done.refs_1_), channel_id=1, source_target_pairs={{0,1},{1,0},{2,3},{3,2},{4,5},{5,4},{6,7},{7,6},{8,9},{9,8},{10,11... | collective-permute-start | bytes 1572872 | tf_op jit(solution)/shard_map/ppermute | solution.py:423
  23.2 14.7 %collective-permute-start.5 = (bf16[1024,256]{1,0:T(8,128)(2,1)S(1)}, bf16[1024,256]{1,0:T(8,128)(2,1)S(1)}, u32[]{:S(2)}, u32[]{:S(2)}) collective-permute-start(bf16[1024,256]{1,0:T(8,128)(2,1)S(1)} %collective-permute-done.refs_1_), channel_id=1, source_target_pairs={{0,2},{1,3},{2,4},{3,5},{4,6},{5,7},{6,0},{7,1},{8,10},{9,11},{10,... | collective-permute-start | bytes 1572872 | tf_op jit(solution)/shard_map/ppermute | solution.py:449
  36.4 9.9 %copy-start.3 = (bf16[1024,256]{1,0:T(8,128)(2,1)}, bf16[1024,256]{1,0:T(8,128)(2,1)S(1)}, u32[]{:S(2)}) copy-start(bf16[1024,256]{1,0:T(8,128)(2,1)S(1)} %collective-permute-done.6.refs_5_.refs_1_) | copy-start | bytes 1572868
  38.0 2.9 %copy-start.4 = (bf16[1024,256]{1,0:T(8,128)(2,1)}, bf16[1024,256]{1,0:T(8,128)(2,1)S(1)}, u32[]{:S(2)}) copy-start(bf16[1024,256]{1,0:T(8,128)(2,1)S(1)} %collective-permute-done.5.refs_2_) | copy-start | bytes 1572868
  38.0 1.1 copy-start.8
  39.0 12.0 %collective-permute-start.9 = (bf16[1024,256]{1,0:T(8,128)(2,1)S(1)}, bf16[1024,256]{1,0:T(8,128)(2,1)S(1)}, u32[]{:S(2)}, u32[]{:S(2)}) collective-permute-start(bf16[1024,256]{1,0:T(8,128)(2,1)S(1)} %collective-permute-done.5.refs_2_), channel_id=1, source_target_pairs={{0,1},{1,0},{2,3},{3,2},{4,5},{5,4},{6,7},{7,6},{8,9},{9,8},{10,11... | collective-permute-start | bytes 1572872 | tf_op jit(solution)/shard_map/ppermute | solution.py:423
  40.3 13.5 %collective-permute-start.8 = (bf16[1024,256]{1,0:T(8,128)(2,1)S(1)}, bf16[1024,256]{1,0:T(8,128)(2,1)S(1)}, u32[]{:S(2)}, u32[]{:S(2)}) collective-permute-start(bf16[1024,256]{1,0:T(8,128)(2,1)S(1)} %collective-permute-done.5.refs_2_), channel_id=1, source_target_pairs={{0,2},{1,3},{2,4},{3,5},{4,6},{5,7},{6,0},{7,1},{8,10},{9,11},{10,... | collective-permute-start | bytes 1572872 | tf_op jit(solution)/shard_map/ppermute | solution.py:449
  51.0 7.0 %copy-start = (bf16[1024,256]{1,0:T(8,128)(2,1)}, bf16[1024,256]{1,0:T(8,128)(2,1)S(1)}, u32[]{:S(2)}) copy-start(bf16[1024,256]{1,0:T(8,128)(2,1)S(1)} %collective-permute-done.9.refs_6_.refs_2_) | copy-start | bytes 1572868
  53.8 4.3 %copy-start.5 = (bf16[1024,256]{1,0:T(8,128)(2,1)}, bf16[1024,256]{1,0:T(8,128)(2,1)S(1)}, u32[]{:S(2)}) copy-start(bf16[1024,256]{1,0:T(8,128)(2,1)S(1)} %collective-permute-done.8.refs_3_) | copy-start | bytes 1572868
  53.8 13.6 %collective-permute-start.14 = (bf16[1152,512]{1,0:T(8,128)(2,1)}, bf16[1152,512]{1,0:T(8,128)(2,1)S(1)}, u32[]{:S(2)}, u32[]{:S(2)}) collective-permute-start(bf16[1152,512]{1,0:T(8,128)(2,1)} %collective-permute-done.10.refs_11_), channel_id=1, source_target_pairs={{0,8},{8,0},{16,24},{24,16},{1,9},{9,1},{17,25},{25,17},{2,10},{10... | collective-permute-start | bytes 3538952 | tf_op jit(solution)/shard_map/ppermute | solution.py:423
  56.4 9.6 %collective-permute-start.13 = (bf16[1152,256]{1,0:T(8,128)(2,1)}, bf16[1152,256]{1,0:T(8,128)(2,1)}, u32[]{:S(2)}, u32[]{:S(2)}) collective-permute-start(bf16[1152,256]{1,0:T(8,128)(2,1)} %get-tuple-element.56), channel_id=1, source_target_pairs={{0,8},{8,0},{16,24},{24,16},{1,9},{9,1},{17,25},{25,17},{2,10},{10... | collective-permute-start | bytes 1769480 | tf_op jit(solution)/shard_map/ppermute | solution.py:423
  57.8 8.2 %copy-start.15 = (bf16[1152,256]{1,0:T(8,128)(2,1)S(1)}, bf16[1152,256]{1,0:T(8,128)(2,1)}, u32[]{:S(2)}) copy-start(bf16[1152,256]{1,0:T(8,128)(2,1)} %get-tuple-element.55) | copy-start | bytes 1769476
  57.8 9.5 %collective-permute-start.12 = (bf16[512,256]{1,0:T(8,128)(2,1)}, bf16[512,256]{1,0:T(8,128)(2,1)S(1)}, u32[]{:S(2)}, u32[]{:S(2)}) collective-permute-start(bf16[512,256]{1,0:T(8,128)(2,1)} %slice.11), channel_id=1, source_target_pairs={{0,2},{1,3},{2,4},{3,5},{4,6},{5,7},{6,0},{7,1},{8,10},{9,11},{10,... | collective-permute-start | bytes 786440 | tf_op jit(solution)/shard_map/ppermute | solution.py:449
  57.8 9.5 %collective-permute-start.11 = (bf16[512,256]{1,0:T(8,128)(2,1)}, bf16[512,256]{1,0:T(8,128)(2,1)S(1)}, u32[]{:S(2)}, u32[]{:S(2)}) collective-permute-start(bf16[512,256]{1,0:T(8,128)(2,1)} %slice.10), channel_id=1, source_target_pairs={{0,1},{1,0},{2,3},{3,2},{4,5},{5,4},{6,7},{7,6},{8,9},{9,8},{10,11... | collective-permute-start | bytes 786440 | tf_op jit(solution)/shard_map/ppermute | solution.py:423
  66.0 5.5 %copy-start.12 = (bf16[1152,256]{1,0:T(8,128)(2,1)S(1)}, bf16[1152,256]{1,0:T(8,128)(2,1)}, u32[]{:S(2)}) copy-start(bf16[1152,256]{1,0:T(8,128)(2,1)} %get-tuple-element.66) | copy-start | bytes 1769476
  66.0 5.5 %copy-start.13 = (bf16[1152,256]{1,0:T(8,128)(2,1)S(1)}, bf16[1152,256]{1,0:T(8,128)(2,1)}, u32[]{:S(2)}) copy-start(bf16[1152,256]{1,0:T(8,128)(2,1)} %get-tuple-element.64) | copy-start | bytes 1769476
  67.3 6.7 %copy-start.6 = (bf16[1152,256]{1,0:T(8,128)(2,1)}, bf16[1152,256]{1,0:T(8,128)(2,1)S(1)}, u32[]{:S(2)}) copy-start(bf16[1152,256]{1,0:T(8,128)(2,1)S(1)} %add.48.refs_0_) | copy-start | bytes 1769476
  67.4 6.7 %copy-start.10 = (bf16[512,256]{1,0:T(8,128)(2,1)}, bf16[512,256]{1,0:T(8,128)(2,1)S(1)}, u32[]{:S(2)}) copy-start(bf16[512,256]{1,0:T(8,128)(2,1)S(1)} %collective-permute-done.12.refs_4_.refs_8_) | copy-start | bytes 786436
  67.4 6.7 %copy-start.11 = (bf16[512,256]{1,0:T(8,128)(2,1)}, bf16[512,256]{1,0:T(8,128)(2,1)S(1)}, u32[]{:S(2)}) copy-start(bf16[512,256]{1,0:T(8,128)(2,1)S(1)} %collective-permute-done.11.refs_3_.refs_7_) | copy-start | bytes 786436
  67.4 6.6 %copy-start.9 = (bf16[1152,512]{1,0:T(8,128)(2,1)}, bf16[1152,512]{1,0:T(8,128)(2,1)S(1)}, u32[]{:S(2)}) copy-start(bf16[1152,512]{1,0:T(8,128)(2,1)S(1)} %collective-permute-done.14.refs_12_) | copy-start | bytes 3538948
  67.4 3.5 %collective-permute-start.15 = (bf16[1152,256]{1,0:T(8,128)(2,1)}, bf16[1152,256]{1,0:T(8,128)(2,1)}, u32[]{:S(2)}, u32[]{:S(2)}) collective-permute-start(bf16[1152,256]{1,0:T(8,128)(2,1)} %get-tuple-element.65), channel_id=1, source_target_pairs={{0,8},{8,0},{16,24},{24,16},{1,9},{9,1},{17,25},{25,17},{2,10},{10... | collective-permute-start | bytes 1769480 | tf_op jit(solution)/shard_map/ppermute | solution.py:423
  68.7 2.8 %collective-permute-start.16 = (bf16[1152,256]{1,0:T(8,128)(2,1)}, bf16[1152,256]{1,0:T(8,128)(2,1)}, u32[]{:S(2)}, u32[]{:S(2)}) collective-permute-start(bf16[1152,256]{1,0:T(8,128)(2,1)} %get-tuple-element.67), channel_id=1, source_target_pairs={{0,8},{8,0},{16,24},{24,16},{1,9},{9,1},{17,25},{25,17},{2,10},{10... | collective-permute-start | bytes 1769480 | tf_op jit(solution)/shard_map/ppermute | solution.py:423
  68.7 10.8 %collective-permute-start.17 = (bf16[1152,256]{1,0:T(8,128)(2,1)S(1)}, bf16[1152,256]{1,0:T(8,128)(2,1)S(1)}, u32[]{:S(2)}, u32[]{:S(2)}) collective-permute-start(bf16[1152,256]{1,0:T(8,128)(2,1)S(1)} %add.48.refs_0_), channel_id=1, source_target_pairs={{4,20},{5,21},{6,22},{7,23},{8,24},{9,25},{10,26},{11,27},{16,0},{... | collective-permute-start | bytes 1769480 | tf_op jit(solution)/shard_map/ppermute | solution.py:445
  74.1 6.9 %copy-start.14 = (bf16[1152,256]{1,0:T(8,128)(2,1)S(1)}, bf16[1152,256]{1,0:T(8,128)(2,1)}, u32[]{:S(2)}) copy-start(bf16[1152,256]{1,0:T(8,128)(2,1)} %get-tuple-element.83) | copy-start | bytes 1769476
  79.6 16.5 %copy-start.16 = (bf16[1152,256]{1,0:T(8,128)(2,1)}, bf16[1152,256]{1,0:T(8,128)(2,1)S(1)}, u32[]{:S(2)}) copy-start(bf16[1152,256]{1,0:T(8,128)(2,1)S(1)} %collective-permute-done.17.refs_4_) | copy-start | bytes 1769476
  79.6 3.2 %collective-permute-start.18 = (bf16[1152,256]{1,0:T(8,128)(2,1)}, bf16[1152,256]{1,0:T(8,128)(2,1)S(1)}, u32[]{:S(2)}, u32[]{:S(2)}) collective-permute-start(bf16[1152,256]{1,0:T(8,128)(2,1)} %get-tuple-element.75), channel_id=1, source_target_pairs={{0,8},{8,0},{16,24},{24,16},{1,9},{9,1},{17,25},{25,17},{2,10},{10... | collective-permute-start | bytes 1769480 | tf_op jit(solution)/shard_map/ppermute | solution.py:423
  80.9 18.5 %collective-permute-start.20 = (bf16[1152,256]{1,0:T(8,128)(2,1)S(1)}, bf16[1152,256]{1,0:T(8,128)(2,1)S(1)}, u32[]{:S(2)}, u32[]{:S(2)}) collective-permute-start(bf16[1152,256]{1,0:T(8,128)(2,1)S(1)} %copy-done.14), channel_id=1, source_target_pairs={{0,16},{8,24},{16,0},{24,8},{1,17},{9,25},{17,1},{25,9},{2,18},{10... | collective-permute-start | bytes 1769480 | tf_op jit(solution)/shard_map/ppermute | solution.py:423
  84.0 12.1 %copy-start.7 = (bf16[1152,256]{1,0:T(8,128)(2,1)}, bf16[1152,256]{1,0:T(8,128)(2,1)S(1)}, u32[]{:S(2)}) copy-start(bf16[1152,256]{1,0:T(8,128)(2,1)S(1)} %add.51.refs_3_) | copy-start | bytes 1769476
  84.0 19.7 %collective-permute-start.21 = (bf16[1152,256]{1,0:T(8,128)(2,1)S(1)}, bf16[1152,256]{1,0:T(8,128)(2,1)S(1)}, u32[]{:S(2)}, u32[]{:S(2)}) collective-permute-start(bf16[1152,256]{1,0:T(8,128)(2,1)S(1)} %add.51.refs_3_), channel_id=1, source_target_pairs={{0,16},{1,17},{2,18},{3,19},{12,28},{13,29},{14,30},{15,31},{20,4}... | collective-permute-start | bytes 1769480 | tf_op jit(solution)/shard_map/ppermute | solution.py:445
  96.1 7.6 %collective-permute-start.19 = (f32[256,128]{1,0:T(8,128)}, f32[256,128]{1,0:T(8,128)S(1)}, u32[]{:S(2)}, u32[]{:S(2)}) collective-permute-start(f32[256,128]{1,0:T(8,128)} %get-tuple-element.81), channel_id=1, source_target_pairs={{8,0},{16,8},{24,16},{9,1},{17,9},{25,17},{10,2},{18,10},{26,18},{... | collective-permute-start | bytes 393224 | tf_op jit(solution)/shard_map/ppermute | solution.py:417
  99.5 4.2 %copy-start.17 = (bf16[1152,256]{1,0:T(8,128)(2,1)}, bf16[1152,256]{1,0:T(8,128)(2,1)S(1)}, u32[]{:S(2)}) copy-start(bf16[1152,256]{1,0:T(8,128)(2,1)S(1)} %collective-permute-done.20.refs_5_) | copy-start | bytes 1769476
  103.7 0.7 copy-start.19
  103.7 0.9 copy-start.18

commit v4 on v3

--- a/solution.py
+++ b/solution.py
@@ -230,7 +230,7 @@
     )(place, *grads, *parts)
 
 
-def last_row(image_ref, last_ref, edge_ref, out_ref, row, sem, place_ref):
+def last_row(place_ref, last_ref, edge_ref, out_ref, row, sem):
     doubled, width = last_ref.shape
     chans, half = doubled // 2, width // 2
     inside = place_ref[0] % TILES != TILES - 1
@@ -243,53 +243,7 @@
 
 
 def finish_kernel(place_ref, image_ref, last_ref, edge_ref, out_ref, row, sem):
-    last_row(image_ref, last_ref, edge_ref, out_ref, row, sem, place_ref).wait()
-
-
-def finish_both_kernel(scale, place_ref, image_ref, last_ref, edge_ref, *refs):
-    totals, others, (out_ref, conv_ref) = refs[:4], refs[4:7], refs[7:9]
-    row, sem, held, sums, in_sems, out_sems = refs[9:]
-    outs, span = totals[0].shape
-    rows = outs // CUTS
-    core, outer, side = place_ref[0] & 1, place_ref[1] >> 1, place_ref[1] & 1
-    step = (core + (outer & 1)) & 3
-    mine = (((outer - step) & 3) >> 1) == (place_ref[0] >> 1)
-    pairs = ((totals[0], others[0], totals[1], others[1]), (totals[2], others[1], totals[3], others[2]))
-
-    def load(ref, half, which, cut):
-        return pltpu.make_async_copy(
-            ref.at[pl.ds(cut * rows, rows)], held.at[half, which, cut], in_sems.at[half, which, cut]
-        )
-
-    def store(half, cut):
-        start = pl.multiple_of((side if half == 0 else 1 - side) * span, span)
-        return pltpu.make_async_copy(
-            sums.at[half, cut], conv_ref.at[pl.ds(cut * rows, rows), pl.ds(start, span)], out_sems.at[half, cut]
-        )
-
-    for cut in range(CUTS):
-        for half in range(2):
-            for which in range(2):
-
-                @pl.when(mine)
-                def _():
-                    load(pairs[half][which], half, which, cut).start()
-
-                @pl.when(jnp.logical_not(mine))
-                def _():
-                    load(pairs[half][2 + which], half, which, cut).start()
-
-    row_copy = last_row(image_ref, last_ref, edge_ref, out_ref, row, sem, place_ref)
-    for cut in range(CUTS):
-        for half in range(2):
-            for which in range(2):
-                load(totals[0], half, which, cut).wait()
-            sums[half, cut] = (held[half, 0, cut].astype(F32) + held[half, 1, cut].astype(F32)) * scale
-            store(half, cut).start()
-    for cut in range(CUTS):
-        for half in range(2):
-            store(half, cut).wait()
-    row_copy.wait()
+    last_row(place_ref, last_ref, edge_ref, out_ref, row, sem).wait()
 
 
 def finish_image(place, image, last, edge):
@@ -307,28 +261,78 @@
     )(place, image, last, edge)
 
 
-def finish_both(place, image, last, edge, totals, others, scale):
+def combine_kernel(scale, place_ref, image_ref, last_ref, edge_ref, *refs):
+    refs, (image_out_ref, out_ref, row, sem, held, sums, in_sems, out_sems) = refs[:-8], refs[-8:]
+    near_first, near_kept, near_got, far_kept, far_got, far_last, over_first, over_both, over_last = refs
+    outs, span = near_first.shape
+    rows = outs // CUTS
+    core, outer, side = place_ref[0] & 1, place_ref[1] >> 1, place_ref[1] & 1
+    step = (core + (outer & 1)) & 3
+    mine = (((outer - step) & 3) >> 1) == (place_ref[0] >> 1)
+    cases = (
+        (mine, ((near_first, over_first), (far_kept, far_got, over_both))),
+        (jnp.logical_not(mine), ((near_kept, near_got, over_both), (far_last, over_last))),
+    )
+
+    def load(ref, half, which, cut):
+        return pltpu.make_async_copy(
+            ref.at[pl.ds(cut * rows, rows)], held.at[half, which, cut], in_sems.at[half, which, cut]
+        )
+
+    def store(half, cut):
+        start = pl.multiple_of((side if half == 0 else 1 - side) * span, span)
+        return pltpu.make_async_copy(
+            sums.at[half, cut], out_ref.at[pl.ds(cut * rows, rows), pl.ds(start, span)], out_sems.at[half, cut]
+        )
+
+    def case(halves):
+        pieces = [(cut, half) for cut in range(CUTS) for half in range(2)]
+        for cut, half in pieces:
+            for which, ref in enumerate(halves[half]):
+                load(ref, half, which, cut).start()
+        row_copy = last_row(place_ref, last_ref, edge_ref, image_out_ref, row, sem)
+        for cut, half in pieces:
+            total = 0.0
+            for which, ref in enumerate(halves[half]):
+                load(ref, half, which, cut).wait()
+                total = total + held[half, which, cut].astype(F32)
+            sums[half, cut] = total * scale
+            store(half, cut).start()
+        row_copy.wait()
+
+    for here, halves in cases:
+
+        @pl.when(here)
+        def _():
+            case(halves)
+
+    for cut in range(CUTS):
+        for half in range(2):
+            store(half, cut).wait()
+
+
+def combine(place, image, last, edge, pieces, scale):
     anywhere, here = pl.BlockSpec(memory_space=pl.ANY), pl.BlockSpec(memory_space=pltpu.VMEM)
-    outs, span = totals[0].shape
+    outs, span = pieces[0].shape
     rows = outs // CUTS
     return pl.pallas_call(
-        functools.partial(finish_both_kernel, scale),
+        functools.partial(combine_kernel, scale),
         out_shape=(jax.ShapeDtypeStruct(image.shape, BF), jax.ShapeDtypeStruct((outs, 2 * span), F32)),
-        in_specs=[pl.BlockSpec(memory_space=pltpu.SMEM), anywhere, here, here] + [anywhere] * 7,
+        in_specs=[pl.BlockSpec(memory_space=pltpu.SMEM), anywhere, here, here] + [anywhere] * len(pieces),
         out_specs=(anywhere, anywhere),
         scratch_shapes=[
             pltpu.VMEM(image.shape[1:], BF),
             pltpu.SemaphoreType.DMA(()),
-            pltpu.VMEM((2, 2, CUTS, rows, span), BF),
+            pltpu.VMEM((2, 3, CUTS, rows, span), BF),
             pltpu.VMEM((2, CUTS, rows, span), F32),
-            pltpu.SemaphoreType.DMA((2, 2, CUTS)),
+            pltpu.SemaphoreType.DMA((2, 3, CUTS)),
             pltpu.SemaphoreType.DMA((2, CUTS)),
         ],
         input_output_aliases={1: 0},
         compiler_params=params(60),
         cost_estimate=SMALL,
-        name="finish",
-    )(place, image, last, edge, *totals, *others)
+        name="combine",
+    )(place, image, last, edge, *pieces)
 
 
 def partial_kernel(count, split, chosen_blocks, place_ref, taps_ref, *refs):
@@ -338,12 +342,12 @@
     inputs = whole + (2 if split else 0)
     blocks, outs = refs[:inputs], refs[inputs : inputs + picks]
     taps, grads, sums, grad_sems, taps_sems, out_sems = refs[inputs + picks :]
-    half = taps_ref.shape[1] // 2
+    half, span = taps_ref.shape[1] // 2, grads.shape[1] // picks
     rows = taps.shape[1]
     part = lambda ref, cut: ref.at[pl.ds(cut * rows, rows)]
 
     def chosen(pick, index):
-        return pltpu.make_async_copy(blocks[index], grads.at[pick], grad_sems.at[pick])
+        return pltpu.make_async_copy(blocks[index], grads.at[:, pl.ds(pick * span, span)], grad_sems.at[pick])
 
     def out_copy(pick, cut):
         return pltpu.make_async_copy(sums.at[pick, cut], part(outs[pick], cut), out_sems.at[pick, cut])
@@ -363,7 +367,7 @@
                     for piece in range(2):
                         pltpu.make_async_copy(
                             blocks[whole + piece],
-                            grads.at[pick, pl.ds(piece * half, half)],
+                            grads.at[pl.ds(piece * half, half), pl.ds(pick * span, span)],
                             grad_sems.at[pick],
                         ).start()
 
@@ -372,13 +376,16 @@
         copy.start()
     for pick in range(1, picks):
         start(pick)
-    for pick in range(picks):
-        chosen(pick, 0).wait()
+    for first in range(0, picks, 2):
+        for pick in (first, first + 1):
+            chosen(pick, 0).wait()
         for cut in range(CUTS):
-            if pick == 0:
+            if first == 0:
                 taps_in[cut].wait()
-            sums[pick, cut] = dot_nn(taps[cut], grads[pick]).astype(BF)
-            out_copy(pick, cut).start()
+            total = dot_nn(taps[cut], grads[:, first * span : (first + 2) * span]).astype(BF)
+            for pick in (first, first + 1):
+                sums[pick, cut] = total[:, (pick - first) * span : (pick - first + 1) * span]
+                out_copy(pick, cut).start()
     for pick in range(picks):
         for cut in range(CUTS):
             out_copy(pick, cut).wait()
@@ -400,7 +407,7 @@
         out_specs=(anywhere,) * picks,
         scratch_shapes=[
             pltpu.VMEM((CUTS, rows, pixels), BF),
-            pltpu.VMEM((picks, pixels, span), BF),
+            pltpu.VMEM((pixels, picks * span), BF),
             pltpu.VMEM((picks, CUTS, rows, span), BF),
             pltpu.SemaphoreType.DMA((picks,)),
             pltpu.SemaphoreType.DMA((CUTS,)),
@@ -455,7 +462,6 @@
     pix_count, ch_count = lax.axis_size("pix"), lax.axis_size("ch")
     pix, ch = lax.axis_index("pix"), lax.axis_index("ch")
     first_tile = pix % TILES == 0
-    last_tile = pix % TILES == TILES - 1
     pixels = tile_rows * width
     scale = 1.0 / float(pix_count * pixels) ** 0.5
 
@@ -476,11 +482,6 @@
         near.append(ring(near[0]))
         mix_sum = mix_part + swap(mix_part, "pix", 2)
         grad_mix = (mix_sum + swap(mix_sum, "pix", 1)) * scale
-        totals = [[None] * 2, [None] * 2]
-
-        def add_up(sums, phase, half):
-            totals[phase][half] = sums[1] + swap(sums[0], "pix", 1)
-
         near[1], far[0], taps, grad_mix, kernel_own = tie((near[1], far[0], taps, grad_mix, kernel_own))
         far.append(swap(near[1], "ch", 1))
         near.append(ring(near[1]))
@@ -493,26 +494,24 @@
         near[3], far[2], first, kernel_x = tie((near[3], far[2], first, kernel_x))
         half = pixels // 2
         far.append((swap(near[3][:half], "ch", 1), ring(far[2][half:])))
-        add_up(first, 0, 0)
+        total_first = first[1] + swap(first[0], "pix", 1)
         kernel_xcore = swap(kernel_x, "pix", 1)
         second = kernel_partials(
             place, taps, near + far[:3], [(0, 0, 4), (0, 1, 0), (1, 0, 4), (1, 1, 0)]
         )
-        far[3], totals[0][0], second, kernel_xcore = tie((far[3], totals[0][0], second, kernel_xcore))
+        far[3], total_first, second, kernel_xcore = tie((far[3], total_first, second, kernel_xcore))
+        over_first = send_over(total_first, 0)
+        got = [swap(second[0], "pix", 1), swap(second[1], "pix", 1)]
         mine = kept_here(pix, ch // 2, 0)
-        arrived_first = send_over(totals[0][0], 0)
-        add_up(second[::2], 0, 1)
-        add_up(second[1::2], 1, 0)
-        crossing = jnp.where(mine, totals[1][0], totals[0][1])
-        crossing, taps = tie((crossing, taps))
-        arrived_both = swap(crossing, "pix", 2)
+        crossing = jnp.where(mine, second[3], second[2]) + jnp.where(mine, got[1], got[0])
         third = kernel_partials(place, taps, far, [(0, 1, 0), (1, 1, 0)])
-        third, arrived_first = tie((third, arrived_first))
-        add_up(third, 1, 1)
-        arrived_last = send_over(totals[1][1], 1)
+        third, over_first, crossing = tie((third, over_first, crossing))
+        over_both = swap(crossing, "pix", 2)
+        total_last = third[1] + swap(third[0], "pix", 1)
+        over_last = send_over(total_last, 1)
         grads = near + far
         parts = [kernel_own, kernel_core, kernel_x, kernel_xcore]
-        image_at = (place, totals[1][1])
+        image_at = (place, total_last)
     else:
         grad_mix = lax.psum(mix_part, "pix") * scale
         grad_all = lax.all_gather(grad_pre, "ch", axis=0)
@@ -524,18 +523,16 @@
     grad_in, last, edge = image_gradient(tie(image_at)[0], rings, grads, parts, width)
     edge = step_along(edge, "pix", -1)
     if rings:
-        grad_in, grad_conv = finish_both(
+        grad_in, grad_conv = combine(
             place,
             grad_in,
             last,
             edge,
-            [totals[0][0], totals[1][0], totals[0][1], totals[1][1]],
-            [arrived_first, arrived_both, arrived_last],
+            [total_first, second[3], got[1], second[2], got[0], total_last, over_first, over_both, over_last],
             scale,
         )
     else:
-        grad_in = finish_image(place, grad_in, last, edge)
-        grad_conv = grad_conv * scale
+        grad_in, grad_conv = finish_image(place, grad_in, last, edge), grad_conv * scale
     return (grad_in, grad_conv.reshape(conv_weight.shape), grad_mix.reshape(mix_weight.shape))
 
 

time: 109 us -> 108 us (level)
  other arithmetic: 7.89 us -> 4.3 us
  waiting for transfers between devices: 29.7 us -> 32.2 us
  starting transfers between devices: 26.1 us -> 28.1 us
  Pallas kernels: 39.4 us -> 37.7 us
    select_n x1 -> x0, other arithmetic: 2.56 us -> none  [shards(): crossing = jnp.where(mine, totals[1][0], totals[0][1])]
    pallas_call x3, Pallas kernels: 18.8 us -> 16.8 us  [kernel_partials(): pl.pallas_call(functools.partial(partial_kernel, count, split, tuple(chos...]
    ppermute x14, starting transfers between devices: 14.3 us -> 15.8 us  [swap(): lax.ppermute(value, axis, [(source, source ^ bits) for source in range(la...]
    slice x2, local copies, waits for them, and re-layouts: 1.43 us -> 0.04 us  [shards(): far.append((swap(near[3][:half], 'ch', 1), ring(far[2][half:])))]
    unnamed x40 -> x44, local copies, waits for them, and re-layouts: 2.02 us -> 3.17 us
    add x2 -> x3, other arithmetic: 2.51 us -> 1.49 us  [the longest x1 1.21 us: shards(): total_first = first[1] + swap(first[0], 'pix', 1)]
  transfers between devices with their start and end apart: 22 -> 22, of which waited for: 9 -> 10; matrix products, arithmetic and copies ran while one was open for 9% -> 5% of each run, Pallas kernels for 30% -> 29%
where the time goes in v4:
time: 108 us; the launch traced here: 107 us
  Pallas kernels  37.7 us (35%)
  waiting for transfers between devices  32.2 us (30%)
  starting transfers between devices  28.1 us (26%)
  other arithmetic  4.3 us (4%)
  local copies, waits for them, and re-layouts  3.97 us (4%)
  between operations  1.11 us (1%)
    ppermute x14, waiting for transfers between devices, swap(): lax.ppermute(value, axis, [(source, source ^ bits) for source in range(la...  20 us
    pallas_call x3, Pallas kernels, kernel_partials(): pl.pallas_call(functools.partial(partial_kernel, count, split, tuple(chos...  16.8 us
    ppermute x14, starting transfers between devices, swap(): lax.ppermute(value, axis, [(source, source ^ bits) for source in range(la...  15.8 us
    pallas_call x1, Pallas kernels, image_gradient(): pl.pallas_call(kernel, out_shape=(jax.ShapeDtypeStruct((2 * pixels // wid...  10.6 us
    ppermute x2, starting transfers between devices, step_along(): lax.ppermute(value, axis, [(source, source + steps) for source in range(c...  6.52 us
    ppermute x4, waiting for transfers between devices, ring(): lax.ppermute(value, 'ch', [(source, (source + 2) % 8) for source in range...  6.38 us
    ppermute x2, waiting for transfers between devices, step_along(): lax.ppermute(value, axis, [(source, source + steps) for source in range(c...  4.97 us
    ppermute x2, starting transfers between devices, send_over(): return lax.ppermute(value, ('pix', 'ch'), pairs)  4.46 us
  transfers between devices with their start and end apart: 22, of which 10 were waited for; matrix products, arithmetic and copies ran while one was open for 5% of the time, Pallas kernels for 29%

profile of v4, /device:TPU:1, one launch (start us, length us, event | category | flops | bytes accessed | tf_op | source)
XLA Modules:
  0.0 107.3 jit_solution(17406465761028696186)
XLA Ops:
  0.6 2.6 %pre_grad.1 = (bf16[1024,256]{1,0:T(8,128)(2,1)}, f32[256,64]{1,0:T(8,128)}) custom-call(bf16[1024,256]{1,0:T(8,128)(2,1)} %bitcast.10, bf16[1024,256]{1,0:T(8,128)(2,1)} %bitcast.11, bf16[256,64]{1,0:T(8,128)(2,1)} %bitcast.13), custom_call_target="tpu_custom_call" | custom-call | flops 1 | bytes 1 | tf_op jit(solution)/shard_map/pre_grad/pallas_call | solution.py:58
  3.3 2.1 %collective-permute-start.1 = (bf16[1024,256]{1,0:T(8,128)(2,1)}, bf16[1024,256]{1,0:T(8,128)(2,1)S(1)}, u32[]{:S(2)}, u32[]{:S(2)}) collective-permute-start(bf16[1024,256]{1,0:T(8,128)(2,1)} %get-tuple-element.44.refs_0_), channel_id=1, source_target_pairs={{0,1},{1,0},{2,3},{3,2},{4,5},{5,4},{6,7},{7,6},{8,9},{9,8},{10,11... | collective-permute-start | bytes 1572872 | tf_op jit(solution)/shard_map/ppermute | solution.py:430
  5.3 1.3 %collective-permute-start = (bf16[1024,256]{1,0:T(8,128)(2,1)}, bf16[1024,256]{1,0:T(8,128)(2,1)S(1)}, u32[]{:S(2)}, u32[]{:S(2)}) collective-permute-start(bf16[1024,256]{1,0:T(8,128)(2,1)} %get-tuple-element.44.refs_0_), channel_id=1, source_target_pairs={{0,2},{1,3},{2,4},{3,5},{4,6},{5,7},{6,0},{7,1},{8,10},{9,11},{10,... | collective-permute-start | bytes 1572872 | tf_op jit(solution)/shard_map/ppermute | solution.py:456
  6.6 1.2 %collective-permute-start.3 = (f32[256,64]{1,0:T(8,128)}, f32[256,64]{1,0:T(8,128)S(1)}, u32[]{:S(2)}, u32[]{:S(2)}) collective-permute-start(f32[256,64]{1,0:T(8,128)} %get-tuple-element.45), channel_id=1, source_target_pairs={{0,16},{8,24},{16,0},{24,8},{1,17},{9,25},{17,1},{25,9},{2,18},{10... | collective-permute-start | bytes 196616 | tf_op jit(solution)/shard_map/ppermute | solution.py:430
  7.9 0.8 slice_bitcast_fusion
  8.6 3.6 %collective-permute-start.2 = (bf16[128,128]{1,0:T(8,128)(2,1)S(1)}, bf16[128,128]{1,0:T(8,128)(2,1)S(1)}, u32[]{:S(2)}, u32[]{:S(2)}) collective-permute-start(bf16[128,128]{1,0:T(8,128)(2,1)S(1)} %slice_bitcast_fusion), channel_id=1, source_target_pairs={{0,8},{8,16},{16,24},{1,9},{9,17},{17,25},{2,10},{10,18},{18,26},{... | collective-permute-start | bytes 98312 | tf_op jit(solution)/shard_map/ppermute | solution.py:424
  12.2 0.9 add.38
  13.1 0.9 collective-permute-start.4
  14.0 0.6 broadcast_select_fusion.prev_ref
  14.7 3.7 %taps.1.taps_ref = bf16[1152,1024]{1,0:T(8,128)(2,1)} custom-call(bf16[32,128,128]{2,1,0:T(8,128)(2,1)} %image_ref.1, bf16[128,128]{1,0:T(8,128)(2,1)} %broadcast_select_fusion.prev_ref), custom_call_target="tpu_custom_call" | custom-call | flops 1 | bytes 1 | tf_op jit(solution)/shard_map/taps/pallas_call | solution.py:95
  18.3 0.7 add_multiply_fusion
  19.0 1.0 collective-permute-done.refs_1_
  20.0 1.8 %collective-permute-start.7 = (bf16[1152,512]{1,0:T(8,128)(2,1)}, bf16[1152,512]{1,0:T(8,128)(2,1)S(1)}, u32[]{:S(2)}, u32[]{:S(2)}) collective-permute-start(bf16[1152,512]{1,0:T(8,128)(2,1)} %bitcast.6.refs_9_), channel_id=1, source_target_pairs={{0,8},{8,0},{16,24},{24,16},{1,9},{9,1},{17,25},{25,17},{2,10},{10... | collective-permute-start | bytes 3538952 | tf_op jit(solution)/shard_map/ppermute | solution.py:430
  21.8 1.2 %collective-permute-start.10 = (bf16[1152,512]{1,0:T(8,128)(2,1)}, bf16[1152,512]{1,0:T(8,128)(2,1)}, u32[]{:S(2)}, u32[]{:S(2)}) collective-permute-start(bf16[1152,512]{1,0:T(8,128)(2,1)} %bitcast.6.refs_9_), channel_id=1, source_target_pairs={{0,16},{8,24},{16,0},{24,8},{1,17},{9,25},{17,1},{25,9},{2,18},{10... | collective-permute-start | bytes 3538952 | tf_op jit(solution)/shard_map/ppermute | solution.py:430
  23.0 0.2 collective-permute-start.6
  23.2 13.1 %collective-permute-done.6.refs_5_.refs_1_ = bf16[1024,256]{1,0:T(8,128)(2,1)S(1)} collective-permute-done((bf16[1024,256]{1,0:T(8,128)(2,1)S(1)}, bf16[1024,256]{1,0:T(8,128)(2,1)S(1)}, u32[]{:S(2)}, u32[]{:S(2)}) %collective-permute-start.6) | collective-permute-done | bytes 524320 | tf_op jit(solution)/shard_map/ppermute | solution.py:430
  36.3 1.6 %collective-permute-done.5.refs_2_ = bf16[1024,256]{1,0:T(8,128)(2,1)S(1)} collective-permute-done((bf16[1024,256]{1,0:T(8,128)(2,1)S(1)}, bf16[1024,256]{1,0:T(8,128)(2,1)S(1)}, u32[]{:S(2)}, u32[]{:S(2)}) %collective-permute-start.5) | collective-permute-done | bytes 524320 | tf_op jit(solution)/shard_map/ppermute | solution.py:456
  38.0 1.1 %copy-done.12 = bf16[1152,512]{1,0:T(8,128)(2,1)} copy-done((bf16[1152,512]{1,0:T(8,128)(2,1)}, bf16[1152,512]{1,0:T(8,128)(2,1)S(1)}, u32[]{:S(2)}) %copy-start.12) | copy-done | bytes 1179672
  39.0 1.2 %collective-permute-start.9 = (bf16[1024,256]{1,0:T(8,128)(2,1)S(1)}, bf16[1024,256]{1,0:T(8,128)(2,1)S(1)}, u32[]{:S(2)}, u32[]{:S(2)}) collective-permute-start(bf16[1024,256]{1,0:T(8,128)(2,1)S(1)} %collective-permute-done.5.refs_2_), channel_id=1, source_target_pairs={{0,1},{1,0},{2,3},{3,2},{4,5},{5,4},{6,7},{7,6},{8,9},{9,8},{10,11... | collective-permute-start | bytes 1572872 | tf_op jit(solution)/shard_map/ppermute | solution.py:430
  40.3 0.6 pad_add_fusion.place_ref
  40.9 4.9 %partials.3 = (bf16[1152,256]{1,0:T(8,128)(2,1)}, bf16[1152,256]{1,0:T(8,128)(2,1)}) custom-call(s32[2]{0:T(128)} %pad_add_fusion.place_ref, bf16[1152,1024]{1,0:T(8,128)(2,1)} %taps.1.taps_ref, bf16[1024,256]{1,0:T(8,128)(2,1)} %get-tuple-element.44.refs_0_, bf16[1024,256]{1,0:T(8,128)(2,1)} %copy-done.2, bf16[1024,256]{1,0:T(8,128)(2,1)} %copy-done.4), custom_call_target="tpu_custom_call" | custom-call | flops 1 | bytes 1 | tf_op jit(solution)/shard_map/partials/pallas_call | solution.py:403
  45.8 3.9 %collective-permute-done.10.refs_11_ = bf16[1152,512]{1,0:T(8,128)(2,1)} collective-permute-done((bf16[1152,512]{1,0:T(8,128)(2,1)}, bf16[1152,512]{1,0:T(8,128)(2,1)}, u32[]{:S(2)}, u32[]{:S(2)}) %collective-permute-start.10) | collective-permute-done | bytes 1179680 | tf_op jit(solution)/shard_map/ppermute | solution.py:430
  49.7 1.3 %collective-permute-done.9.refs_6_.refs_2_ = bf16[1024,256]{1,0:T(8,128)(2,1)S(1)} collective-permute-done((bf16[1024,256]{1,0:T(8,128)(2,1)S(1)}, bf16[1024,256]{1,0:T(8,128)(2,1)S(1)}, u32[]{:S(2)}, u32[]{:S(2)}) %collective-permute-start.9) | collective-permute-done | bytes 524320 | tf_op jit(solution)/shard_map/ppermute | solution.py:430
  51.0 2.8 %collective-permute-done.8.refs_3_ = bf16[1024,256]{1,0:T(8,128)(2,1)S(1)} collective-permute-done((bf16[1024,256]{1,0:T(8,128)(2,1)S(1)}, bf16[1024,256]{1,0:T(8,128)(2,1)S(1)}, u32[]{:S(2)}, u32[]{:S(2)}) %collective-permute-start.8) | collective-permute-done | bytes 524320 | tf_op jit(solution)/shard_map/ppermute | solution.py:456
  53.8 2.6 %collective-permute-start.14 = (bf16[1152,512]{1,0:T(8,128)(2,1)}, bf16[1152,512]{1,0:T(8,128)(2,1)S(1)}, u32[]{:S(2)}, u32[]{:S(2)}) collective-permute-start(bf16[1152,512]{1,0:T(8,128)(2,1)} %collective-permute-done.10.refs_11_), channel_id=1, source_target_pairs={{0,8},{8,0},{16,24},{24,16},{1,9},{9,1},{17,25},{25,17},{2,10},{10... | collective-permute-start | bytes 3538952 | tf_op jit(solution)/shard_map/ppermute | solution.py:430
  56.5 0.1 collective-permute-start.12
  56.5 0.3 collective-permute-start.11
  56.8 6.6 %partials.4 = (bf16[1152,256]{1,0:T(8,128)(2,1)}, bf16[1152,256]{1,0:T(8,128)(2,1)}, bf16[1152,256]{1,0:T(8,128)(2,1)}, bf16[1152,256]{1,0:T(8,128)(2,1)}) custom-call(s32[2]{0:T(128)} %pad_add_fusion.place_ref, bf16[1152,1024]{1,0:T(8,128)(2,1)} %taps.1.taps_ref, bf16[1024,256]{1,0:T(8,128)(2,1)} %get-tuple-element.44.refs_0_, bf16[1024,256]{1,0:T(8,128)(2,1)} %copy-done.2, ...), custom_call_target="tpu_custom_call" | custom-call | flops 1 | bytes 1 | tf_op jit(solution)/shard_map/partials/pallas_call | solution.py:403
  63.4 1.2 %add.40.refs_0_ = bf16[1152,256]{1,0:T(8,128)(2,1)S(1)} add(bf16[1152,256]{1,0:T(8,128)(2,1)S(1)} %copy-done.16, bf16[1152,256]{1,0:T(8,128)(2,1)} %collective-permute-done.13) | non-fusion elementwise | flops 294912 | bytes 1769472 | tf_op jit(solution)/shard_map/add | solution.py:497
  64.7 1.0 collective-permute-done.12.refs_4_.refs_8_
  65.7 1.4 %collective-permute-start.16 = (bf16[1152,256]{1,0:T(8,128)(2,1)}, bf16[1152,256]{1,0:T(8,128)(2,1)S(1)}, u32[]{:S(2)}, u32[]{:S(2)}) collective-permute-start(bf16[1152,256]{1,0:T(8,128)(2,1)} %get-tuple-element.70), channel_id=1, source_target_pairs={{0,8},{8,0},{16,24},{24,16},{1,9},{9,1},{17,25},{25,17},{2,10},{10... | collective-permute-start | bytes 1769480 | tf_op jit(solution)/shard_map/ppermute | solution.py:430
  67.1 0.6 collective-permute-start.17
  67.8 3.0 %collective-permute-start.15 = (bf16[1152,256]{1,0:T(8,128)(2,1)S(1)}, bf16[1152,256]{1,0:T(8,128)(2,1)}, u32[]{:S(2)}, u32[]{:S(2)}) collective-permute-start(bf16[1152,256]{1,0:T(8,128)(2,1)S(1)} %add.40.refs_0_), channel_id=1, source_target_pairs={{4,20},{5,21},{6,22},{7,23},{8,24},{9,25},{10,26},{11,27},{16,0},{... | collective-permute-start | bytes 1769480 | tf_op jit(solution)/shard_map/ppermute | solution.py:452
  70.8 5.3 %partials.5 = (bf16[1152,256]{1,0:T(8,128)(2,1)}, bf16[1152,256]{1,0:T(8,128)(2,1)}) custom-call(s32[2]{0:T(128)} %pad_add_fusion.place_ref, bf16[1152,1024]{1,0:T(8,128)(2,1)} %taps.1.taps_ref, bf16[1024,256]{1,0:T(8,128)(2,1)} %copy-done.1, bf16[1024,256]{1,0:T(8,128)(2,1)} %copy-done.3, bf16[1024,256]{1,0:T(8,128)(2,1)} %copy-done, ...), custom_call_target="tpu_custom_call" | custom-call | flops 1 | bytes 1 | tf_op jit(solution)/shard_map/partials/pallas_call | solution.py:403
  76.2 0.1 select_add_fusion
  76.3 0.7 copy-done.10
  77.0 0.2 copy-done.11
  77.2 0.4 copy-done.21
  77.5 2.1 %collective-permute-start.18 = (bf16[1152,256]{1,0:T(8,128)(2,1)S(1)}, bf16[1152,256]{1,0:T(8,128)(2,1)S(1)}, u32[]{:S(2)}, u32[]{:S(2)}) collective-permute-start(bf16[1152,256]{1,0:T(8,128)(2,1)S(1)} %copy-done.21), channel_id=1, source_target_pairs={{0,8},{8,0},{16,24},{24,16},{1,9},{9,1},{17,25},{25,17},{2,10},{10... | collective-permute-start | bytes 1769480 | tf_op jit(solution)/shard_map/ppermute | solution.py:430
  79.7 1.6 %collective-permute-done.18 = bf16[1152,256]{1,0:T(8,128)(2,1)S(1)} collective-permute-done((bf16[1152,256]{1,0:T(8,128)(2,1)S(1)}, bf16[1152,256]{1,0:T(8,128)(2,1)S(1)}, u32[]{:S(2)}, u32[]{:S(2)}) %collective-permute-start.18) | collective-permute-done | bytes 589856 | tf_op jit(solution)/shard_map/ppermute | solution.py:430
  81.3 0.2 add.47.refs_5_
  81.5 1.5 %collective-permute-start.21 = (bf16[1152,256]{1,0:T(8,128)(2,1)S(1)}, bf16[1152,256]{1,0:T(8,128)(2,1)S(1)}, u32[]{:S(2)}, u32[]{:S(2)}) collective-permute-start(bf16[1152,256]{1,0:T(8,128)(2,1)S(1)} %add.47.refs_5_), channel_id=1, source_target_pairs={{0,16},{1,17},{2,18},{3,19},{12,28},{13,29},{14,30},{15,31},{20,4}... | collective-permute-start | bytes 1769480 | tf_op jit(solution)/shard_map/ppermute | solution.py:452
  82.9 10.6 %image_grad.1 = (bf16[32,128,128]{2,1,0:T(8,128)(2,1)}, f32[256,128]{1,0:T(8,128)}, f32[256,128]{1,0:T(8,128)}) custom-call(s32[2]{0:T(128)} %pad_add_fusion.place_ref, bf16[1024,256]{1,0:T(8,128)(2,1)} %get-tuple-element.44.refs_0_, bf16[1024,256]{1,0:T(8,128)(2,1)} %copy-done.2, bf16[1024,256]{1,0:T(8,128)(2,1)} %copy-done.4, bf16[1024,256]{1,0:T(8,128)(2,1)} %copy-done.5, ...), custom_call_target="tpu_custom_call" | custom-call | flops 1 | bytes 1 | tf_op jit(solution)/shard_map/image_grad/pallas_call | solution.py:211
  93.6 3.0 %collective-permute-start.19 = (f32[256,128]{1,0:T(8,128)}, f32[256,128]{1,0:T(8,128)S(1)}, u32[]{:S(2)}, u32[]{:S(2)}) collective-permute-start(f32[256,128]{1,0:T(8,128)} %get-tuple-element.79), channel_id=1, source_target_pairs={{8,0},{16,8},{24,16},{9,1},{17,9},{25,17},{10,2},{18,10},{26,18},{... | collective-permute-start | bytes 393224 | tf_op jit(solution)/shard_map/ppermute | solution.py:424
  96.6 5.0 %collective-permute-done.19.edge_ref = f32[256,128]{1,0:T(8,128)S(1)} collective-permute-done((f32[256,128]{1,0:T(8,128)}, f32[256,128]{1,0:T(8,128)S(1)}, u32[]{:S(2)}, u32[]{:S(2)}) %collective-permute-start.19) | collective-permute-done | bytes 131104 | tf_op jit(solution)/shard_map/ppermute | solution.py:424
  101.6 0.9 collective-permute-done.21.refs_8_
  102.4 0.8 copy-done.19
  103.3 3.9 %combine.1 = (bf16[32,128,128]{2,1,0:T(8,128)(2,1)}, f32[1152,512]{1,0:T(8,128)}) custom-call(s32[2]{0:T(128)} %pad_add_fusion.place_ref, bf16[32,128,128]{2,1,0:T(8,128)(2,1)} %get-tuple-element.77.image_ref, f32[256,128]{1,0:T(8,128)} %get-tuple-element.78.last_ref, f32[256,128]{1,0:T(8,128)} %copy-done.20, ...), custom_call_target="tpu_custom_call", output_to_operand_aliasing={{0}: (1, {})} | custom-call | flops 1 | bytes 1 | tf_op jit(solution)/shard_map/combine/pallas_call | solution.py:318
  (57 shorter events, 0.2 us)
Async XLA Ops:
  3.3 15.7 %collective-permute-start.1 = (bf16[1024,256]{1,0:T(8,128)(2,1)}, bf16[1024,256]{1,0:T(8,128)(2,1)S(1)}, u32[]{:S(2)}, u32[]{:S(2)}) collective-permute-start(bf16[1024,256]{1,0:T(8,128)(2,1)} %get-tuple-element.44.refs_0_), channel_id=1, source_target_pairs={{0,1},{1,0},{2,3},{3,2},{4,5},{5,4},{6,7},{7,6},{8,9},{9,8},{10,11... | collective-permute-start | bytes 1572872 | tf_op jit(solution)/shard_map/ppermute | solution.py:430
  5.3 14.7 %collective-permute-start = (bf16[1024,256]{1,0:T(8,128)(2,1)}, bf16[1024,256]{1,0:T(8,128)(2,1)S(1)}, u32[]{:S(2)}, u32[]{:S(2)}) collective-permute-start(bf16[1024,256]{1,0:T(8,128)(2,1)} %get-tuple-element.44.refs_0_), channel_id=1, source_target_pairs={{0,2},{1,3},{2,4},{3,5},{4,6},{5,7},{6,0},{7,1},{8,10},{9,11},{10,... | collective-permute-start | bytes 1572872 | tf_op jit(solution)/shard_map/ppermute | solution.py:456
  6.6 5.5 %collective-permute-start.3 = (f32[256,64]{1,0:T(8,128)}, f32[256,64]{1,0:T(8,128)S(1)}, u32[]{:S(2)}, u32[]{:S(2)}) collective-permute-start(f32[256,64]{1,0:T(8,128)} %get-tuple-element.45), channel_id=1, source_target_pairs={{0,16},{8,24},{16,0},{24,8},{1,17},{9,25},{17,1},{25,9},{2,18},{10... | collective-permute-start | bytes 196616 | tf_op jit(solution)/shard_map/ppermute | solution.py:430
  8.6 5.4 %collective-permute-start.2 = (bf16[128,128]{1,0:T(8,128)(2,1)S(1)}, bf16[128,128]{1,0:T(8,128)(2,1)S(1)}, u32[]{:S(2)}, u32[]{:S(2)}) collective-permute-start(bf16[128,128]{1,0:T(8,128)(2,1)S(1)} %slice_bitcast_fusion), channel_id=1, source_target_pairs={{0,8},{8,16},{16,24},{1,9},{9,17},{17,25},{2,10},{10,18},{18,26},{... | collective-permute-start | bytes 98312 | tf_op jit(solution)/shard_map/ppermute | solution.py:424
  13.1 5.2 %collective-permute-start.4 = (f32[256,64]{1,0:T(8,128)S(1)}, f32[256,64]{1,0:T(8,128)S(1)}, u32[]{:S(2)}, u32[]{:S(2)}) collective-permute-start(f32[256,64]{1,0:T(8,128)S(1)} %add.38), channel_id=1, source_target_pairs={{0,8},{8,0},{16,24},{24,16},{1,9},{9,1},{17,25},{25,17},{2,10},{10... | collective-permute-start | bytes 196616 | tf_op jit(solution)/shard_map/ppermute | solution.py:430
  19.0 26.8 %copy-start.1 = (bf16[1024,256]{1,0:T(8,128)(2,1)}, bf16[1024,256]{1,0:T(8,128)(2,1)S(1)}, u32[]{:S(2)}) copy-start(bf16[1024,256]{1,0:T(8,128)(2,1)S(1)} %collective-permute-done.1.refs_4_.refs_0_) | copy-start | bytes 1572868
  20.0 20.8 %copy-start.2 = (bf16[1024,256]{1,0:T(8,128)(2,1)}, bf16[1024,256]{1,0:T(8,128)(2,1)S(1)}, u32[]{:S(2)}) copy-start(bf16[1024,256]{1,0:T(8,128)(2,1)S(1)} %collective-permute-done.refs_1_) | copy-start | bytes 1572868
  20.0 17.9 %collective-permute-start.7 = (bf16[1152,512]{1,0:T(8,128)(2,1)}, bf16[1152,512]{1,0:T(8,128)(2,1)S(1)}, u32[]{:S(2)}, u32[]{:S(2)}) collective-permute-start(bf16[1152,512]{1,0:T(8,128)(2,1)} %bitcast.6.refs_9_), channel_id=1, source_target_pairs={{0,8},{8,0},{16,24},{24,16},{1,9},{9,1},{17,25},{25,17},{2,10},{10... | collective-permute-start | bytes 3538952 | tf_op jit(solution)/shard_map/ppermute | solution.py:430
  21.8 27.9 %collective-permute-start.10 = (bf16[1152,512]{1,0:T(8,128)(2,1)}, bf16[1152,512]{1,0:T(8,128)(2,1)}, u32[]{:S(2)}, u32[]{:S(2)}) collective-permute-start(bf16[1152,512]{1,0:T(8,128)(2,1)} %bitcast.6.refs_9_), channel_id=1, source_target_pairs={{0,16},{8,24},{16,0},{24,8},{1,17},{9,25},{17,1},{25,9},{2,18},{10... | collective-permute-start | bytes 3538952 | tf_op jit(solution)/shard_map/ppermute | solution.py:430
  23.0 13.3 %collective-permute-start.6 = (bf16[1024,256]{1,0:T(8,128)(2,1)S(1)}, bf16[1024,256]{1,0:T(8,128)(2,1)S(1)}, u32[]{:S(2)}, u32[]{:S(2)}) collective-permute-start(bf16[1024,256]{1,0:T(8,128)(2,1)S(1)} %collective-permute-done.refs_1_), channel_id=1, source_target_pairs={{0,1},{1,0},{2,3},{3,2},{4,5},{5,4},{6,7},{7,6},{8,9},{9,8},{10,11... | collective-permute-start | bytes 1572872 | tf_op jit(solution)/shard_map/ppermute | solution.py:430
  23.2 14.7 %collective-permute-start.5 = (bf16[1024,256]{1,0:T(8,128)(2,1)S(1)}, bf16[1024,256]{1,0:T(8,128)(2,1)S(1)}, u32[]{:S(2)}, u32[]{:S(2)}) collective-permute-start(bf16[1024,256]{1,0:T(8,128)(2,1)S(1)} %collective-permute-done.refs_1_), channel_id=1, source_target_pairs={{0,2},{1,3},{2,4},{3,5},{4,6},{5,7},{6,0},{7,1},{8,10},{9,11},{10,... | collective-permute-start | bytes 1572872 | tf_op jit(solution)/shard_map/ppermute | solution.py:456
  36.3 9.5 %copy-start.3 = (bf16[1024,256]{1,0:T(8,128)(2,1)}, bf16[1024,256]{1,0:T(8,128)(2,1)S(1)}, u32[]{:S(2)}) copy-start(bf16[1024,256]{1,0:T(8,128)(2,1)S(1)} %collective-permute-done.6.refs_5_.refs_1_) | copy-start | bytes 1572868
  37.9 2.9 %copy-start.4 = (bf16[1024,256]{1,0:T(8,128)(2,1)}, bf16[1024,256]{1,0:T(8,128)(2,1)S(1)}, u32[]{:S(2)}) copy-start(bf16[1024,256]{1,0:T(8,128)(2,1)S(1)} %collective-permute-done.5.refs_2_) | copy-start | bytes 1572868
  37.9 1.1 %copy-start.12 = (bf16[1152,512]{1,0:T(8,128)(2,1)}, bf16[1152,512]{1,0:T(8,128)(2,1)S(1)}, u32[]{:S(2)}) copy-start(bf16[1152,512]{1,0:T(8,128)(2,1)S(1)} %collective-permute-done.7.refs_10_) | copy-start | bytes 3538948
  39.0 12.0 %collective-permute-start.9 = (bf16[1024,256]{1,0:T(8,128)(2,1)S(1)}, bf16[1024,256]{1,0:T(8,128)(2,1)S(1)}, u32[]{:S(2)}, u32[]{:S(2)}) collective-permute-start(bf16[1024,256]{1,0:T(8,128)(2,1)S(1)} %collective-permute-done.5.refs_2_), channel_id=1, source_target_pairs={{0,1},{1,0},{2,3},{3,2},{4,5},{5,4},{6,7},{7,6},{8,9},{9,8},{10,11... | collective-permute-start | bytes 1572872 | tf_op jit(solution)/shard_map/ppermute | solution.py:430
  40.3 13.5 %collective-permute-start.8 = (bf16[1024,256]{1,0:T(8,128)(2,1)S(1)}, bf16[1024,256]{1,0:T(8,128)(2,1)S(1)}, u32[]{:S(2)}, u32[]{:S(2)}) collective-permute-start(bf16[1024,256]{1,0:T(8,128)(2,1)S(1)} %collective-permute-done.5.refs_2_), channel_id=1, source_target_pairs={{0,2},{1,3},{2,4},{3,5},{4,6},{5,7},{6,0},{7,1},{8,10},{9,11},{10,... | collective-permute-start | bytes 1572872 | tf_op jit(solution)/shard_map/ppermute | solution.py:456
  51.0 5.8 %copy-start = (bf16[1024,256]{1,0:T(8,128)(2,1)}, bf16[1024,256]{1,0:T(8,128)(2,1)S(1)}, u32[]{:S(2)}) copy-start(bf16[1024,256]{1,0:T(8,128)(2,1)S(1)} %collective-permute-done.9.refs_6_.refs_2_) | copy-start | bytes 1572868
  53.8 3.0 %copy-start.5 = (bf16[1024,256]{1,0:T(8,128)(2,1)}, bf16[1024,256]{1,0:T(8,128)(2,1)S(1)}, u32[]{:S(2)}) copy-start(bf16[1024,256]{1,0:T(8,128)(2,1)S(1)} %collective-permute-done.8.refs_3_) | copy-start | bytes 1572868
  53.8 11.9 %collective-permute-start.14 = (bf16[1152,512]{1,0:T(8,128)(2,1)}, bf16[1152,512]{1,0:T(8,128)(2,1)S(1)}, u32[]{:S(2)}, u32[]{:S(2)}) collective-permute-start(bf16[1152,512]{1,0:T(8,128)(2,1)} %collective-permute-done.10.refs_11_), channel_id=1, source_target_pairs={{0,8},{8,0},{16,24},{24,16},{1,9},{9,1},{17,25},{25,17},{2,10},{10... | collective-permute-start | bytes 3538952 | tf_op jit(solution)/shard_map/ppermute | solution.py:430
  56.4 7.0 %collective-permute-start.13 = (bf16[1152,256]{1,0:T(8,128)(2,1)}, bf16[1152,256]{1,0:T(8,128)(2,1)}, u32[]{:S(2)}, u32[]{:S(2)}) collective-permute-start(bf16[1152,256]{1,0:T(8,128)(2,1)} %get-tuple-element.57), channel_id=1, source_target_pairs={{0,8},{8,0},{16,24},{24,16},{1,9},{9,1},{17,25},{25,17},{2,10},{10... | collective-permute-start | bytes 1769480 | tf_op jit(solution)/shard_map/ppermute | solution.py:430
  56.5 7.0 %copy-start.16 = (bf16[1152,256]{1,0:T(8,128)(2,1)S(1)}, bf16[1152,256]{1,0:T(8,128)(2,1)}, u32[]{:S(2)}) copy-start(bf16[1152,256]{1,0:T(8,128)(2,1)} %get-tuple-element.56) | copy-start | bytes 1769476
  56.5 9.2 %collective-permute-start.12 = (bf16[512,256]{1,0:T(8,128)(2,1)S(1)}, bf16[512,256]{1,0:T(8,128)(2,1)S(1)}, u32[]{:S(2)}, u32[]{:S(2)}) collective-permute-start(bf16[512,256]{1,0:T(8,128)(2,1)S(1)} %slice.11), channel_id=1, source_target_pairs={{0,2},{1,3},{2,4},{3,5},{4,6},{5,7},{6,0},{7,1},{8,10},{9,11},{10,... | collective-permute-start | bytes 786440 | tf_op jit(solution)/shard_map/ppermute | solution.py:456
  56.5 9.2 %collective-permute-start.11 = (bf16[512,256]{1,0:T(8,128)(2,1)S(1)}, bf16[512,256]{1,0:T(8,128)(2,1)S(1)}, u32[]{:S(2)}, u32[]{:S(2)}) collective-permute-start(bf16[512,256]{1,0:T(8,128)(2,1)S(1)} %slice.10), channel_id=1, source_target_pairs={{0,1},{1,0},{2,3},{3,2},{4,5},{5,4},{6,7},{7,6},{8,9},{9,8},{10,11... | collective-permute-start | bytes 786440 | tf_op jit(solution)/shard_map/ppermute | solution.py:430
  64.6 11.5 %copy-start.6 = (bf16[1152,256]{1,0:T(8,128)(2,1)}, bf16[1152,256]{1,0:T(8,128)(2,1)S(1)}, u32[]{:S(2)}) copy-start(bf16[1152,256]{1,0:T(8,128)(2,1)S(1)} %add.40.refs_0_) | copy-start | bytes 1769476
  65.7 5.1 %copy-start.14 = (bf16[512,256]{1,0:T(8,128)(2,1)}, bf16[512,256]{1,0:T(8,128)(2,1)S(1)}, u32[]{:S(2)}) copy-start(bf16[512,256]{1,0:T(8,128)(2,1)S(1)} %collective-permute-done.12.refs_4_.refs_8_) | copy-start | bytes 786436
  65.7 1.4 %copy-start.15 = (bf16[512,256]{1,0:T(8,128)(2,1)}, bf16[512,256]{1,0:T(8,128)(2,1)S(1)}, u32[]{:S(2)}) copy-start(bf16[512,256]{1,0:T(8,128)(2,1)S(1)} %collective-permute-done.11.refs_3_.refs_7_) | copy-start | bytes 786436
  65.7 5.1 %copy-start.13 = (bf16[1152,512]{1,0:T(8,128)(2,1)}, bf16[1152,512]{1,0:T(8,128)(2,1)S(1)}, u32[]{:S(2)}) copy-start(bf16[1152,512]{1,0:T(8,128)(2,1)S(1)} %collective-permute-done.14.refs_12_) | copy-start | bytes 3538948
  65.7 10.4 %collective-permute-start.16 = (bf16[1152,256]{1,0:T(8,128)(2,1)}, bf16[1152,256]{1,0:T(8,128)(2,1)S(1)}, u32[]{:S(2)}, u32[]{:S(2)}) collective-permute-start(bf16[1152,256]{1,0:T(8,128)(2,1)} %get-tuple-element.70), channel_id=1, source_target_pairs={{0,8},{8,0},{16,24},{24,16},{1,9},{9,1},{17,25},{25,17},{2,10},{10... | collective-permute-start | bytes 1769480 | tf_op jit(solution)/shard_map/ppermute | solution.py:430
  67.1 9.0 %collective-permute-start.17 = (bf16[1152,256]{1,0:T(8,128)(2,1)}, bf16[1152,256]{1,0:T(8,128)(2,1)S(1)}, u32[]{:S(2)}, u32[]{:S(2)}) collective-permute-start(bf16[1152,256]{1,0:T(8,128)(2,1)} %get-tuple-element.71), channel_id=1, source_target_pairs={{0,8},{8,0},{16,24},{24,16},{1,9},{9,1},{17,25},{25,17},{2,10},{10... | collective-permute-start | bytes 1769480 | tf_op jit(solution)/shard_map/ppermute | solution.py:430
  67.8 9.4 %collective-permute-start.15 = (bf16[1152,256]{1,0:T(8,128)(2,1)S(1)}, bf16[1152,256]{1,0:T(8,128)(2,1)}, u32[]{:S(2)}, u32[]{:S(2)}) collective-permute-start(bf16[1152,256]{1,0:T(8,128)(2,1)S(1)} %add.40.refs_0_), channel_id=1, source_target_pairs={{4,20},{5,21},{6,22},{7,23},{8,24},{9,25},{10,26},{11,27},{16,0},{... | collective-permute-start | bytes 1769480 | tf_op jit(solution)/shard_map/ppermute | solution.py:452
  70.8 5.4 %copy-start.8 = (bf16[1152,256]{1,0:T(8,128)(2,1)S(1)}, bf16[1152,256]{1,0:T(8,128)(2,1)}, u32[]{:S(2)}) copy-start(bf16[1152,256]{1,0:T(8,128)(2,1)} %get-tuple-element.69.refs_3_) | copy-start | bytes 1769476
  70.8 5.4 %copy-start.9 = (bf16[1152,256]{1,0:T(8,128)(2,1)S(1)}, bf16[1152,256]{1,0:T(8,128)(2,1)}, u32[]{:S(2)}) copy-start(bf16[1152,256]{1,0:T(8,128)(2,1)} %get-tuple-element.68.refs_1_) | copy-start | bytes 1769476
  76.1 1.4 %copy-start.21 = (bf16[1152,256]{1,0:T(8,128)(2,1)S(1)}, bf16[1152,256]{1,0:T(8,128)(2,1)}, u32[]{:S(2)}) copy-start(bf16[1152,256]{1,0:T(8,128)(2,1)} %get-tuple-element.73) | copy-start | bytes 1769476
  76.1 5.2 %copy-start.17 = (bf16[1152,256]{1,0:T(8,128)(2,1)S(1)}, bf16[1152,256]{1,0:T(8,128)(2,1)}, u32[]{:S(2)}) copy-start(bf16[1152,256]{1,0:T(8,128)(2,1)} %get-tuple-element.72) | copy-start | bytes 1769476
  76.1 0.8 copy-start.10
  76.2 1.0 copy-start.11
  77.5 3.8 %collective-permute-start.18 = (bf16[1152,256]{1,0:T(8,128)(2,1)S(1)}, bf16[1152,256]{1,0:T(8,128)(2,1)S(1)}, u32[]{:S(2)}, u32[]{:S(2)}) collective-permute-start(bf16[1152,256]{1,0:T(8,128)(2,1)S(1)} %copy-done.21), channel_id=1, source_target_pairs={{0,8},{8,0},{16,24},{24,16},{1,9},{9,1},{17,25},{25,17},{2,10},{10... | collective-permute-start | bytes 1769480 | tf_op jit(solution)/shard_map/ppermute | solution.py:430
  79.6 16.9 %collective-permute-start.20 = (bf16[1152,256]{1,0:T(8,128)(2,1)S(1)}, bf16[1152,256]{1,0:T(8,128)(2,1)S(1)}, u32[]{:S(2)}, u32[]{:S(2)}) collective-permute-start(bf16[1152,256]{1,0:T(8,128)(2,1)S(1)} %select_add_fusion), channel_id=1, source_target_pairs={{0,16},{8,24},{16,0},{24,8},{1,17},{9,25},{17,1},{25,9},{2,18},{10... | collective-permute-start | bytes 1769480 | tf_op jit(solution)/shard_map/ppermute | solution.py:430
  81.4 12.1 %copy-start.7 = (bf16[1152,256]{1,0:T(8,128)(2,1)}, bf16[1152,256]{1,0:T(8,128)(2,1)S(1)}, u32[]{:S(2)}) copy-start(bf16[1152,256]{1,0:T(8,128)(2,1)S(1)} %add.47.refs_5_) | copy-start | bytes 1769476
  81.5 21.0 %collective-permute-start.21 = (bf16[1152,256]{1,0:T(8,128)(2,1)S(1)}, bf16[1152,256]{1,0:T(8,128)(2,1)S(1)}, u32[]{:S(2)}, u32[]{:S(2)}) collective-permute-start(bf16[1152,256]{1,0:T(8,128)(2,1)S(1)} %add.47.refs_5_), channel_id=1, source_target_pairs={{0,16},{1,17},{2,18},{3,19},{12,28},{13,29},{14,30},{15,31},{20,4}... | collective-permute-start | bytes 1769480 | tf_op jit(solution)/shard_map/ppermute | solution.py:452
  93.6 8.0 %collective-permute-start.19 = (f32[256,128]{1,0:T(8,128)}, f32[256,128]{1,0:T(8,128)S(1)}, u32[]{:S(2)}, u32[]{:S(2)}) collective-permute-start(f32[256,128]{1,0:T(8,128)} %get-tuple-element.79), channel_id=1, source_target_pairs={{8,0},{16,8},{24,16},{9,1},{17,9},{25,17},{10,2},{18,10},{26,18},{... | collective-permute-start | bytes 393224 | tf_op jit(solution)/shard_map/ppermute | solution.py:424
  96.6 5.9 %copy-start.18 = (bf16[1152,256]{1,0:T(8,128)(2,1)}, bf16[1152,256]{1,0:T(8,128)(2,1)S(1)}, u32[]{:S(2)}) copy-start(bf16[1152,256]{1,0:T(8,128)(2,1)S(1)} %collective-permute-done.20.refs_7_) | copy-start | bytes 1769476
  101.6 0.9 copy-start.20
  102.4 0.8 copy-start.19
